TPU v7x, 512 devices: a whole 4x4x16 slice. The times are simulated.
512 devices in a mesh: tm: 64 (over z_lo, y, core), lon: 8 (over x, z_hi).
Axes of the slice: x: 4, y: 4, z: 16 (z_hi: 2, z_lo: 8; z = z_hi * 8 + z_lo), core: 2. Of those that a mesh axis runs over, the one named last changes fastest.
Arguments:
- first_guess: float32 [64, 2880, 128], P('tm', 'lon'), may hold values from -13 to 13
- observed: float32 [64, 2880, 128], P('tm', 'lon'), may hold values from -6 to 6
- track_mask: int32 [64, 2880, 128], P('tm', 'lon'), may hold values 0 or 1
- land_mask: int32 [2880, 128], P('lon'), may hold values 0 or 1
- bending_weight: float32 [2880, 128], P('lon'), may hold values from 0.005 to 0.05
Outputs:
- analysis: float32 [64, 2880, 128], P('tm', 'lon')
- final_gradient: float32 [64, 2880, 128], P('tm', 'lon')
All inputs are finite; a program needn't handle non-finite values. No bound on the sum of `track_mask` or of `land_mask` on one device may be relied on, other than what follows from the above.
Results may differ from a plain program's by a relative error of at most 0.0003.
Values sent between devices are 32-bit elements; how exact they have to be, the bound alone decides.
A program may use at most 64 MiB of HBM per device.

v0:
```python
import math

import jax
import jax.numpy as jnp
from jax import lax
from jax.sharding import PartitionSpec as P

CAP = 64
MW = 64
ITERS = 2


time_coupling = 1.0


def padded(cells, sides, width, closed):
    for axis, dim in sides:
        count = lax.axis_size(axis)
        ends = count if closed else count - 1
        head = lax.slice_in_dim(cells, 0, width, axis=dim)
        tail = lax.slice_in_dim(cells, cells.shape[dim] - width, cells.shape[dim], axis=dim)
        cells = jnp.concatenate(
            [
                lax.ppermute(tail, axis, [(i, (i + 1) % count) for i in range(ends)]),
                cells,
                lax.ppermute(head, axis, [((i + 1) % count, i) for i in range(ends)]),
            ],
            axis=dim,
        )
    return cells


def bending_table(row_count):
    positions = jnp.arange(row_count, dtype=jnp.float32)
    latitude = (90.0 - (row_count - positions - 0.5) * 0.125) * (math.pi / 180.0)
    return 1.0 / (jnp.cos(latitude) + 0.5) ** 2


def laplace(surface, bending_row):
    timed = padded(surface, (("tm", 0),), 1, False)
    rimmed = padded(surface, (("lon", 1),), 1, True)
    across = jnp.pad(surface, ((0, 0), (0, 0), (1, 1)))
    centre = 2.0 * surface
    zonal = rimmed[:, 2:] + rimmed[:, :-2] - centre
    return (
        time_coupling * (timed[2:] + timed[:-2] - centre)
        + bending_row * zonal
        + (across[:, :, 2:] + across[:, :, :-2] - centre)
    )


def mode_table(leading, span_rows, circle):
    positions = leading + jnp.arange(span_rows, dtype=jnp.int32)
    harmonic = jnp.arange(MW, dtype=jnp.int32)
    angles = (positions[:, None] * harmonic[None, :] % circle).astype(jnp.float32) * (
        2.0 * math.pi / circle
    )
    return jnp.concatenate([jnp.cos(angles), jnp.sin(angles)], axis=1)


def mode_weights(circle):
    harmonic = jnp.arange(MW, dtype=jnp.int32)
    single = jnp.where(harmonic == 0, 1.0 / circle, 2.0 / circle).astype(jnp.float32)
    return jnp.concatenate([single, single])


def cap_shrink():
    cap_rows = jnp.arange(CAP, dtype=jnp.float32)
    return 0.9 * (cap_rows + 1.0) / CAP


def polar_filter(gradient_now):
    row_count = gradient_now.shape[2]
    longitudes = gradient_now.shape[1]
    circle = longitudes * lax.axis_size("lon")
    cap_panel = gradient_now[:, :, row_count - CAP :]
    own_rows = mode_table(lax.axis_index("lon") * longitudes, longitudes, circle)
    slab_part = lax.all_gather(cap_panel, "lon", axis=1, tiled=True)
    slab_rows = mode_table(jnp.int32(0), slab_part.shape[1], circle)
    amplitudes = jnp.einsum("dic,ik->dck", slab_part, slab_rows, precision=lax.Precision.HIGHEST)
    smoothed = jnp.einsum(
        "dck,ik->dic", amplitudes * mode_weights(circle), own_rows, precision=lax.Precision.HIGHEST
    )
    filtered = cap_panel - cap_shrink() * (cap_panel - smoothed)
    return jnp.concatenate([gradient_now[:, :, : row_count - CAP], filtered], axis=2)


def on_device(first_guess, observed, track_mask, land_mask, bending_weight):
    bending_row = bending_table(first_guess.shape[2])
    weight = track_mask.astype(jnp.float32) * (1.0 - land_mask.astype(jnp.float32))[None]
    smooth = bending_weight[None]

    def gradient_at(surface):
        return weight * (surface - observed) + laplace(
            smooth * laplace(surface, bending_row), bending_row
        )

    analysis = first_guess
    gradient_now = gradient_at(analysis)
    for iteration in range(ITERS):
        search = polar_filter(gradient_now)
        slope = lax.psum(jnp.sum(gradient_now * search), ("tm", "lon"))
        curved = weight * search + laplace(smooth * laplace(search, bending_row), bending_row)
        curvature = lax.psum(jnp.sum(search * curved), ("tm", "lon"))
        stepsize = slope / curvature
        analysis = analysis - stepsize * search
        gradient_now = gradient_at(analysis)
    return (analysis, gradient_now)


def solution(mesh):
    in_specs = (
        P("tm", "lon", None),
        P("tm", "lon", None),
        P("tm", "lon", None),
        P("lon", None),
        P("lon", None),
    )
    out_specs = (P("tm", "lon", None), P("tm", "lon", None))
    return jax.shard_map(
        on_device, mesh=mesh, in_specs=in_specs, out_specs=out_specs, check_vma=False
    )
```

profile of v0, /device:TPU:1, one launch (start us, length us, event | category | flops | bytes accessed | tf_op | source)
XLA Modules:
  0.0 812.9 jit_solution(11991949210889096333)
XLA Ops:
  1.7 4.6 collective-permute-start.1
  6.3 5.5 collective-permute-start
  13.3 11.9 %collective-permute-start.3 = (f32[1,1,128]{1,2,0:T(8,128)}, f32[1,1,128]{1,2,0:T(8,128)}, u32[]{:S(2)}, u32[]{:S(2)}) collective-permute-start(f32[1,1,128]{1,2,0:T(8,128)} %copy.35), channel_id=1, source_target_pairs={{0,1},{1,2},{2,3},{3,4},{4,5},{5,6},{6,7},{7,0},{8,9},{9,10},{10,1... | collective-permute-start | bytes 1544 | tf_op jit(solution)/shard_map/ppermute | solution.py:24
  25.8 4.2 collective-permute-start.2
  30.1 6.1 fusion.4
  36.2 1.6 fusion.102
  38.9 3.0 collective-permute-done.2
  41.9 1.9 fusion.16
  43.8 3.7 collective-permute-start.5
  47.5 1.9 collective-permute-start.4
  49.4 1.6 fusion.120
  51.0 9.5 %collective-permute-start.6 = (f32[1,1,128]{1,2,0:T(8,128)}, f32[1,1,128]{1,2,0:T(8,128)}, u32[]{:S(2)}, u32[]{:S(2)}) collective-permute-start(f32[1,1,128]{1,2,0:T(8,128)} %get-tuple-element.36), channel_id=1, source_target_pairs={{1,0},{2,1},{3,2},{4,3},{5,4},{6,5},{7,6},{0,7},{9,8},{10,9},{11,1... | collective-permute-start | bytes 1544 | tf_op jit(solution)/shard_map/ppermute | solution.py:26
  60.5 4.5 collective-permute-start.7
  66.1 1.8 copy.25
  67.9 1.7 copy.26
  69.7 8.7 %collective-permute-done.7 = f32[1,1,128]{1,2,0:T(8,128)} collective-permute-done((f32[1,1,128]{1,2,0:T(8,128)}, f32[1,1,128]{1,2,0:T(8,128)}, u32[]{:S(2)}, u32[]{:S(2)}) %collective-permute-start.7) | collective-permute-done | bytes 544 | tf_op jit(solution)/shard_map/ppermute | solution.py:24
  79.0 2.0 fusion.20
  82.6 112.1 %all_gather.6 = f32[1,2880,64]{2,0,1:T(1,128)S(1)} all-gather(f32[1,360,64]{2,0,1:T(1,128)} %copy.38), channel_id=1, replica_groups=mesh['tm'=64,'lon'=8] {'lon'}, dimensions={1}, use_global_device_ids=true | all-gather | bytes 829440 | tf_op jit(solution)/shard_map/all_gather | solution.py:78
  194.7 3.0 convolution_multiply_fusion.1
  198.2 2.4 collective-permute-start.8
  200.6 26.6 %collective-permute-start.9 = (f32[1,360,128]{1,2,0:T(8,128)S(1)}, f32[1,360,128]{1,2,0:T(8,128)S(1)}, u32[]{:S(2)}, u32[]{:S(2)}) collective-permute-start(f32[1,360,128]{1,2,0:T(8,128)S(1)} %pad_maximum_fusion.3), channel_id=1, source_target_pairs={{0,8},{8,16},{16,24},{24,32},{32,40},{40,48},{48,56},{56,64},{64,7... | collective-permute-start | bytes 552968 | tf_op jit(solution)/shard_map/ppermute | solution.py:24
  227.3 8.4 %collective-permute-start.10 = (f32[1,1,128]{1,2,0:T(8,128)S(1)}, f32[1,1,128]{1,2,0:T(8,128)S(1)}, u32[]{:S(2)}, u32[]{:S(2)}) collective-permute-start(f32[1,1,128]{1,2,0:T(8,128)S(1)} %get-tuple-element.32), channel_id=1, source_target_pairs={{1,0},{2,1},{3,2},{4,3},{5,4},{6,5},{7,6},{0,7},{9,8},{10,9},{11,1... | collective-permute-start | bytes 1544 | tf_op jit(solution)/shard_map/ppermute | solution.py:26
  235.7 5.6 collective-permute-start.11
  241.3 11.7 %collective-permute-done.11 = f32[1,1,128]{1,2,0:T(8,128)S(1)} collective-permute-done((f32[1,1,128]{1,2,0:T(8,128)S(1)}, f32[1,1,128]{1,2,0:T(8,128)S(1)}, u32[]{:S(2)}, u32[]{:S(2)}) %collective-permute-start.11) | collective-permute-done | bytes 544 | tf_op jit(solution)/shard_map/ppermute | solution.py:24
  253.2 5.0 collective-permute-start.13
  258.2 1.9 collective-permute-start.12
  260.3 3.1 collective-permute-start.14
  263.3 10.9 %collective-permute-start.15 = (f32[1,1,128]{1,2,0:T(8,128)S(1)}, f32[1,1,128]{1,2,0:T(8,128)S(1)}, u32[]{:S(2)}, u32[]{:S(2)}) collective-permute-start(f32[1,1,128]{1,2,0:T(8,128)S(1)} %get-tuple-element.31), channel_id=1, source_target_pairs={{0,1},{1,2},{2,3},{3,4},{4,5},{5,6},{6,7},{7,0},{8,9},{9,10},{10,1... | collective-permute-start | bytes 1544 | tf_op jit(solution)/shard_map/ppermute | solution.py:24
  274.9 7.2 collective-permute-done.15
  283.0 102.0 %all-reduce.11 = (f32[]{:T(128)}, f32[]{:T(128)}) all-reduce(f32[]{:T(128)} %get-tuple-element.9, f32[]{:T(128)} %get-tuple-element.8), channel_id=1, replica_groups=mesh['tm'=64,'lon'=8] {'tm','lon'}, use_global_device_ids=true, to_apply=%region_1.2 | all-reduce | flops 2 | bytes 16 | tf_op jit(solution)/shard_map/psum | solution.py:102
  387.4 2.9 collective-permute-start.17
  390.3 1.9 collective-permute-start.16
  392.3 7.9 collective-permute-start.18
  400.3 6.1 collective-permute-start.19
  406.4 12.0 %collective-permute-done.19 = f32[1,1,128]{1,2,0:T(8,128)S(1)} collective-permute-done((f32[1,1,128]{1,2,0:T(8,128)S(1)}, f32[1,1,128]{1,2,0:T(8,128)S(1)}, u32[]{:S(2)}, u32[]{:S(2)}) %collective-permute-start.19) | collective-permute-done | bytes 544 | tf_op jit(solution)/shard_map/ppermute | solution.py:24
  418.6 3.4 collective-permute-start.21
  422.0 1.9 collective-permute-start.20
  424.0 4.1 collective-permute-start.22
  428.1 9.9 %collective-permute-start.23 = (f32[1,1,128]{1,2,0:T(8,128)S(1)}, f32[1,1,128]{1,2,0:T(8,128)S(1)}, u32[]{:S(2)}, u32[]{:S(2)}) collective-permute-start(f32[1,1,128]{1,2,0:T(8,128)S(1)} %get-tuple-element.27), channel_id=1, source_target_pairs={{0,1},{1,2},{2,3},{3,4},{4,5},{5,6},{6,7},{7,0},{8,9},{9,10},{10,1... | collective-permute-start | bytes 1544 | tf_op jit(solution)/shard_map/ppermute | solution.py:24
  438.0 6.8 collective-permute-done.23
  447.4 1.7 copy.41
  449.1 128.4 %all_gather.7 = f32[1,2880,64]{2,0,1:T(1,128)S(1)} all-gather(f32[1,360,64]{2,0,1:T(1,128)} %copy.41), channel_id=1, replica_groups=mesh['tm'=64,'lon'=8] {'lon'}, dimensions={1}, use_global_device_ids=true | all-gather | bytes 829440 | tf_op jit(solution)/shard_map/all_gather | solution.py:78
  577.4 3.0 convolution_multiply_fusion
  581.0 7.7 collective-permute-start.24
  588.8 1.9 collective-permute-start.25
  590.8 3.4 collective-permute-start.26
  594.2 10.7 %collective-permute-start.27 = (f32[1,1,128]{1,2,0:T(8,128)S(1)}, f32[1,1,128]{1,2,0:T(8,128)S(1)}, u32[]{:S(2)}, u32[]{:S(2)}) collective-permute-start(f32[1,1,128]{1,2,0:T(8,128)S(1)} %get-tuple-element.23), channel_id=1, source_target_pairs={{0,1},{1,2},{2,3},{3,4},{4,5},{5,6},{6,7},{7,0},{8,9},{9,10},{10,1... | collective-permute-start | bytes 1544 | tf_op jit(solution)/shard_map/ppermute | solution.py:24
  604.9 6.2 collective-permute-done.27
  611.4 3.6 collective-permute-start.29
  614.9 1.9 collective-permute-start.28
  616.9 3.5 collective-permute-start.30
  620.5 10.5 %collective-permute-start.31 = (f32[1,1,128]{1,2,0:T(8,128)S(1)}, f32[1,1,128]{1,2,0:T(8,128)S(1)}, u32[]{:S(2)}, u32[]{:S(2)}) collective-permute-start(f32[1,1,128]{1,2,0:T(8,128)S(1)} %get-tuple-element.21), channel_id=1, source_target_pairs={{0,1},{1,2},{2,3},{3,4},{4,5},{5,6},{6,7},{7,0},{8,9},{9,10},{10,1... | collective-permute-start | bytes 1544 | tf_op jit(solution)/shard_map/ppermute | solution.py:24
  631.0 5.4 collective-permute-done.31
  637.3 115.4 %all-reduce.10 = (f32[]{:T(128)}, f32[]{:T(128)}) all-reduce(f32[]{:T(128)} %get-tuple-element.7, f32[]{:T(128)} %get-tuple-element.6), channel_id=1, replica_groups=mesh['tm'=64,'lon'=8] {'tm','lon'}, use_global_device_ids=true, to_apply=%region_5.6 | all-reduce | flops 2 | bytes 16 | tf_op jit(solution)/shard_map/psum | solution.py:102
  754.0 1.9 collective-permute-start.33
  756.0 2.4 collective-permute-start.32
  758.5 7.0 collective-permute-start.34
  765.5 7.0 collective-permute-start.35
  772.9 11.6 %collective-permute-done.35 = f32[1,1,128]{1,2,0:T(8,128)S(1)} collective-permute-done((f32[1,1,128]{1,2,0:T(8,128)S(1)}, f32[1,1,128]{1,2,0:T(8,128)S(1)}, u32[]{:S(2)}, u32[]{:S(2)}) %collective-permute-start.35) | collective-permute-done | bytes 544 | tf_op jit(solution)/shard_map/ppermute | solution.py:24
  784.7 4.8 collective-permute-start.37
  789.5 1.9 collective-permute-start.36
  791.5 4.3 collective-permute-start.38
  795.8 9.7 %collective-permute-start.39 = (f32[1,1,128]{1,2,0:T(8,128)S(1)}, f32[1,1,128]{1,2,0:T(8,128)S(1)}, u32[]{:S(2)}, u32[]{:S(2)}) collective-permute-start(f32[1,1,128]{1,2,0:T(8,128)S(1)} %get-tuple-element.17), channel_id=1, source_target_pairs={{0,1},{1,2},{2,3},{3,4},{4,5},{5,6},{6,7},{7,0},{8,9},{9,10},{10,1... | collective-permute-start | bytes 1544 | tf_op jit(solution)/shard_map/ppermute | solution.py:24
  806.3 5.5 collective-permute-done.39
  (100 shorter events, 18.4 us)
Async XLA Ops:
  1.7 40.2 %copy-start.6 = (f32[1,360,128]{1,2,0:T(8,128)}, f32[1,360,128]{1,2,0:T(8,128)S(1)}, u32[]{:S(2)}) copy-start(f32[1,360,128]{1,2,0:T(8,128)S(1)} %copy.39) | copy-start | bytes 552964
  1.7 40.2 %collective-permute-start.1 = (f32[1,360,128]{1,2,0:T(8,128)S(1)}, f32[1,360,128]{1,2,0:T(8,128)S(1)}, u32[]{:S(2)}, u32[]{:S(2)}) collective-permute-start(f32[1,360,128]{1,2,0:T(8,128)S(1)} %copy.39), channel_id=1, source_target_pairs={{0,8},{8,16},{16,24},{24,32},{32,40},{40,48},{48,56},{56,64},{64,7... | collective-permute-start | bytes 552968 | tf_op jit(solution)/shard_map/ppermute | solution.py:24
  6.3 35.6 %collective-permute-start = (f32[1,360,128]{1,2,0:T(8,128)S(1)}, f32[1,360,128]{1,2,0:T(8,128)}, u32[]{:S(2)}, u32[]{:S(2)}) collective-permute-start(f32[1,360,128]{1,2,0:T(8,128)S(1)} %copy.39), channel_id=1, source_target_pairs={{8,0},{16,8},{24,16},{32,24},{40,32},{48,40},{56,48},{64,56},{72,6... | collective-permute-start | bytes 552968 | tf_op jit(solution)/shard_map/ppermute | solution.py:26
  13.3 25.6 %collective-permute-start.3 = (f32[1,1,128]{1,2,0:T(8,128)}, f32[1,1,128]{1,2,0:T(8,128)}, u32[]{:S(2)}, u32[]{:S(2)}) collective-permute-start(f32[1,1,128]{1,2,0:T(8,128)} %copy.35), channel_id=1, source_target_pairs={{0,1},{1,2},{2,3},{3,4},{4,5},{5,6},{6,7},{7,0},{8,9},{9,10},{10,1... | collective-permute-start | bytes 1544 | tf_op jit(solution)/shard_map/ppermute | solution.py:24
  25.8 16.0 %collective-permute-start.2 = (f32[1,1,128]{1,2,0:T(8,128)}, f32[1,1,128]{1,2,0:T(8,128)}, u32[]{:S(2)}, u32[]{:S(2)}) collective-permute-start(f32[1,1,128]{1,2,0:T(8,128)} %copy.33), channel_id=1, source_target_pairs={{1,0},{2,1},{3,2},{4,3},{5,4},{6,5},{7,6},{0,7},{9,8},{10,9},{11,1... | collective-permute-start | bytes 1544 | tf_op jit(solution)/shard_map/ppermute | solution.py:26
  43.8 34.5 %collective-permute-start.5 = (f32[1,360,128]{1,2,0:T(8,128)}, f32[1,360,128]{1,2,0:T(8,128)S(1)}, u32[]{:S(2)}, u32[]{:S(2)}) collective-permute-start(f32[1,360,128]{1,2,0:T(8,128)} %fusion.16), channel_id=1, source_target_pairs={{0,8},{8,16},{16,24},{24,32},{32,40},{40,48},{48,56},{56,64},{64,7... | collective-permute-start | bytes 552968 | tf_op jit(solution)/shard_map/ppermute | solution.py:24
  47.5 31.6 %collective-permute-start.4 = (f32[1,360,128]{1,2,0:T(8,128)}, f32[1,360,128]{1,2,0:T(8,128)}, u32[]{:S(2)}, u32[]{:S(2)}) collective-permute-start(f32[1,360,128]{1,2,0:T(8,128)} %fusion.16), channel_id=1, source_target_pairs={{8,0},{16,8},{24,16},{32,24},{40,32},{48,40},{56,48},{64,56},{72,6... | collective-permute-start | bytes 552968 | tf_op jit(solution)/shard_map/ppermute | solution.py:26
  51.0 18.7 %collective-permute-start.6 = (f32[1,1,128]{1,2,0:T(8,128)}, f32[1,1,128]{1,2,0:T(8,128)}, u32[]{:S(2)}, u32[]{:S(2)}) collective-permute-start(f32[1,1,128]{1,2,0:T(8,128)} %get-tuple-element.36), channel_id=1, source_target_pairs={{1,0},{2,1},{3,2},{4,3},{5,4},{6,5},{7,6},{0,7},{9,8},{10,9},{11,1... | collective-permute-start | bytes 1544 | tf_op jit(solution)/shard_map/ppermute | solution.py:26
  60.5 17.8 %collective-permute-start.7 = (f32[1,1,128]{1,2,0:T(8,128)}, f32[1,1,128]{1,2,0:T(8,128)}, u32[]{:S(2)}, u32[]{:S(2)}) collective-permute-start(f32[1,1,128]{1,2,0:T(8,128)} %get-tuple-element.37), channel_id=1, source_target_pairs={{0,1},{1,2},{2,3},{3,4},{4,5},{5,6},{6,7},{7,0},{8,9},{9,10},{10,1... | collective-permute-start | bytes 1544 | tf_op jit(solution)/shard_map/ppermute | solution.py:24
  66.1 14.9 %copy-start.4 = (f32[1,360,128]{1,2,0:T(8,128)}, f32[1,360,128]{1,2,0:T(8,128)S(1)}, u32[]{:S(2)}) copy-start(f32[1,360,128]{1,2,0:T(8,128)S(1)} %copy.28) | copy-start | bytes 552964
  78.3 0.7 copy-start.15
  81.0 0.7 copy-start.7
  81.8 200.3 %copy-start.2 = (f32[1,360,64]{1,2,0:T(8,128)}, f32[1,360,64]{1,2,0:T(8,128)S(1)}, u32[]{:S(2)}) copy-start(f32[1,360,64]{1,2,0:T(8,128)S(1)} %get-tuple-element.34) | copy-start | bytes 276484
  194.7 3.1 copy-start.8
  194.7 3.1 copy-start.11
  194.7 3.1 copy-start.13
  198.2 84.8 %copy-start.3 = (f32[1,360,64]{1,2,0:T(8,128)}, f32[1,360,64]{1,2,0:T(8,128)S(1)}, u32[]{:S(2)}) copy-start(f32[1,360,64]{1,2,0:T(8,128)S(1)} %fusion.9) | copy-start | bytes 276484
  198.2 54.8 %collective-permute-start.8 = (f32[1,360,128]{1,2,0:T(8,128)S(1)}, f32[1,360,128]{1,2,0:T(8,128)S(1)}, u32[]{:S(2)}, u32[]{:S(2)}) collective-permute-start(f32[1,360,128]{1,2,0:T(8,128)S(1)} %pad_maximum_fusion.3), channel_id=1, source_target_pairs={{8,0},{16,8},{24,16},{32,24},{40,32},{48,40},{56,48},{64,56},{72,6... | collective-permute-start | bytes 552968 | tf_op jit(solution)/shard_map/ppermute | solution.py:26
  200.6 52.4 %collective-permute-start.9 = (f32[1,360,128]{1,2,0:T(8,128)S(1)}, f32[1,360,128]{1,2,0:T(8,128)S(1)}, u32[]{:S(2)}, u32[]{:S(2)}) collective-permute-start(f32[1,360,128]{1,2,0:T(8,128)S(1)} %pad_maximum_fusion.3), channel_id=1, source_target_pairs={{0,8},{8,16},{16,24},{24,32},{32,40},{40,48},{48,56},{56,64},{64,7... | collective-permute-start | bytes 552968 | tf_op jit(solution)/shard_map/ppermute | solution.py:24
  227.3 14.0 %collective-permute-start.10 = (f32[1,1,128]{1,2,0:T(8,128)S(1)}, f32[1,1,128]{1,2,0:T(8,128)S(1)}, u32[]{:S(2)}, u32[]{:S(2)}) collective-permute-start(f32[1,1,128]{1,2,0:T(8,128)S(1)} %get-tuple-element.32), channel_id=1, source_target_pairs={{1,0},{2,1},{3,2},{4,3},{5,4},{6,5},{7,6},{0,7},{9,8},{10,9},{11,1... | collective-permute-start | bytes 1544 | tf_op jit(solution)/shard_map/ppermute | solution.py:26
  235.7 17.4 %collective-permute-start.11 = (f32[1,1,128]{1,2,0:T(8,128)S(1)}, f32[1,1,128]{1,2,0:T(8,128)S(1)}, u32[]{:S(2)}, u32[]{:S(2)}) collective-permute-start(f32[1,1,128]{1,2,0:T(8,128)S(1)} %get-tuple-element.33), channel_id=1, source_target_pairs={{0,1},{1,2},{2,3},{3,4},{4,5},{5,6},{6,7},{7,0},{8,9},{9,10},{10,1... | collective-permute-start | bytes 1544 | tf_op jit(solution)/shard_map/ppermute | solution.py:24
  253.2 28.8 %collective-permute-start.13 = (f32[1,360,128]{1,2,0:T(8,128)S(1)}, f32[1,360,128]{1,2,0:T(8,128)S(1)}, u32[]{:S(2)}, u32[]{:S(2)}) collective-permute-start(f32[1,360,128]{1,2,0:T(8,128)S(1)} %fusion.24), channel_id=1, source_target_pairs={{0,8},{8,16},{16,24},{24,32},{32,40},{40,48},{48,56},{56,64},{64,7... | collective-permute-start | bytes 552968 | tf_op jit(solution)/shard_map/ppermute | solution.py:24
  258.2 23.8 %collective-permute-start.12 = (f32[1,360,128]{1,2,0:T(8,128)S(1)}, f32[1,360,128]{1,2,0:T(8,128)S(1)}, u32[]{:S(2)}, u32[]{:S(2)}) collective-permute-start(f32[1,360,128]{1,2,0:T(8,128)S(1)} %fusion.24), channel_id=1, source_target_pairs={{8,0},{16,8},{24,16},{32,24},{40,32},{48,40},{56,48},{64,56},{72,6... | collective-permute-start | bytes 552968 | tf_op jit(solution)/shard_map/ppermute | solution.py:26
  260.3 14.6 %collective-permute-start.14 = (f32[1,1,128]{1,2,0:T(8,128)S(1)}, f32[1,1,128]{1,2,0:T(8,128)S(1)}, u32[]{:S(2)}, u32[]{:S(2)}) collective-permute-start(f32[1,1,128]{1,2,0:T(8,128)S(1)} %get-tuple-element.30), channel_id=1, source_target_pairs={{1,0},{2,1},{3,2},{4,3},{5,4},{6,5},{7,6},{0,7},{9,8},{10,9},{11,1... | collective-permute-start | bytes 1544 | tf_op jit(solution)/shard_map/ppermute | solution.py:26
  263.3 18.7 %collective-permute-start.15 = (f32[1,1,128]{1,2,0:T(8,128)S(1)}, f32[1,1,128]{1,2,0:T(8,128)S(1)}, u32[]{:S(2)}, u32[]{:S(2)}) collective-permute-start(f32[1,1,128]{1,2,0:T(8,128)S(1)} %get-tuple-element.31), channel_id=1, source_target_pairs={{0,1},{1,2},{2,3},{3,4},{4,5},{5,6},{6,7},{7,0},{8,9},{9,10},{10,1... | collective-permute-start | bytes 1544 | tf_op jit(solution)/shard_map/ppermute | solution.py:24
  387.4 31.0 %collective-permute-start.17 = (f32[1,360,128]{1,2,0:T(8,128)S(1)}, f32[1,360,128]{1,2,0:T(8,128)S(1)}, u32[]{:S(2)}, u32[]{:S(2)}) collective-permute-start(f32[1,360,128]{1,2,0:T(8,128)S(1)} %multiply_subtract_fusion.9), channel_id=1, source_target_pairs={{0,8},{8,16},{16,24},{24,32},{32,40},{40,48},{48,56},{56,64},{64,7... | collective-permute-start | bytes 552968 | tf_op jit(solution)/shard_map/ppermute | solution.py:24
  390.3 28.0 %collective-permute-start.16 = (f32[1,360,128]{1,2,0:T(8,128)S(1)}, f32[1,360,128]{1,2,0:T(8,128)S(1)}, u32[]{:S(2)}, u32[]{:S(2)}) collective-permute-start(f32[1,360,128]{1,2,0:T(8,128)S(1)} %multiply_subtract_fusion.9), channel_id=1, source_target_pairs={{8,0},{16,8},{24,16},{32,24},{40,32},{48,40},{56,48},{64,56},{72,6... | collective-permute-start | bytes 552968 | tf_op jit(solution)/shard_map/ppermute | solution.py:26
  392.3 14.0 %collective-permute-start.18 = (f32[1,1,128]{1,2,0:T(8,128)S(1)}, f32[1,1,128]{1,2,0:T(8,128)S(1)}, u32[]{:S(2)}, u32[]{:S(2)}) collective-permute-start(f32[1,1,128]{1,2,0:T(8,128)S(1)} %get-tuple-element.28), channel_id=1, source_target_pairs={{1,0},{2,1},{3,2},{4,3},{5,4},{6,5},{7,6},{0,7},{9,8},{10,9},{11,1... | collective-permute-start | bytes 1544 | tf_op jit(solution)/shard_map/ppermute | solution.py:26
  400.3 18.1 %collective-permute-start.19 = (f32[1,1,128]{1,2,0:T(8,128)S(1)}, f32[1,1,128]{1,2,0:T(8,128)S(1)}, u32[]{:S(2)}, u32[]{:S(2)}) collective-permute-start(f32[1,1,128]{1,2,0:T(8,128)S(1)} %get-tuple-element.29), channel_id=1, source_target_pairs={{0,1},{1,2},{2,3},{3,4},{4,5},{5,6},{6,7},{7,0},{8,9},{9,10},{10,1... | collective-permute-start | bytes 1544 | tf_op jit(solution)/shard_map/ppermute | solution.py:24
  418.6 26.3 %collective-permute-start.21 = (f32[1,360,128]{1,2,0:T(8,128)S(1)}, f32[1,360,128]{1,2,0:T(8,128)S(1)}, u32[]{:S(2)}, u32[]{:S(2)}) collective-permute-start(f32[1,360,128]{1,2,0:T(8,128)S(1)} %fusion.34), channel_id=1, source_target_pairs={{0,8},{8,16},{16,24},{24,32},{32,40},{40,48},{48,56},{56,64},{64,7... | collective-permute-start | bytes 552968 | tf_op jit(solution)/shard_map/ppermute | solution.py:24
  422.0 22.8 %collective-permute-start.20 = (f32[1,360,128]{1,2,0:T(8,128)S(1)}, f32[1,360,128]{1,2,0:T(8,128)S(1)}, u32[]{:S(2)}, u32[]{:S(2)}) collective-permute-start(f32[1,360,128]{1,2,0:T(8,128)S(1)} %fusion.34), channel_id=1, source_target_pairs={{8,0},{16,8},{24,16},{32,24},{40,32},{48,40},{56,48},{64,56},{72,6... | collective-permute-start | bytes 552968 | tf_op jit(solution)/shard_map/ppermute | solution.py:26
  424.0 14.0 %collective-permute-start.22 = (f32[1,1,128]{1,2,0:T(8,128)S(1)}, f32[1,1,128]{1,2,0:T(8,128)S(1)}, u32[]{:S(2)}, u32[]{:S(2)}) collective-permute-start(f32[1,1,128]{1,2,0:T(8,128)S(1)} %get-tuple-element.26), channel_id=1, source_target_pairs={{1,0},{2,1},{3,2},{4,3},{5,4},{6,5},{7,6},{0,7},{9,8},{10,9},{11,1... | collective-permute-start | bytes 1544 | tf_op jit(solution)/shard_map/ppermute | solution.py:26
  428.1 16.8 %collective-permute-start.23 = (f32[1,1,128]{1,2,0:T(8,128)S(1)}, f32[1,1,128]{1,2,0:T(8,128)S(1)}, u32[]{:S(2)}, u32[]{:S(2)}) collective-permute-start(f32[1,1,128]{1,2,0:T(8,128)S(1)} %get-tuple-element.27), channel_id=1, source_target_pairs={{0,1},{1,2},{2,3},{3,4},{4,5},{5,6},{6,7},{7,0},{8,9},{9,10},{10,1... | collective-permute-start | bytes 1544 | tf_op jit(solution)/shard_map/ppermute | solution.py:24
  446.0 0.7 copy-start.9
  577.4 3.1 copy-start.10
  577.4 3.1 copy-start.12
  577.4 3.1 copy-start.14
  577.4 3.5 copy-start
  581.0 30.1 %collective-permute-start.24 = (f32[1,360,128]{1,2,0:T(8,128)S(1)}, f32[1,360,128]{1,2,0:T(8,128)S(1)}, u32[]{:S(2)}, u32[]{:S(2)}) collective-permute-start(f32[1,360,128]{1,2,0:T(8,128)S(1)} %pad_maximum_fusion.4), channel_id=1, source_target_pairs={{8,0},{16,8},{24,16},{32,24},{40,32},{48,40},{56,48},{64,56},{72,6... | collective-permute-start | bytes 552968 | tf_op jit(solution)/shard_map/ppermute | solution.py:26
  588.8 22.4 %collective-permute-start.25 = (f32[1,360,128]{1,2,0:T(8,128)S(1)}, f32[1,360,128]{1,2,0:T(8,128)S(1)}, u32[]{:S(2)}, u32[]{:S(2)}) collective-permute-start(f32[1,360,128]{1,2,0:T(8,128)S(1)} %pad_maximum_fusion.4), channel_id=1, source_target_pairs={{0,8},{8,16},{16,24},{24,32},{32,40},{40,48},{48,56},{56,64},{64,7... | collective-permute-start | bytes 552968 | tf_op jit(solution)/shard_map/ppermute | solution.py:24
  590.8 163.2 %copy-start.1 = (f32[1,360,64]{1,2,0:T(8,128)S(1)}, f32[1,360,64]{1,2,0:T(8,128)}, u32[]{:S(2)}) copy-start(f32[1,360,64]{1,2,0:T(8,128)} %get-tuple-element.24) | copy-start | bytes 276484
  590.8 14.1 %collective-permute-start.26 = (f32[1,1,128]{1,2,0:T(8,128)S(1)}, f32[1,1,128]{1,2,0:T(8,128)S(1)}, u32[]{:S(2)}, u32[]{:S(2)}) collective-permute-start(f32[1,1,128]{1,2,0:T(8,128)S(1)} %get-tuple-element.22), channel_id=1, source_target_pairs={{1,0},{2,1},{3,2},{4,3},{5,4},{6,5},{7,6},{0,7},{9,8},{10,9},{11,1... | collective-permute-start | bytes 1544 | tf_op jit(solution)/shard_map/ppermute | solution.py:26
  594.2 16.9 %collective-permute-start.27 = (f32[1,1,128]{1,2,0:T(8,128)S(1)}, f32[1,1,128]{1,2,0:T(8,128)S(1)}, u32[]{:S(2)}, u32[]{:S(2)}) collective-permute-start(f32[1,1,128]{1,2,0:T(8,128)S(1)} %get-tuple-element.23), channel_id=1, source_target_pairs={{0,1},{1,2},{2,3},{3,4},{4,5},{5,6},{6,7},{7,0},{8,9},{9,10},{10,1... | collective-permute-start | bytes 1544 | tf_op jit(solution)/shard_map/ppermute | solution.py:24
  611.4 25.0 %collective-permute-start.29 = (f32[1,360,128]{1,2,0:T(8,128)S(1)}, f32[1,360,128]{1,2,0:T(8,128)S(1)}, u32[]{:S(2)}, u32[]{:S(2)}) collective-permute-start(f32[1,360,128]{1,2,0:T(8,128)S(1)} %fusion.42), channel_id=1, source_target_pairs={{0,8},{8,16},{16,24},{24,32},{32,40},{40,48},{48,56},{56,64},{64,7... | collective-permute-start | bytes 552968 | tf_op jit(solution)/shard_map/ppermute | solution.py:24
  614.9 21.5 %collective-permute-start.28 = (f32[1,360,128]{1,2,0:T(8,128)S(1)}, f32[1,360,128]{1,2,0:T(8,128)S(1)}, u32[]{:S(2)}, u32[]{:S(2)}) collective-permute-start(f32[1,360,128]{1,2,0:T(8,128)S(1)} %fusion.42), channel_id=1, source_target_pairs={{8,0},{16,8},{24,16},{32,24},{40,32},{48,40},{56,48},{64,56},{72,6... | collective-permute-start | bytes 552968 | tf_op jit(solution)/shard_map/ppermute | solution.py:26
  616.9 14.0 %collective-permute-start.30 = (f32[1,1,128]{1,2,0:T(8,128)S(1)}, f32[1,1,128]{1,2,0:T(8,128)S(1)}, u32[]{:S(2)}, u32[]{:S(2)}) collective-permute-start(f32[1,1,128]{1,2,0:T(8,128)S(1)} %get-tuple-element.20), channel_id=1, source_target_pairs={{1,0},{2,1},{3,2},{4,3},{5,4},{6,5},{7,6},{0,7},{9,8},{10,9},{11,1... | collective-permute-start | bytes 1544 | tf_op jit(solution)/shard_map/ppermute | solution.py:26
  620.5 15.9 %collective-permute-start.31 = (f32[1,1,128]{1,2,0:T(8,128)S(1)}, f32[1,1,128]{1,2,0:T(8,128)S(1)}, u32[]{:S(2)}, u32[]{:S(2)}) collective-permute-start(f32[1,1,128]{1,2,0:T(8,128)S(1)} %get-tuple-element.21), channel_id=1, source_target_pairs={{0,1},{1,2},{2,3},{3,4},{4,5},{5,6},{6,7},{7,0},{8,9},{9,10},{10,1... | collective-permute-start | bytes 1544 | tf_op jit(solution)/shard_map/ppermute | solution.py:24
  637.3 174.6 %copy-start.5 = (f32[1,360,128]{1,2,0:T(8,128)S(1)}, f32[1,360,128]{1,2,0:T(8,128)}, u32[]{:S(2)}) copy-start(f32[1,360,128]{1,2,0:T(8,128)} %copy-done.4) | copy-start | bytes 552964
  754.0 30.4 %collective-permute-start.33 = (f32[1,360,128]{1,2,0:T(8,128)S(1)}, f32[1,360,128]{1,2,0:T(8,128)S(1)}, u32[]{:S(2)}, u32[]{:S(2)}) collective-permute-start(f32[1,360,128]{1,2,0:T(8,128)S(1)} %multiply_subtract_fusion.8), channel_id=1, source_target_pairs={{0,8},{8,16},{16,24},{24,32},{32,40},{40,48},{48,56},{56,64},{64,7... | collective-permute-start | bytes 552968 | tf_op jit(solution)/shard_map/ppermute | solution.py:24
  756.0 28.5 %collective-permute-start.32 = (f32[1,360,128]{1,2,0:T(8,128)S(1)}, f32[1,360,128]{1,2,0:T(8,128)S(1)}, u32[]{:S(2)}, u32[]{:S(2)}) collective-permute-start(f32[1,360,128]{1,2,0:T(8,128)S(1)} %multiply_subtract_fusion.8), channel_id=1, source_target_pairs={{8,0},{16,8},{24,16},{32,24},{40,32},{48,40},{56,48},{64,56},{72,6... | collective-permute-start | bytes 552968 | tf_op jit(solution)/shard_map/ppermute | solution.py:26
  758.5 14.4 %collective-permute-start.34 = (f32[1,1,128]{1,2,0:T(8,128)S(1)}, f32[1,1,128]{1,2,0:T(8,128)S(1)}, u32[]{:S(2)}, u32[]{:S(2)}) collective-permute-start(f32[1,1,128]{1,2,0:T(8,128)S(1)} %get-tuple-element.18), channel_id=1, source_target_pairs={{1,0},{2,1},{3,2},{4,3},{5,4},{6,5},{7,6},{0,7},{9,8},{10,9},{11,1... | collective-permute-start | bytes 1544 | tf_op jit(solution)/shard_map/ppermute | solution.py:26
  765.5 19.0 %collective-permute-start.35 = (f32[1,1,128]{1,2,0:T(8,128)S(1)}, f32[1,1,128]{1,2,0:T(8,128)S(1)}, u32[]{:S(2)}, u32[]{:S(2)}) collective-permute-start(f32[1,1,128]{1,2,0:T(8,128)S(1)} %get-tuple-element.19), channel_id=1, source_target_pairs={{0,1},{1,2},{2,3},{3,4},{4,5},{5,6},{6,7},{7,0},{8,9},{9,10},{10,1... | collective-permute-start | bytes 1544 | tf_op jit(solution)/shard_map/ppermute | solution.py:24
  784.7 27.2 %collective-permute-start.37 = (f32[1,360,128]{1,2,0:T(8,128)S(1)}, f32[1,360,128]{1,2,0:T(8,128)S(1)}, u32[]{:S(2)}, u32[]{:S(2)}) collective-permute-start(f32[1,360,128]{1,2,0:T(8,128)S(1)} %fusion.52), channel_id=1, source_target_pairs={{0,8},{8,16},{16,24},{24,32},{32,40},{40,48},{48,56},{56,64},{64,7... | collective-permute-start | bytes 552968 | tf_op jit(solution)/shard_map/ppermute | solution.py:24
  789.5 22.4 %collective-permute-start.36 = (f32[1,360,128]{1,2,0:T(8,128)S(1)}, f32[1,360,128]{1,2,0:T(8,128)S(1)}, u32[]{:S(2)}, u32[]{:S(2)}) collective-permute-start(f32[1,360,128]{1,2,0:T(8,128)S(1)} %fusion.52), channel_id=1, source_target_pairs={{8,0},{16,8},{24,16},{32,24},{40,32},{48,40},{56,48},{64,56},{72,6... | collective-permute-start | bytes 552968 | tf_op jit(solution)/shard_map/ppermute | solution.py:26
  791.5 14.8 %collective-permute-start.38 = (f32[1,1,128]{1,2,0:T(8,128)S(1)}, f32[1,1,128]{1,2,0:T(8,128)S(1)}, u32[]{:S(2)}, u32[]{:S(2)}) collective-permute-start(f32[1,1,128]{1,2,0:T(8,128)S(1)} %get-tuple-element.16), channel_id=1, source_target_pairs={{1,0},{2,1},{3,2},{4,3},{5,4},{6,5},{7,6},{0,7},{9,8},{10,9},{11,1... | collective-permute-start | bytes 1544 | tf_op jit(solution)/shard_map/ppermute | solution.py:26
  795.8 16.0 %collective-permute-start.39 = (f32[1,1,128]{1,2,0:T(8,128)S(1)}, f32[1,1,128]{1,2,0:T(8,128)S(1)}, u32[]{:S(2)}, u32[]{:S(2)}) collective-permute-start(f32[1,1,128]{1,2,0:T(8,128)S(1)} %get-tuple-element.17), channel_id=1, source_target_pairs={{0,1},{1,2},{2,3},{3,4},{4,5},{5,6},{6,7},{7,0},{8,9},{9,10},{10,1... | collective-permute-start | bytes 1544 | tf_op jit(solution)/shard_map/ppermute | solution.py:24
where the time goes:
time: 821 us; the launch traced here: 813 us
  blocking collectives  458 us (56%)
  starting transfers between devices  230 us (28%)
  waiting for transfers between devices  79.2 us (10%)
  local copies, waits for them, and re-layouts  17.8 us (2%)
  other arithmetic  17 us (2%)
    all_gather x2, blocking collectives, polar_filter(): slab_part = lax.all_gather(cap_panel, 'lon', axis=1, tiled=True)  240 us
    psum x2, blocking collectives, on_device(): slope = lax.psum(jnp.sum(gradient_now * search), ('tm', 'lon'))  217 us
    ppermute x20, starting transfers between devices, padded(): lax.ppermute(tail, axis, [(i, (i + 1) % count) for i in range(ends)])  145 us
    ppermute x20, starting transfers between devices, padded(): lax.ppermute(head, axis, [((i + 1) % count, i) for i in range(ends)])  85 us
    ppermute x20, waiting for transfers between devices, padded(): lax.ppermute(tail, axis, [(i, (i + 1) % count) for i in range(ends)])  75.2 us
  transfers between devices with their start and end apart: 40, of which 12 were waited for; matrix products, arithmetic and copies ran while one was open for 2% of the time, Pallas kernels for 0%

commit v1 on v0

v1 whole, which is shorter than its diff:
```python
import functools

import jax
import jax.numpy as jnp
import numpy as np
from jax import lax
from jax.experimental import pallas as pl
from jax.experimental.pallas import tpu as pltpu
from jax.sharding import PartitionSpec as P

CAP = 64
MW = 64
MESH = pl.DeviceIdType.MESH
OFF = 16
EXT = 8
F32 = jnp.float32


def tables(segments, length, rows):
    circle = segments * length
    harmonic = np.arange(MW)
    w = np.where(harmonic == 0, 1.0 / circle, 2.0 / circle)
    padded = -(-length // 128) * 128
    forward = np.zeros((segments, 2 * MW, padded), np.float32)
    inverse = np.zeros((segments, length + 16, 2 * MW), np.float32)
    for s in range(segments):
        a = 2 * np.pi * ((np.arange(length) + s * length)[:, None] * harmonic % circle) / circle
        forward[s, :MW, :length] = np.cos(a).T
        forward[s, MW:, :length] = np.sin(a).T
        a = 2 * np.pi * ((np.arange(length + 16) - 8 + s * length)[:, None] * harmonic % circle) / circle
        inverse[s] = np.concatenate([w * np.cos(a), w * np.sin(a)], axis=1)
    phi = (90.0 - (rows - np.arange(rows) - 0.5) * 0.125) * (np.pi / 180.0)
    bend = 1.0 / (np.cos(phi) + 0.5) ** 2
    shrink = np.zeros(rows)
    shrink[rows - CAP:] = 0.9 * (np.arange(CAP) + 1.0) / CAP
    row = np.zeros((8, rows), np.float32)
    row[0] = bend
    row[1] = -2.0 * (bend + 1.0)
    row[2] = shrink
    row[3] = 1.0 - shrink
    return forward, inverse, row


def kernel(
    NT, N, first_ref, obs_ref, track_ref, land_ref, bw_ref, fwd_ref, inv_ref, row_ref,
    out_a, out_g,
    E, G, U, B, W, obs, track, land, fwd, inv, V, TV, T2V, Y, V0, padded, amp, rs_buf, quarter,
    z_buf, AT, dots, res_a, res_g,
    lsem, hs, hr, bs, br, xs, xr, zs, zr, ats, atr, ds_, dr,
):
    tm = lax.axis_index("tm")
    lon = lax.axis_index("lon")
    x, zh = lon // 2, lon % 2
    zl, k = tm // 8, tm % 8
    rows = 128

    def inside(t):
        return (t >= 0) & (t < NT)

    def when_t(dt, fn):
        if dt == 0:
            fn()
        else:
            pl.when(inside(tm + dt))(fn)

    def lon_at(d):
        return lax.rem(lon + d + 8, 8)

    own = pl.ds(OFF, N)
    loads = [
        pltpu.make_async_copy(first_ref.at[0], E.at[2, own], lsem.at[0]),
        pltpu.make_async_copy(bw_ref, B.at[own], lsem.at[1]),
        pltpu.make_async_copy(obs_ref.at[0], obs, lsem.at[2]),
        pltpu.make_async_copy(track_ref.at[0], track, lsem.at[3]),
        pltpu.make_async_copy(land_ref, land, lsem.at[4]),
        pltpu.make_async_copy(fwd_ref.at[lon], fwd, lsem.at[5]),
        pltpu.make_async_copy(inv_ref.at[lon], inv, lsem.at[6]),
    ]
    for c in loads:
        c.start()

    barrier = pltpu.get_barrier_semaphore()

    def greet(t, l):
        pl.semaphore_signal(barrier, inc=1, device_id={"tm": t, "lon": l}, device_id_type=MESH)

    count = jnp.int32(0)
    for dt in (-2, -1, 0, 1, 2):
        steps = [d for d in range(4) if (dt, d) != (0, 0)]
        dls = [2 * d for d in steps] + ([-1, 1] if abs(dt) < 2 else [])

        def signals(dt=dt, dls=dls):
            for dl in dls:
                greet(tm + dt, lon_at(dl))

        when_t(dt, signals)
        count = count + jnp.where(inside(tm + dt), len(dls), 0)
    for d in range(1, 8):
        greet(zl * 8 + lax.rem(k + d, 8), lon)
    z = zh * 8 + zl
    for d in range(1, 16):
        zz = lax.rem(z + d, 16)
        greet(lax.rem(zz, 8) * 8 + k, x * 2 + zz // 8)
    count = count + 7 + 15

    for dt in (-2, -1, 1, 2):

        @pl.when(jnp.logical_not(inside(tm + dt)))
        def _(dt=dt):
            for X in (E, G, U):
                X[2 + dt] = jnp.zeros(X.shape[1:], F32)
            for p in range(2):
                AT[p, 2 + dt] = jnp.zeros(AT.shape[2:], F32)

    padded[pl.ds(N, padded.shape[0] - N)] = jnp.zeros((padded.shape[0] - N, rows), F32)

    pl.semaphore_wait(barrier, count)

    def remote(src, dst, send, recv, t, l):
        return pltpu.make_async_remote_copy(
            src_ref=src, dst_ref=dst, send_sem=send, recv_sem=recv,
            device_id={"tm": t, "lon": l}, device_id_type=MESH,
        )

    head, tail = pl.ds(OFF, 8), pl.ds(OFF + N - 8, 8)
    left, right = pl.ds(OFF - 8, 8), pl.ds(OFF + N, 8)
    halo_kinds = [(dt, 0) for dt in (1, -1, 2, -2)] + [(dt, dl) for dt in (0, 1, -1) for dl in (1, -1)]

    def halo_copy(p, X, i, sending):
        dt, dl = halo_kinds[i]
        src, dst = (own, own) if dl == 0 else ((tail, left) if dl == 1 else (head, right))
        return remote(X.at[2, src], X.at[2 - dt, dst], hs.at[p, i], hr.at[p, i], tm + dt, lon_at(dl))

    order = [4, 5, 6, 7, 8, 9, 0, 1, 2, 3]

    def halo_send(p, X):
        for i in order:
            when_t(halo_kinds[i][0], lambda i=i: halo_copy(p, X, i, True).start())

    def halo_wait(p, X):
        for i in order:
            when_t(-halo_kinds[i][0], lambda i=i: halo_copy(p, X, i, False).wait_recv())

    def halo_done(p, X):
        for i in order:
            when_t(halo_kinds[i][0], lambda i=i: halo_copy(p, X, i, True).wait_send())

    edge_b = [
        remote(B.at[tail], B.at[left], bs.at[0], br.at[0], tm, lon_at(1)),
        remote(B.at[head], B.at[right], bs.at[1], br.at[1], tm, lon_at(-1)),
    ]

    loads[0].wait()
    halo_send(0, E)
    loads[1].wait()
    for c in edge_b:
        c.start()

    lane = lax.broadcasted_iota(jnp.int32, (8, rows), 1)
    first_lane, last_lane = lane[:1] == 0, lane[:1] == rows - 1
    bend = row_ref[0:1]
    centre = row_ref[1:2]
    shrink = row_ref[2:3]
    keep = row_ref[3:4]

    def flat(ref, start, n):
        v = ref[pl.ds(start, n)]
        up, down = ref[pl.ds(start + 1, n)], ref[pl.ds(start - 1, n)]
        lo = jnp.where(first_lane, 0.0, pltpu.roll(v, 1, axis=1))
        hi = jnp.where(last_lane, 0.0, pltpu.roll(v, rows - 1, axis=1))
        return bend * (up + down) + (lo + hi) + centre * v

    ext_chunks = [(EXT, 96), (EXT + 96, 96), (EXT + 192, 96), (EXT + 288, N + 16 - 288)]
    own_chunks = [(OFF + c, 72) for c in range(0, N, 72)]
    centre_t2 = jnp.where((tm == 0) | (tm == NT - 1), 5.0, 6.0).astype(F32)

    def second(a, b, c):
        return a + b - 2.0 * c

    def second2(a, b, c, d, e):
        return a + e - 4.0 * (b + d) + centre_t2 * c

    def operator(field, emit):
        for s, n in ext_chunks:
            Y[pl.ds(s, n)] = B[pl.ds(s, n)] * (TV[pl.ds(s, n)] + flat(field, s, n))
        for s, n in own_chunks:
            emit(s, n, B[pl.ds(s, n)] * (T2V[pl.ds(s, n)] + flat(TV, s, n)) + flat(Y, s, n))

    for c in loads[2:5]:
        c.wait()
    W[...] = track[...].astype(F32) * (1.0 - land[...].astype(F32))

    halo_wait(0, E)
    for c in edge_b:
        c.wait_recv()
    for s, n in ext_chunks:
        r = pl.ds(s, n)
        TV[r] = second(E[1, r], E[3, r], E[2, r])
    for s, n in own_chunks:
        r = pl.ds(s, n)
        T2V[r] = second2(E[0, r], E[1, r], E[2, r], E[3, r], E[4, r])

    def emit_g(s, n, u):
        l = pl.ds(s - OFF, n)
        g = W[l] * (E[2, pl.ds(s, n)] - obs[l]) + u
        G[2, pl.ds(s, n)] = g
        padded[l] = g

    operator(E.at[2], emit_g)
    for c in loads[5:]:
        c.wait()

    half = lax.broadcasted_iota(jnp.int32, (MW, rows), 1) < MW

    def rs_copy(p, d):
        q = lax.rem(x + d, 4)
        return remote(
            amp.at[p, pl.ds(16 * q, 16)], rs_buf.at[p, d], xs.at[p, d], xr.at[p, d], tm, q * 2 + zh
        )

    def z_copy(p):
        return remote(quarter.at[p, 0], z_buf.at[p], zs.at[p], zr.at[p], tm, lon + 1 - 2 * zh)

    at_kinds = [(dt, d) for dt in (0, 1, -1, 2, -2) for d in range(4) if (dt, d) != (0, 0)]

    def at_copy(p, i):
        dt, d = at_kinds[i]
        xx = lax.rem(x + d, 4)
        return remote(
            quarter.at[p, 1], AT.at[p, 2 - dt, pl.ds(16 * x, 16)], ats.at[p, i], atr.at[p, i], tm + dt, xx * 2 + zh
        )

    def at_recv(p, i):
        dt, d = at_kinds[i]
        xx = lax.rem(x - d + 4, 4)
        return remote(
            quarter.at[p, 1], AT.at[p, 2 - dt, pl.ds(16 * xx, 16)], ats.at[p, i], atr.at[p, i], tm, lon
        )

    def transform_start(p):
        part = lax.dot(fwd[...], padded[...], precision=lax.Precision.HIGHEST, preferred_element_type=F32)
        amp[p] = jnp.where(half, pltpu.roll(part[:MW], MW, axis=1), part[MW:])
        for d in (1, 2, 3):
            rs_copy(p, d).start()

    def transform_cross(p):
        total = amp[p, pl.ds(16 * x, 16)]
        for d in (1, 2, 3):
            rs_copy(p, d).wait_recv()
            total = total + rs_buf[p, d]
        quarter[p, 0] = total
        z_copy(p).start()

    def transform_spread(p):
        z_copy(p).wait_recv()
        total = quarter[p, 0] + z_buf[p]
        quarter[p, 1] = total
        for i, (dt, _) in enumerate(at_kinds):
            when_t(dt, lambda i=i: at_copy(p, i).start())
        AT[p, 2, pl.ds(16 * x, 16)] = total

    def transform_finish(p):
        for i, (dt, _) in enumerate(at_kinds):
            when_t(-dt, lambda i=i: at_recv(p, i).wait_recv())

    def transform_done(p):
        for d in (1, 2, 3):
            rs_copy(p, d).wait_send()
        z_copy(p).wait_send()
        for i, (dt, _) in enumerate(at_kinds):
            when_t(dt, lambda i=i: at_copy(p, i).wait_send())

    def stack(a):
        c = jnp.where(half, 0.0, pltpu.roll(a, MW, axis=1))
        s = jnp.where(half, 0.0, a)
        return jnp.concatenate([c, s], axis=0)

    def filtered(p, X, field):
        a = [AT[p, i] for i in range(5)]
        three = jnp.concatenate(
            [stack(a[2]), stack(second(a[1], a[3], a[2])), stack(second2(*a))], axis=1
        )
        for s, n in ext_chunks:
            r = pl.ds(s, n)
            smooth = lax.dot(
                inv[pl.ds(s - EXT, n)], three, precision=lax.Precision.HIGHEST, preferred_element_type=F32
            )
            field[r] = keep * X[2, r] + shrink * smooth[:, :rows]
            TV[r] = keep * second(X[1, r], X[3, r], X[2, r]) + shrink * smooth[:, rows:2 * rows]
            T2V[r] = (
                keep * second2(X[0, r], X[1, r], X[2, r], X[3, r], X[4, r])
                + shrink * smooth[:, 2 * rows:]
            )

    starts, sizes = (0, 8, 12), (8, 4, 16)

    def stage_place(stage):
        return (k, x, z)[stage]

    def stage_device(stage, place):
        if stage == 0:
            return zl * 8 + place, lon
        if stage == 1:
            return tm, place * 2 + zh
        return lax.rem(place, 8) * 8 + k, x * 2 + place // 8

    def dot_copy(p, stage, d):
        size, start = sizes[stage], starts[stage]
        mine = stage_place(stage)
        t, l = stage_device(stage, lax.rem(mine + d, size))
        slot = dots.at[p, start + mine]
        return remote(slot, slot, ds_.at[p, start + d], dr.at[p, start + d], t, l)

    def dot_recv(p, stage, d):
        size, start = sizes[stage], starts[stage]
        mine = stage_place(stage)
        slot = dots.at[p, start + lax.rem(mine - d + size, size)]
        return remote(slot, slot, ds_.at[p, start + d], dr.at[p, start + d], tm, lon)

    def dot_send(p, stage, tile):
        dots[p, starts[stage] + stage_place(stage)] = tile
        for d in range(1, sizes[stage]):
            dot_copy(p, stage, d).start()

    def dot_take(p, stage):
        for d in range(1, sizes[stage]):
            dot_recv(p, stage, d).wait_recv()
        total = dots[p, starts[stage]]
        for i in range(1, sizes[stage]):
            total = total + dots[p, starts[stage] + i]
        return total

    def dot_done(p):
        for stage in range(3):
            for d in range(1, sizes[stage]):
                dot_copy(p, stage, d).wait_send()

    row8 = lax.broadcasted_iota(jnp.int32, (8, rows), 0)

    def pack(slope, curve):
        return jnp.where(row8 == 0, slope, jnp.where(row8 == 1, curve, 0.0))

    def ratio(tile):
        return jnp.sum(tile[0:1], axis=1, keepdims=True) / jnp.sum(tile[1:2], axis=1, keepdims=True)

    transform_start(0)
    halo_send(1, G)
    transform_cross(0)
    transform_spread(0)
    transform_finish(0)
    halo_wait(1, G)
    filtered(0, G, V0)
    acc = [jnp.zeros((1, rows), F32), jnp.zeros((1, rows), F32)]

    def emit_u(s, n, u):
        l, r = pl.ds(s - OFF, n), pl.ds(s, n)
        v = V0[r]
        u = W[l] * v + u
        U[2, r] = u
        padded[l] = u
        acc[0] = acc[0] + jnp.sum(G[2, r] * v, axis=0, keepdims=True)
        acc[1] = acc[1] + jnp.sum(v * u, axis=0, keepdims=True)

    operator(V0, emit_u)

    transform_start(1)
    dot_send(0, 0, pack(*acc))
    halo_send(2, U)
    transform_cross(1)
    dot_send(0, 1, dot_take(0, 0))
    dot_send(0, 2, dot_take(0, 1))
    transform_spread(1)
    step0 = ratio(dot_take(0, 2))
    transform_finish(1)
    halo_wait(2, U)
    filtered(1, U, V)
    acc[0] = acc[1] = jnp.zeros((1, rows), F32)

    def emit_last(s, n, u1):
        l, r = pl.ds(s - OFF, n), pl.ds(s, n)
        v1, v0, u0 = V[r], V0[r], U[2, r]
        u1 = W[l] * v1 + u1
        search = v0 - step0 * v1
        curved = u0 - step0 * u1
        gradient = G[2, r] - step0 * u0
        acc[0] = acc[0] + jnp.sum(gradient * search, axis=0, keepdims=True)
        acc[1] = acc[1] + jnp.sum(search * curved, axis=0, keepdims=True)
        V[r] = search
        obs[l] = curved
        res_g[l] = gradient
        res_a[l] = E[2, r] - step0 * v0

    operator(V, emit_last)
    dot_send(1, 0, pack(*acc))
    dot_send(1, 1, dot_take(1, 0))
    dot_send(1, 2, dot_take(1, 1))
    step1 = ratio(dot_take(1, 2))
    res_a[...] = res_a[...] - step1 * V[own]
    res_g[...] = res_g[...] - step1 * obs[...]
    ca = pltpu.make_async_copy(res_a, out_a.at[0], lsem.at[0])
    cg = pltpu.make_async_copy(res_g, out_g.at[0], lsem.at[1])
    ca.start()
    cg.start()
    for p, X in enumerate((E, G, U)):
        halo_done(p, X)
    for c in edge_b:
        c.wait_send()
    for p in range(2):
        transform_done(p)
        dot_done(p)
    ca.wait()
    cg.wait()


def on_device(NT, NL, first, obs, track, land, bw):
    _, N, rows = first.shape
    forward, inverse, row = tables(NL, N, rows)
    plane = pltpu.VMEM((N + 32, rows), F32)
    planes = pltpu.VMEM((5, N + 32, rows), F32)
    flat = pltpu.VMEM((N, rows), F32)
    whole = pltpu.VMEM((N, rows), jnp.int32)
    dma = pltpu.SemaphoreType.DMA
    hbm = pl.BlockSpec(memory_space=pl.ANY)
    return pl.pallas_call(
        functools.partial(kernel, NT, N),
        out_shape=[jax.ShapeDtypeStruct(first.shape, F32)] * 2,
        in_specs=[hbm] * 7 + [pl.BlockSpec(memory_space=pltpu.VMEM)],
        out_specs=[hbm] * 2,
        scratch_shapes=[
            planes, planes, planes,
            plane, flat, flat, whole, whole,
            pltpu.VMEM(forward.shape[1:], F32), pltpu.VMEM(inverse.shape[1:], F32),
            plane, plane, plane, plane, plane,
            pltpu.VMEM((forward.shape[2], rows), F32),
            pltpu.VMEM((2, MW, rows), F32),
            pltpu.VMEM((2, 4, 16, rows), F32),
            pltpu.VMEM((2, 2, 16, rows), F32),
            pltpu.VMEM((2, 16, rows), F32),
            pltpu.VMEM((2, 5, MW, rows), F32),
            pltpu.VMEM((2, 28, 8, rows), F32),
            flat, flat,
            dma((7,)), dma((3, 10)), dma((3, 10)), dma((2,)), dma((2,)),
            dma((2, 4)), dma((2, 4)), dma((2,)), dma((2,)), dma((2, 19)), dma((2, 19)),
            dma((2, 28)), dma((2, 28)),
        ],
        compiler_params=pltpu.CompilerParams(
            collective_id=0, has_side_effects=True, vmem_limit_bytes=40 * 1024 * 1024
        ),
    )(first, obs, track, land, bw, forward, inverse, row)


def solution(mesh):
    in_specs = (
        P("tm", "lon", None),
        P("tm", "lon", None),
        P("tm", "lon", None),
        P("lon", None),
        P("lon", None),
    )
    out_specs = (P("tm", "lon", None), P("tm", "lon", None))
    return jax.shard_map(
        functools.partial(on_device, mesh.shape["tm"], mesh.shape["lon"]),
        mesh=mesh, in_specs=in_specs, out_specs=out_specs, check_vma=False,
    )
```

time: 821 us -> 105 us (0.13)
  blocking collectives: 458 us -> 0 us
  starting transfers between devices: 230 us -> 0 us
  Pallas kernels: 0 us -> 94.3 us
  waiting for transfers between devices: 79.2 us -> 0 us
  other arithmetic: 17 us -> 0 us
  local copies, waits for them, and re-layouts: 17.8 us -> 9.44 us
    all_gather x2 -> x0, blocking collectives: 240 us -> none  [polar_filter(): slab_part = lax.all_gather(cap_panel, 'lon', axis=1, tiled=True)]
    ppermute x40 -> x0, starting transfers between devices: 230 us -> none  [the longest x20 145 us: padded(): lax.ppermute(tail, axis, [(i, (i + 1) % count) for i in range(ends)])]
    psum x2 -> x0, blocking collectives: 217 us -> none  [on_device(): slope = lax.psum(jnp.sum(gradient_now * search), ('tm', 'lon'))]
    pallas_call x0 -> x1, Pallas kernels: none -> 94.3 us  [on_device(): pl.pallas_call(functools.partial(kernel, NT, N), out_shape=[jax.ShapeDtyp...]
    ppermute x40 -> x0, waiting for transfers between devices: 79.2 us -> none  [the longest x20 75.2 us: padded(): lax.ppermute(tail, axis, [(i, (i + 1) % count) for i in range(ends)])]
  transfers between devices with their start and end apart: 40 -> 0, of which waited for: 12 -> 0; matrix products, arithmetic and copies ran while one was open for 2% -> 0% of each run, Pallas kernels for 0% -> 0%
where the time goes in v1:
time: 105 us; the launch traced here: 104 us
  Pallas kernels  94.3 us (90%)
  local copies, waits for them, and re-layouts  9.44 us (9%)
    pallas_call x1, Pallas kernels, on_device(): pl.pallas_call(functools.partial(kernel, NT, N), out_shape=[jax.ShapeDtyp...  94.3 us
    unnamed x18, local copies, waits for them, and re-layouts  9.44 us

profile of v1, /device:TPU:1, one launch (start us, length us, event | category | flops | bytes accessed | tf_op | source)
XLA Modules:
  0.0 104.4 jit_solution(18322041202978535471)
XLA Ops:
  0.6 0.0 copy-start
  0.6 1.4 %copy-done = f32[8,128,384]{2,1,0:T(8,128)S(1)} copy-done((f32[8,128,384]{2,1,0:T(8,128)S(1)}, f32[8,128,384]{2,1,0:T(8,128)}, u32[]{:S(2)}) %copy-start) | copy-done | bytes 1572888
  2.0 0.0 copy-start.1
  2.0 1.4 %copy-done.1 = f32[8,376,128]{2,1,0:T(8,128)S(1)} copy-done((f32[8,376,128]{2,1,0:T(8,128)S(1)}, f32[8,376,128]{2,1,0:T(8,128)}, u32[]{:S(2)}) %copy-start.1) | copy-done | bytes 1540120
  3.4 0.0 copy-start.2
  3.4 0.9 copy-done.2
  4.4 0.0 copy-start.3
  4.4 0.9 copy-done.3
  5.3 0.0 copy-start.4
  5.3 0.9 copy-done.4
  6.2 0.0 copy-start.5
  6.2 0.9 copy-done.5
  7.1 0.0 copy-start.6
  7.1 0.9 copy-done.6
  8.1 0.0 copy-start.7
  8.1 0.7 copy-done.7
  8.7 94.3 %shard_map.95 = (f32[1,360,128]{2,1,0:T(8,128)S(1)}, f32[1,360,128]{2,1,0:T(8,128)S(1)}) custom-call(f32[1,360,128]{2,1,0:T(8,128)S(1)} %copy-done.2, f32[1,360,128]{2,1,0:T(8,128)S(1)} %copy-done.3, s32[1,360,128]{2,1,0:T(8,128)S(1)} %copy-done.4, s32[360,128]{1,0:T(8,128)S(1)} %copy-done.5, f32[360,128]{1,0:T(8,128)S(1)} %copy-done.6, ...), custom_call_target="tpu_custom_call" | custom-call | tf_op jit(solution)/shard_map/pallas_call | solution.py:424
  103.0 0.7 copy.12
  103.7 0.7 copy.13
Async XLA Ops:
  0.6 1.4 %copy-start = (f32[8,128,384]{2,1,0:T(8,128)S(1)}, f32[8,128,384]{2,1,0:T(8,128)}, u32[]{:S(2)}) copy-start(f32[8,128,384]{2,1,0:T(8,128)} %constant.6.clone.fwd_ref) | copy-start | bytes 4718596
  2.0 1.4 %copy-start.1 = (f32[8,376,128]{2,1,0:T(8,128)S(1)}, f32[8,376,128]{2,1,0:T(8,128)}, u32[]{:S(2)}) copy-start(f32[8,376,128]{2,1,0:T(8,128)} %constant.7.clone.inv_ref) | copy-start | bytes 4620292
  3.4 0.9 copy-start.2
  4.4 0.9 copy-start.3
  5.3 0.9 copy-start.4
  6.2 0.9 copy-start.5
  7.1 0.9 copy-start.6
  8.1 0.7 copy-start.7

commit v2 on v1

--- a/solution.py
+++ b/solution.py
@@ -45,8 +45,8 @@
     NT, N, first_ref, obs_ref, track_ref, land_ref, bw_ref, fwd_ref, inv_ref, row_ref,
     out_a, out_g,
     E, G, U, B, W, obs, track, land, fwd, inv, V, TV, T2V, Y, V0, padded, amp, rs_buf, quarter,
-    z_buf, AT, dots, res_a, res_g,
-    lsem, hs, hr, bs, br, xs, xr, zs, zr, ats, atr, ds_, dr,
+    z_buf, AT, dots_a, dots_b, ts, tr, ls, lr, res_a, res_g,
+    hello, lsem, hs, hr, es, er, rs_, rr, xs, xr, zs, zr, ats, atr, ds_, dr,
 ):
     tm = lax.axis_index("tm")
     lon = lax.axis_index("lon")
@@ -76,32 +76,34 @@
         pltpu.make_async_copy(fwd_ref.at[lon], fwd, lsem.at[5]),
         pltpu.make_async_copy(inv_ref.at[lon], inv, lsem.at[6]),
     ]
-    for c in loads:
-        c.start()
+    loads[0].start()
 
     barrier = pltpu.get_barrier_semaphore()
 
-    def greet(t, l):
-        pl.semaphore_signal(barrier, inc=1, device_id={"tm": t, "lon": l}, device_id_type=MESH)
-
-    count = jnp.int32(0)
-    for dt in (-2, -1, 0, 1, 2):
-        steps = [d for d in range(4) if (dt, d) != (0, 0)]
-        dls = [2 * d for d in steps] + ([-1, 1] if abs(dt) < 2 else [])
-
-        def signals(dt=dt, dls=dls):
-            for dl in dls:
-                greet(tm + dt, lon_at(dl))
-
-        when_t(dt, signals)
-        count = count + jnp.where(inside(tm + dt), len(dls), 0)
+    def greet(t, l, sem=barrier):
+        pl.semaphore_signal(sem, inc=1, device_id={"tm": t, "lon": l}, device_id_type=MESH)
+
+    z = zh * 8 + zl
+
+    def on_z(place, xx):
+        place = lax.rem(place + 16, 16)
+        return lax.rem(place, 8) * 8 + k, lax.rem(xx + 4, 4) * 2 + place // 8
+
+    fours = [(dz, dx) for dz in (4, -4) for dx in (0, 1, -1)]
+    for dz, dx in fours:
+        greet(*on_z(z + dz, x + dx))
+    for dz in (3, -3, 2, -2, 1, -1):
+        greet(*on_z(z + dz, x))
     for d in range(1, 8):
         greet(zl * 8 + lax.rem(k + d, 8), lon)
-    z = zh * 8 + zl
-    for d in range(1, 16):
-        zz = lax.rem(z + d, 16)
-        greet(lax.rem(zz, 8) * 8 + k, x * 2 + zz // 8)
-    count = count + 7 + 15
+    for d in range(1, 4):
+        greet(tm, lon_at(2 * d))
+    count = jnp.int32(len(fours) + 6 + 7 + 3)
+    for dt in (-2, -1, 1, 2):
+        when_t(dt, lambda dt=dt: greet(tm + dt, lon))
+        count = count + jnp.where(inside(tm + dt), 1, 0)
+    for c in loads[1:]:
+        c.start()
 
     for dt in (-2, -1, 1, 2):
 
@@ -111,10 +113,16 @@
                 X[2 + dt] = jnp.zeros(X.shape[1:], F32)
             for p in range(2):
                 AT[p, 2 + dt] = jnp.zeros(AT.shape[2:], F32)
+            if abs(dt) == 1:
+                for p in range(3):
+                    tr[p, (dt + 1) // 2] = jnp.zeros(tr.shape[2:], F32)
 
     padded[pl.ds(N, padded.shape[0] - N)] = jnp.zeros((padded.shape[0] - N, rows), F32)
 
-    pl.semaphore_wait(barrier, count)
+    with jax.named_scope("entry barrier"):
+        pl.semaphore_wait(barrier, count)
+    for dz, dx in fours:
+        greet(*on_z(z + dz, x + dx), sem=hello)
 
     def remote(src, dst, send, recv, t, l):
         return pltpu.make_async_remote_copy(
@@ -122,39 +130,78 @@
             device_id={"tm": t, "lon": l}, device_id_type=MESH,
         )
 
-    head, tail = pl.ds(OFF, 8), pl.ds(OFF + N - 8, 8)
-    left, right = pl.ds(OFF - 8, 8), pl.ds(OFF + N, 8)
-    halo_kinds = [(dt, 0) for dt in (1, -1, 2, -2)] + [(dt, dl) for dt in (0, 1, -1) for dl in (1, -1)]
-
-    def halo_copy(p, X, i, sending):
-        dt, dl = halo_kinds[i]
-        src, dst = (own, own) if dl == 0 else ((tail, left) if dl == 1 else (head, right))
-        return remote(X.at[2, src], X.at[2 - dt, dst], hs.at[p, i], hr.at[p, i], tm + dt, lon_at(dl))
-
-    order = [4, 5, 6, 7, 8, 9, 0, 1, 2, 3]
+    shifts = (1, -1, 2, -2)
+
+    def halo_copy(p, X, i):
+        dt = shifts[i]
+        return remote(X.at[2, own], X.at[2 - dt, own], hs.at[p, i], hr.at[p, i], tm + dt, lon)
 
     def halo_send(p, X):
-        for i in order:
-            when_t(halo_kinds[i][0], lambda i=i: halo_copy(p, X, i, True).start())
+        for i, dt in enumerate(shifts):
+            when_t(dt, lambda i=i: halo_copy(p, X, i).start())
 
     def halo_wait(p, X):
-        for i in order:
-            when_t(-halo_kinds[i][0], lambda i=i: halo_copy(p, X, i, False).wait_recv())
+        for i, dt in enumerate(shifts):
+            when_t(-dt, lambda i=i: halo_copy(p, X, i).wait_recv())
 
     def halo_done(p, X):
-        for i in order:
-            when_t(halo_kinds[i][0], lambda i=i: halo_copy(p, X, i, True).wait_send())
-
-    edge_b = [
-        remote(B.at[tail], B.at[left], bs.at[0], br.at[0], tm, lon_at(1)),
-        remote(B.at[head], B.at[right], bs.at[1], br.at[1], tm, lon_at(-1)),
-    ]
-
-    loads[0].wait()
-    halo_send(0, E)
+        for i, dt in enumerate(shifts):
+            when_t(dt, lambda i=i: halo_copy(p, X, i).wait_send())
+
+    first_row, last_row = OFF, OFF + N - 1
+
+    def edge_copy(p, i):
+        return remote(ts.at[p], tr.at[p, i], es.at[p, i], er.at[p, i], tm + (1, -1)[i], lon)
+
+    def edge_send(p, X):
+        ts[p, 0:1] = X[2, first_row:first_row + 1]
+        ts[p, 1:2] = X[2, last_row:last_row + 1]
+        for i, dt in enumerate((1, -1)):
+            when_t(dt, lambda i=i: edge_copy(p, i).start())
+
+    def rim_copy(p, i):
+        return remote(ls.at[p, i], lr.at[p, i], rs_.at[p, i], rr.at[p, i], tm, lon_at((1, -1)[i]))
+
+    def rim_send(p, X):
+        for i, dt in enumerate((1, -1)):
+            when_t(-dt, lambda i=i: edge_copy(p, i).wait_recv())
+        bent = tr[p, 0] + tr[p, 1] - 2.0 * ts[p]
+        ls[p, 0, 0:1] = X[2, last_row:last_row + 1]
+        ls[p, 0, 1:2] = X[2, last_row - 1:last_row]
+        ls[p, 0, 2:3] = bent[1:2]
+        ls[p, 0, 3:4] = B[last_row:last_row + 1]
+        ls[p, 1, 0:1] = X[2, first_row:first_row + 1]
+        ls[p, 1, 1:2] = X[2, first_row + 1:first_row + 2]
+        ls[p, 1, 2:3] = bent[0:1]
+        ls[p, 1, 3:4] = B[first_row:first_row + 1]
+        for i in range(2):
+            rim_copy(p, i).start()
+
+    def rim_take(p, X):
+        for i in range(2):
+            rim_copy(p, i).wait_recv()
+        for i, (near, far) in enumerate(((first_row - 1, first_row - 2), (last_row + 1, last_row + 2))):
+            X[2, near:near + 1] = lr[p, i, 0:1]
+            X[2, far:far + 1] = lr[p, i, 1:2]
+            X[1, near:near + 1] = lr[p, i, 2:3] + 2.0 * lr[p, i, 0:1]
+            X[3, near:near + 1] = jnp.zeros((1, rows), F32)
+            if p == 0:
+                B[near:near + 1] = lr[p, i, 3:4]
+
+    def edge_done(p):
+        for i, dt in enumerate((1, -1)):
+            when_t(dt, lambda i=i: edge_copy(p, i).wait_send())
+            rim_copy(p, i).wait_send()
+
+    with jax.named_scope("guess edges"):
+        loads[0].wait()
+        edge_send(0, E)
+        halo_send(0, E)
     loads[1].wait()
-    for c in edge_b:
-        c.start()
+    with jax.named_scope("far hello"):
+        pl.semaphore_wait(hello, len(fours))
+    with jax.named_scope("guess rim"):
+        rim_send(0, E)
 
     lane = lax.broadcasted_iota(jnp.int32, (8, rows), 1)
     first_lane, last_lane = lane[:1] == 0, lane[:1] == rows - 1
@@ -186,13 +233,15 @@
         for s, n in own_chunks:
             emit(s, n, B[pl.ds(s, n)] * (T2V[pl.ds(s, n)] + flat(TV, s, n)) + flat(Y, s, n))
 
-    for c in loads[2:5]:
-        c.wait()
-    W[...] = track[...].astype(F32) * (1.0 - land[...].astype(F32))
-
-    halo_wait(0, E)
-    for c in edge_b:
-        c.wait_recv()
+    with jax.named_scope("weights"):
+        for c in loads[2:5]:
+            c.wait()
+        W[...] = track[...].astype(F32) * (1.0 - land[...].astype(F32))
+
+    with jax.named_scope("guess halo wait"):
+        halo_wait(0, E)
+    with jax.named_scope("guess rim wait"):
+        rim_take(0, E)
     for s, n in ext_chunks:
         r = pl.ds(s, n)
         TV[r] = second(E[1, r], E[3, r], E[2, r])
@@ -206,7 +255,8 @@
         G[2, pl.ds(s, n)] = g
         padded[l] = g
 
-    operator(E.at[2], emit_g)
+    with jax.named_scope("first operator"):
+        operator(E.at[2], emit_g)
     for c in loads[5:]:
         c.wait()
 
@@ -292,64 +342,83 @@
                 + shrink * smooth[:, 2 * rows:]
             )
 
-    starts, sizes = (0, 8, 12), (8, 4, 16)
+    sizes = (32, 16)
 
     def stage_place(stage):
-        return (k, x, z)[stage]
+        return (x * 8 + k, z)[stage]
 
     def stage_device(stage, place):
         if stage == 0:
-            return zl * 8 + place, lon
-        if stage == 1:
-            return tm, place * 2 + zh
-        return lax.rem(place, 8) * 8 + k, x * 2 + place // 8
+            return zl * 8 + lax.rem(place, 8), (place // 8) * 2 + zh
+        return on_z(place, x)
+
+    def dot_slots(stage):
+        return (dots_a, dots_b)[stage]
 
     def dot_copy(p, stage, d):
-        size, start = sizes[stage], starts[stage]
-        mine = stage_place(stage)
+        size, mine, slots = sizes[stage], stage_place(stage), dot_slots(stage)
         t, l = stage_device(stage, lax.rem(mine + d, size))
-        slot = dots.at[p, start + mine]
-        return remote(slot, slot, ds_.at[p, start + d], dr.at[p, start + d], t, l)
+        slot = slots.at[p, mine]
+        return remote(slot, slot, ds_.at[p, stage, d], dr.at[p, stage, d], t, l)
 
     def dot_recv(p, stage, d):
-        size, start = sizes[stage], starts[stage]
-        mine = stage_place(stage)
-        slot = dots.at[p, start + lax.rem(mine - d + size, size)]
-        return remote(slot, slot, ds_.at[p, start + d], dr.at[p, start + d], tm, lon)
-
-    def dot_send(p, stage, tile):
-        dots[p, starts[stage] + stage_place(stage)] = tile
-        for d in range(1, sizes[stage]):
+        size, mine, slots = sizes[stage], stage_place(stage), dot_slots(stage)
+        slot = slots.at[p, lax.rem(mine - d + size, size)]
+        return remote(slot, slot, ds_.at[p, stage, d], dr.at[p, stage, d], tm, lon)
+
+    def dot_send(p, stage, line):
+        dot_slots(stage)[p, stage_place(stage)] = line
+
+        @pl.loop(1, sizes[stage])
+        def _(d):
             dot_copy(p, stage, d).start()
 
     def dot_take(p, stage):
-        for d in range(1, sizes[stage]):
+        @pl.loop(1, sizes[stage])
+        def _(d):
             dot_recv(p, stage, d).wait_recv()
-        total = dots[p, starts[stage]]
+
+        total = dot_slots(stage)[p, 0]
         for i in range(1, sizes[stage]):
-            total = total + dots[p, starts[stage] + i]
+            total = total + dot_slots(stage)[p, i]
         return total
 
     def dot_done(p):
-        for stage in range(3):
-            for d in range(1, sizes[stage]):
+        for stage in range(2):
+
+            @pl.loop(1, sizes[stage])
+            def _(d):
                 dot_copy(p, stage, d).wait_send()
 
-    row8 = lax.broadcasted_iota(jnp.int32, (8, rows), 0)
+    low = lane[:1] < MW
 
     def pack(slope, curve):
-        return jnp.where(row8 == 0, slope, jnp.where(row8 == 1, curve, 0.0))
-
-    def ratio(tile):
-        return jnp.sum(tile[0:1], axis=1, keepdims=True) / jnp.sum(tile[1:2], axis=1, keepdims=True)
-
-    transform_start(0)
-    halo_send(1, G)
-    transform_cross(0)
-    transform_spread(0)
-    transform_finish(0)
-    halo_wait(1, G)
-    filtered(0, G, V0)
+        return jnp.where(low, slope + pltpu.roll(slope, MW, axis=1), curve + pltpu.roll(curve, MW, axis=1))
+
+    def ratio(line):
+        slope = jnp.sum(jnp.where(low, line, 0.0), axis=1, keepdims=True)
+        return slope / jnp.sum(jnp.where(low, 0.0, line), axis=1, keepdims=True)
+
+    with jax.named_scope("transform zero"):
+        transform_start(0)
+    with jax.named_scope("edges one send"):
+        edge_send(1, G)
+    with jax.named_scope("cross zero"):
+        transform_cross(0)
+    with jax.named_scope("rim one send"):
+        rim_send(1, G)
+    with jax.named_scope("halo one send"):
+        halo_send(1, G)
+    with jax.named_scope("spread zero"):
+        transform_spread(0)
+    with jax.named_scope("rim one wait"):
+        rim_take(1, G)
+    with jax.named_scope("halo one wait"):
+        halo_wait(1, G)
+    with jax.named_scope("finish zero"):
+        transform_finish(0)
+    with jax.named_scope("filter zero"):
+        filtered(0, G, V0)
     acc = [jnp.zeros((1, rows), F32), jnp.zeros((1, rows), F32)]
 
     def emit_u(s, n, u):
@@ -361,19 +430,34 @@
         acc[0] = acc[0] + jnp.sum(G[2, r] * v, axis=0, keepdims=True)
         acc[1] = acc[1] + jnp.sum(v * u, axis=0, keepdims=True)
 
-    operator(V0, emit_u)
-
-    transform_start(1)
-    dot_send(0, 0, pack(*acc))
-    halo_send(2, U)
-    transform_cross(1)
-    dot_send(0, 1, dot_take(0, 0))
-    dot_send(0, 2, dot_take(0, 1))
-    transform_spread(1)
-    step0 = ratio(dot_take(0, 2))
-    transform_finish(1)
-    halo_wait(2, U)
-    filtered(1, U, V)
+    with jax.named_scope("operator one"):
+        operator(V0, emit_u)
+
+    with jax.named_scope("transform one"):
+        transform_start(1)
+    with jax.named_scope("edges two send"):
+        dot_send(0, 0, pack(*acc))
+        edge_send(2, U)
+    with jax.named_scope("cross one"):
+        transform_cross(1)
+    with jax.named_scope("rim two send"):
+        rim_send(2, U)
+    with jax.named_scope("halo two send"):
+        halo_send(2, U)
+    with jax.named_scope("sums zero"):
+        dot_send(0, 1, dot_take(0, 0))
+    with jax.named_scope("spread one"):
+        transform_spread(1)
+    with jax.named_scope("rim two wait"):
+        rim_take(2, U)
+    with jax.named_scope("step zero"):
+        step0 = ratio(dot_take(0, 1))
+    with jax.named_scope("halo two wait"):
+        halo_wait(2, U)
+    with jax.named_scope("finish one"):
+        transform_finish(1)
+    with jax.named_scope("filter one"):
+        filtered(1, U, V)
     acc[0] = acc[1] = jnp.zeros((1, rows), F32)
 
     def emit_last(s, n, u1):
@@ -390,24 +474,28 @@
         res_g[l] = gradient
         res_a[l] = E[2, r] - step0 * v0
 
-    operator(V, emit_last)
-    dot_send(1, 0, pack(*acc))
-    dot_send(1, 1, dot_take(1, 0))
-    dot_send(1, 2, dot_take(1, 1))
-    step1 = ratio(dot_take(1, 2))
-    res_a[...] = res_a[...] - step1 * V[own]
-    res_g[...] = res_g[...] - step1 * obs[...]
+    with jax.named_scope("operator two"):
+        operator(V, emit_last)
+    with jax.named_scope("sums one a"):
+        dot_send(1, 0, pack(*acc))
+    with jax.named_scope("sums one b"):
+        dot_send(1, 1, dot_take(1, 0))
+    with jax.named_scope("sums one c"):
+        step1 = ratio(dot_take(1, 1))
+    with jax.named_scope("update"):
+        res_a[...] = res_a[...] - step1 * V[own]
+        res_g[...] = res_g[...] - step1 * obs[...]
     ca = pltpu.make_async_copy(res_a, out_a.at[0], lsem.at[0])
     cg = pltpu.make_async_copy(res_g, out_g.at[0], lsem.at[1])
     ca.start()
     cg.start()
-    for p, X in enumerate((E, G, U)):
-        halo_done(p, X)
-    for c in edge_b:
-        c.wait_send()
-    for p in range(2):
-        transform_done(p)
-        dot_done(p)
+    with jax.named_scope("drain"):
+        for p, X in enumerate((E, G, U)):
+            halo_done(p, X)
+            edge_done(p)
+        for p in range(2):
+            transform_done(p)
+            dot_done(p)
     ca.wait()
     cg.wait()
 
@@ -420,7 +508,7 @@
     flat = pltpu.VMEM((N, rows), F32)
     whole = pltpu.VMEM((N, rows), jnp.int32)
     dma = pltpu.SemaphoreType.DMA
-    hbm = pl.BlockSpec(memory_space=pl.ANY)
+    hbm = pl.BlockSpec(memory_space=pltpu.HBM)
     return pl.pallas_call(
         functools.partial(kernel, NT, N),
         out_shape=[jax.ShapeDtypeStruct(first.shape, F32)] * 2,
@@ -437,14 +525,20 @@
             pltpu.VMEM((2, 2, 16, rows), F32),
             pltpu.VMEM((2, 16, rows), F32),
             pltpu.VMEM((2, 5, MW, rows), F32),
-            pltpu.VMEM((2, 28, 8, rows), F32),
+            pltpu.VMEM((2, 32, 1, rows), F32),
+            pltpu.VMEM((2, 16, 1, rows), F32),
+            pltpu.VMEM((3, 2, rows), F32),
+            pltpu.VMEM((3, 2, 2, rows), F32),
+            pltpu.VMEM((3, 2, 4, rows), F32),
+            pltpu.VMEM((3, 2, 4, rows), F32),
             flat, flat,
-            dma((7,)), dma((3, 10)), dma((3, 10)), dma((2,)), dma((2,)),
+            pltpu.SemaphoreType.REGULAR, dma((7,)), dma((3, 4)), dma((3, 4)),
+            dma((3, 2)), dma((3, 2)), dma((3, 2)), dma((3, 2)),
             dma((2, 4)), dma((2, 4)), dma((2,)), dma((2,)), dma((2, 19)), dma((2, 19)),
-            dma((2, 28)), dma((2, 28)),
+            dma((2, 2, 32)), dma((2, 2, 32)),
         ],
         compiler_params=pltpu.CompilerParams(
-            collective_id=0, has_side_effects=True, vmem_limit_bytes=40 * 1024 * 1024
+            collective_id=0, has_side_effects=True, vmem_limit_bytes=56 * 1024 * 1024
         ),
     )(first, obs, track, land, bw, forward, inverse, row)
 

time: 105 us -> 83.2 us (0.79)
  Pallas kernels: 94.3 us -> 79.1 us
  local copies, waits for them, and re-layouts: 9.44 us -> 3.22 us
    pallas_call x1, Pallas kernels: 94.3 us -> 79.1 us  [on_device(): pl.pallas_call(functools.partial(kernel, NT, N), out_shape=[jax.ShapeDtyp...]
    unnamed x18 -> x2, local copies, waits for them, and re-layouts: 9.44 us -> 3.22 us
where the time goes in v2:
time: 83.2 us; the launch traced here: 83 us
  Pallas kernels  79.1 us (95%)
  local copies, waits for them, and re-layouts  3.22 us (4%)
    pallas_call x1, Pallas kernels, on_device(): pl.pallas_call(functools.partial(kernel, NT, N), out_shape=[jax.ShapeDtyp...  79.1 us
    unnamed x2, local copies, waits for them, and re-layouts  3.22 us

profile of v2, /device:TPU:1, one launch (start us, length us, event | category | flops | bytes accessed | tf_op | source)
XLA Modules:
  0.0 83.0 jit_solution(10845491922724314895)
XLA Ops:
  0.6 79.1 %shard_map.95 = (f32[1,360,128]{2,1,0:T(8,128)}, f32[1,360,128]{2,1,0:T(8,128)}) custom-call(f32[1,360,128]{2,1,0:T(8,128)} %first_ref.1, f32[1,360,128]{2,1,0:T(8,128)} %obs_ref.1, s32[1,360,128]{2,1,0:T(8,128)} %track_ref.1, s32[360,128]{1,0:T(8,128)} %land_ref.1, f32[360,128]{1,0:T(8,128)} %bw_ref.1, f32[8,128,384]{2,1,0:T(8,128)} %constant.6.clone.fwd_ref, ...), custom_call_target="tpu_custom_call" | custom-call | tf_op jit(solution)/shard_map/pallas_call | solution.py:512
  79.8 1.6 %copy.12 = f32[1,360,128]{2,1,0:T(8,128)} copy(f32[1,360,128]{2,1,0:T(8,128)} %get-tuple-element.4) | data formatting | bytes 368640
  81.4 1.6 %copy.13 = f32[1,360,128]{2,1,0:T(8,128)} copy(f32[1,360,128]{2,1,0:T(8,128)} %get-tuple-element.5) | data formatting | bytes 368640

commit v3 on v2

--- a/solution.py
+++ b/solution.py
@@ -42,10 +42,10 @@
 
 
 def kernel(
-    NT, N, first_ref, obs_ref, track_ref, land_ref, bw_ref, fwd_ref, inv_ref, row_ref,
-    out_a, out_g,
-    E, G, U, B, W, obs, track, land, fwd, inv, V, TV, T2V, Y, V0, padded, amp, rs_buf, quarter,
-    z_buf, AT, dots_a, dots_b, ts, tr, ls, lr, res_a, res_g,
+    NT, N, first_ref, obs_ref, track_ref, land_ref, bw_ref, fwd_ref, inv_ref, row_hbm,
+    out_a, out_s, out_g, out_c, out_step,
+    row_ref, E, G, U, B, W, obs, track, land, fwd, inv, V, TV, T2V, Y, V0, padded, amp, rs_buf, quarter,
+    z_buf, AT, dots_a, dots_b, ts, tr, ls, lr,
     hello, lsem, hs, hr, es, er, rs_, rr, xs, xr, zs, zr, ats, atr, ds_, dr,
 ):
     tm = lax.axis_index("tm")
@@ -75,8 +75,10 @@
         pltpu.make_async_copy(land_ref, land, lsem.at[4]),
         pltpu.make_async_copy(fwd_ref.at[lon], fwd, lsem.at[5]),
         pltpu.make_async_copy(inv_ref.at[lon], inv, lsem.at[6]),
+        pltpu.make_async_copy(row_hbm, row_ref, lsem.at[7]),
     ]
     loads[0].start()
+    loads[7].start()
 
     barrier = pltpu.get_barrier_semaphore()
 
@@ -102,7 +104,7 @@
     for dt in (-2, -1, 1, 2):
         when_t(dt, lambda dt=dt: greet(tm + dt, lon))
         count = count + jnp.where(inside(tm + dt), 1, 0)
-    for c in loads[1:]:
+    for c in loads[1:7]:
         c.start()
 
     for dt in (-2, -1, 1, 2):
@@ -130,23 +132,38 @@
             device_id={"tm": t, "lon": l}, device_id_type=MESH,
         )
 
-    shifts = (1, -1, 2, -2)
-
-    def halo_copy(p, X, i):
-        dt = shifts[i]
+    side = 1 - 2 * lax.rem(tm, 2)
+    send_days = (-side, 2 * side, side)
+    recv_days = (-side, -2 * side, side, 2 * side)
+
+    def plane_copy(p, X, i):
+        dt = send_days[i]
         return remote(X.at[2, own], X.at[2 - dt, own], hs.at[p, i], hr.at[p, i], tm + dt, lon)
 
+    def hand_copy(p, X):
+        return remote(X.at[2 - side, own], X.at[2 - 2 * side, own], hs.at[p, 3], hr.at[p, 3], tm + side, lon)
+
+    def plane_recv(p, X, i):
+        return remote(X.at[2, own], X.at[2 + recv_days[i], own], hs.at[p, i], hr.at[p, i], tm, lon)
+
     def halo_send(p, X):
-        for i, dt in enumerate(shifts):
-            when_t(dt, lambda i=i: halo_copy(p, X, i).start())
+        for i in range(3):
+            pl.when(inside(tm + send_days[i]))(lambda i=i: plane_copy(p, X, i).start())
+
+    def halo_hand(p, X):
+        @pl.when(inside(tm - side))
+        def _():
+            plane_recv(p, X, 0).wait_recv()
+            hand_copy(p, X).start()
 
     def halo_wait(p, X):
-        for i, dt in enumerate(shifts):
-            when_t(-dt, lambda i=i: halo_copy(p, X, i).wait_recv())
+        for i in (1, 2, 3):
+            pl.when(inside(tm + recv_days[i]))(lambda i=i: plane_recv(p, X, i).wait_recv())
 
     def halo_done(p, X):
-        for i, dt in enumerate(shifts):
-            when_t(dt, lambda i=i: halo_copy(p, X, i).wait_send())
+        for i in range(3):
+            pl.when(inside(tm + send_days[i]))(lambda i=i: plane_copy(p, X, i).wait_send())
+        pl.when(inside(tm - side))(lambda: hand_copy(p, X).wait_send())
 
     first_row, last_row = OFF, OFF + N - 1
 
@@ -202,9 +219,12 @@
         pl.semaphore_wait(hello, len(fours))
     with jax.named_scope("guess rim"):
         rim_send(0, E)
+    with jax.named_scope("guess hand on"):
+        halo_hand(0, E)
 
     lane = lax.broadcasted_iota(jnp.int32, (8, rows), 1)
     first_lane, last_lane = lane[:1] == 0, lane[:1] == rows - 1
+    loads[7].wait()
     bend = row_ref[0:1]
     centre = row_ref[1:2]
     shrink = row_ref[2:3]
@@ -257,46 +277,44 @@
 
     with jax.named_scope("first operator"):
         operator(E.at[2], emit_g)
-    for c in loads[5:]:
+    for c in loads[5:7]:
         c.wait()
 
     half = lax.broadcasted_iota(jnp.int32, (MW, rows), 1) < MW
 
     def rs_copy(p, d):
         q = lax.rem(x + d, 4)
-        return remote(
-            amp.at[p, pl.ds(16 * q, 16)], rs_buf.at[p, d], xs.at[p, d], xr.at[p, d], tm, q * 2 + zh
-        )
+        return remote(amp.at[p, pl.ds(16 * q, 16)], rs_buf.at[p, d], xs.at[p], xr.at[p], tm, q * 2 + zh)
+
+    def rs_all(p):
+        return remote(rs_buf.at[p, pl.ds(1, 3)], rs_buf.at[p, pl.ds(1, 3)], xs.at[p], xr.at[p], tm, lon)
 
     def z_copy(p):
         return remote(quarter.at[p, 0], z_buf.at[p], zs.at[p], zr.at[p], tm, lon + 1 - 2 * zh)
 
-    at_kinds = [(dt, d) for dt in (0, 1, -1, 2, -2) for d in range(4) if (dt, d) != (0, 0)]
-
-    def at_copy(p, i):
-        dt, d = at_kinds[i]
+    days = (2, -2, 1, -1, 0)
+
+    def at_copy(p, i, d):
+        dt = days[i]
         xx = lax.rem(x + d, 4)
         return remote(
             quarter.at[p, 1], AT.at[p, 2 - dt, pl.ds(16 * x, 16)], ats.at[p, i], atr.at[p, i], tm + dt, xx * 2 + zh
         )
 
-    def at_recv(p, i):
-        dt, d = at_kinds[i]
-        xx = lax.rem(x - d + 4, 4)
-        return remote(
-            quarter.at[p, 1], AT.at[p, 2 - dt, pl.ds(16 * xx, 16)], ats.at[p, i], atr.at[p, i], tm, lon
-        )
+    def at_all(p, i):
+        some = AT.at[p, 2 - days[i], pl.ds(0, MW if days[i] else MW - 16)]
+        return remote(some, some, ats.at[p, i], atr.at[p, i], tm, lon)
 
     def transform_start(p):
         part = lax.dot(fwd[...], padded[...], precision=lax.Precision.HIGHEST, preferred_element_type=F32)
         amp[p] = jnp.where(half, pltpu.roll(part[:MW], MW, axis=1), part[MW:])
-        for d in (1, 2, 3):
+        for d in (2, 1, 3):
             rs_copy(p, d).start()
 
     def transform_cross(p):
         total = amp[p, pl.ds(16 * x, 16)]
+        rs_all(p).wait_recv()
         for d in (1, 2, 3):
-            rs_copy(p, d).wait_recv()
             total = total + rs_buf[p, d]
         quarter[p, 0] = total
         z_copy(p).start()
@@ -305,20 +323,20 @@
         z_copy(p).wait_recv()
         total = quarter[p, 0] + z_buf[p]
         quarter[p, 1] = total
-        for i, (dt, _) in enumerate(at_kinds):
-            when_t(dt, lambda i=i: at_copy(p, i).start())
+        for i, dt in enumerate(days):
+            for d in (2, 1, 3, 0) if dt else (2, 1, 3):
+                when_t(dt, lambda i=i, d=d: at_copy(p, i, d).start())
         AT[p, 2, pl.ds(16 * x, 16)] = total
 
     def transform_finish(p):
-        for i, (dt, _) in enumerate(at_kinds):
-            when_t(-dt, lambda i=i: at_recv(p, i).wait_recv())
+        for i, dt in enumerate(days):
+            when_t(-dt, lambda i=i: at_all(p, i).wait_recv())
 
     def transform_done(p):
-        for d in (1, 2, 3):
-            rs_copy(p, d).wait_send()
+        rs_all(p).wait_send()
         z_copy(p).wait_send()
-        for i, (dt, _) in enumerate(at_kinds):
-            when_t(dt, lambda i=i: at_copy(p, i).wait_send())
+        for i, dt in enumerate(days):
+            when_t(dt, lambda i=i: at_all(p, i).wait_send())
 
     def stack(a):
         c = jnp.where(half, 0.0, pltpu.roll(a, MW, axis=1))
@@ -357,27 +375,30 @@
 
     def dot_copy(p, stage, d):
         size, mine, slots = sizes[stage], stage_place(stage), dot_slots(stage)
-        t, l = stage_device(stage, lax.rem(mine + d, size))
+        if stage == 0:
+            other = lax.rem(x + d // 8, 4) * 8 + lax.rem(k + d % 8, 8)
+        else:
+            other = lax.rem(mine + d, size)
+        t, l = stage_device(stage, other)
         slot = slots.at[p, mine]
-        return remote(slot, slot, ds_.at[p, stage, d], dr.at[p, stage, d], t, l)
-
-    def dot_recv(p, stage, d):
-        size, mine, slots = sizes[stage], stage_place(stage), dot_slots(stage)
-        slot = slots.at[p, lax.rem(mine - d + size, size)]
-        return remote(slot, slot, ds_.at[p, stage, d], dr.at[p, stage, d], tm, lon)
+        return remote(slot, slot, ds_.at[p, stage], dr.at[p, stage], t, l)
+
+    def dot_all(p, stage):
+        some = dot_slots(stage).at[p, pl.ds(0, sizes[stage] - 1)]
+        return remote(some, some, ds_.at[p, stage], dr.at[p, stage], tm, lon)
+
+    steps = (
+        [8 * dx + dk for dx in (2, 1, 3, 0) for dk in (4, 3, 5, 2, 6, 1, 7, 0)][:-1],
+        [8, 7, 9, 6, 10, 5, 11, 4, 12, 3, 13, 2, 14, 1, 15],
+    )
 
     def dot_send(p, stage, line):
         dot_slots(stage)[p, stage_place(stage)] = line
-
-        @pl.loop(1, sizes[stage])
-        def _(d):
+        for d in steps[stage]:
             dot_copy(p, stage, d).start()
 
     def dot_take(p, stage):
-        @pl.loop(1, sizes[stage])
-        def _(d):
-            dot_recv(p, stage, d).wait_recv()
-
+        dot_all(p, stage).wait_recv()
         total = dot_slots(stage)[p, 0]
         for i in range(1, sizes[stage]):
             total = total + dot_slots(stage)[p, i]
@@ -385,10 +406,7 @@
 
     def dot_done(p):
         for stage in range(2):
-
-            @pl.loop(1, sizes[stage])
-            def _(d):
-                dot_copy(p, stage, d).wait_send()
+            dot_all(p, stage).wait_send()
 
     low = lane[:1] < MW
 
@@ -411,6 +429,8 @@
         halo_send(1, G)
     with jax.named_scope("spread zero"):
         transform_spread(0)
+    with jax.named_scope("hand on one"):
+        halo_hand(1, G)
     with jax.named_scope("rim one wait"):
         rim_take(1, G)
     with jax.named_scope("halo one wait"):
@@ -448,6 +468,8 @@
         dot_send(0, 1, dot_take(0, 0))
     with jax.named_scope("spread one"):
         transform_spread(1)
+    with jax.named_scope("hand on two"):
+        halo_hand(2, U)
     with jax.named_scope("rim two wait"):
         rim_take(2, U)
     with jax.named_scope("step zero"):
@@ -466,13 +488,13 @@
         u1 = W[l] * v1 + u1
         search = v0 - step0 * v1
         curved = u0 - step0 * u1
+        out_c[0, l] = curved
+        out_s[0, l] = search
         gradient = G[2, r] - step0 * u0
         acc[0] = acc[0] + jnp.sum(gradient * search, axis=0, keepdims=True)
         acc[1] = acc[1] + jnp.sum(search * curved, axis=0, keepdims=True)
-        V[r] = search
-        obs[l] = curved
-        res_g[l] = gradient
-        res_a[l] = E[2, r] - step0 * v0
+        out_g[0, l] = gradient
+        out_a[0, l] = E[2, r] - step0 * v0
 
     with jax.named_scope("operator two"):
         operator(V, emit_last)
@@ -480,24 +502,16 @@
         dot_send(1, 0, pack(*acc))
     with jax.named_scope("sums one b"):
         dot_send(1, 1, dot_take(1, 0))
+    for p, X in enumerate((E, G, U)):
+        halo_done(p, X)
+        edge_done(p)
+    for p in range(2):
+        transform_done(p)
+    dot_done(0)
     with jax.named_scope("sums one c"):
-        step1 = ratio(dot_take(1, 1))
-    with jax.named_scope("update"):
-        res_a[...] = res_a[...] - step1 * V[own]
-        res_g[...] = res_g[...] - step1 * obs[...]
-    ca = pltpu.make_async_copy(res_a, out_a.at[0], lsem.at[0])
-    cg = pltpu.make_async_copy(res_g, out_g.at[0], lsem.at[1])
-    ca.start()
-    cg.start()
+        out_step[...] = jnp.broadcast_to(ratio(dot_take(1, 1)), out_step.shape)
     with jax.named_scope("drain"):
-        for p, X in enumerate((E, G, U)):
-            halo_done(p, X)
-            edge_done(p)
-        for p in range(2):
-            transform_done(p)
-            dot_done(p)
-    ca.wait()
-    cg.wait()
+        dot_done(1)
 
 
 def on_device(NT, NL, first, obs, track, land, bw):
@@ -509,13 +523,13 @@
     whole = pltpu.VMEM((N, rows), jnp.int32)
     dma = pltpu.SemaphoreType.DMA
     hbm = pl.BlockSpec(memory_space=pltpu.HBM)
-    return pl.pallas_call(
+    surface, search, gradient, curved, step = pl.pallas_call(
         functools.partial(kernel, NT, N),
-        out_shape=[jax.ShapeDtypeStruct(first.shape, F32)] * 2,
-        in_specs=[hbm] * 7 + [pl.BlockSpec(memory_space=pltpu.VMEM)],
-        out_specs=[hbm] * 2,
+        out_shape=[pltpu.VMEM(first.shape, F32)] * 4 + [pltpu.VMEM((1, rows), F32)],
+        in_specs=[hbm] * 8,
+        out_specs=[pl.BlockSpec(memory_space=pltpu.VMEM)] * 5,
         scratch_shapes=[
-            planes, planes, planes,
+            pltpu.VMEM(row.shape, F32), planes, planes, planes,
             plane, flat, flat, whole, whole,
             pltpu.VMEM(forward.shape[1:], F32), pltpu.VMEM(inverse.shape[1:], F32),
             plane, plane, plane, plane, plane,
@@ -531,16 +545,16 @@
             pltpu.VMEM((3, 2, 2, rows), F32),
             pltpu.VMEM((3, 2, 4, rows), F32),
             pltpu.VMEM((3, 2, 4, rows), F32),
-            flat, flat,
-            pltpu.SemaphoreType.REGULAR, dma((7,)), dma((3, 4)), dma((3, 4)),
+            pltpu.SemaphoreType.REGULAR, dma((8,)), dma((3, 4)), dma((3, 4)),
             dma((3, 2)), dma((3, 2)), dma((3, 2)), dma((3, 2)),
-            dma((2, 4)), dma((2, 4)), dma((2,)), dma((2,)), dma((2, 19)), dma((2, 19)),
-            dma((2, 2, 32)), dma((2, 2, 32)),
+            dma((2,)), dma((2,)), dma((2,)), dma((2,)), dma((2, 5)), dma((2, 5)),
+            dma((2, 2)), dma((2, 2)),
         ],
         compiler_params=pltpu.CompilerParams(
             collective_id=0, has_side_effects=True, vmem_limit_bytes=56 * 1024 * 1024
         ),
     )(first, obs, track, land, bw, forward, inverse, row)
+    return surface - step[None] * search, gradient - step[None] * curved
 
 
 def solution(mesh):

time: 83.2 us -> 75.2 us (0.904)
  Pallas kernels: 79.1 us -> 73.6 us
  local copies, waits for them, and re-layouts: 3.22 us -> 0 us
    pallas_call x1, Pallas kernels: 79.1 us -> 73.6 us  [on_device(): pl.pallas_call(functools.partial(kernel, NT, N), out_shape=[pltpu.VMEM(fi...]
    unnamed x2 -> x0, local copies, waits for them, and re-layouts: 3.22 us -> none
where the time goes in v3:
time: 75.2 us; the launch traced here: 75.1 us
  Pallas kernels  73.6 us (98%)
  other arithmetic  0.79 us (1%)
    pallas_call x1, Pallas kernels, on_device(): pl.pallas_call(functools.partial(kernel, NT, N), out_shape=[pltpu.VMEM(fi...  73.6 us

profile of v3, /device:TPU:1, one launch (start us, length us, event | category | flops | bytes accessed | tf_op | source)
XLA Modules:
  0.0 75.1 jit_solution(4811465502097571652)
XLA Ops:
  0.6 73.6 %shard_map.95 = (f32[1,360,128]{2,1,0:T(8,128)S(1)}, f32[1,360,128]{2,1,0:T(8,128)S(1)}, f32[1,360,128]{2,1,0:T(8,128)S(1)}, f32[1,360,128]{2,1,0:T(8,128)S(1)}, f32[1,128]{1,0:T(1,128)S(1)}) custom-call(f32[1,360,128]{2,1,0:T(8,128)} %first_ref.1, f32[1,360,128]{2,1,0:T(8,128)} %obs_ref.1, s32[1,360,128]{2,1,0:T(8,128)} %track_ref.1, s32[360,128]{1,0:T(8,128)} %land_ref.1, ...), custom_call_target="tpu_custom_call" | custom-call | tf_op jit(solution)/shard_map/pallas_call | solution.py:526
  74.3 0.8 %multiply_subtract_fusion = (f32[1,360,128]{2,1,0:T(8,128)}, f32[1,360,128]{2,1,0:T(8,128)}) fusion(f32[1,360,128]{2,1,0:T(8,128)S(1)} %get-tuple-element.10, f32[1,360,128]{2,1,0:T(8,128)S(1)} %get-tuple-element.11, f32[128]{0:T(128)S(1)} %bitcast.1, f32[1,360,128]{2,1,0:T(8,128)S(1)} %get-tuple-element.7, f32[1,360,128]{2,1,0:T(8,128)S(1)} %get-tuple-element.9), kind=kLoop, calls=%fused_computation | loop fusion | flops 184320 | bytes 1106432 | tf_op jit(solution)/shard_map/sub | solution.py:557

commit v4 on v3

--- a/solution.py
+++ b/solution.py
@@ -44,7 +44,7 @@
 def kernel(
     NT, N, first_ref, obs_ref, track_ref, land_ref, bw_ref, fwd_ref, inv_ref, row_hbm,
     out_a, out_s, out_g, out_c, out_step,
-    row_ref, E, G, U, B, W, obs, track, land, fwd, inv, V, TV, T2V, Y, V0, padded, amp, rs_buf, quarter,
+    row_ref, E, G, U, B, W, obs, track, land, fwd, inv, V, TV, T2V, Y, V0, LV0, padded, amp, rs_buf, quarter,
     z_buf, AT, dots_a, dots_b, ts, tr, ls, lr,
     hello, lsem, hs, hr, es, er, rs_, rr, xs, xr, zs, zr, ats, atr, ds_, dr,
 ):
@@ -237,8 +237,8 @@
         hi = jnp.where(last_lane, 0.0, pltpu.roll(v, rows - 1, axis=1))
         return bend * (up + down) + (lo + hi) + centre * v
 
-    ext_chunks = [(EXT, 96), (EXT + 96, 96), (EXT + 192, 96), (EXT + 288, N + 16 - 288)]
     own_chunks = [(OFF + c, 72) for c in range(0, N, 72)]
+    ext_chunks = [(EXT, 8)] + own_chunks + [(OFF + N, 8)]
     centre_t2 = jnp.where((tm == 0) | (tm == NT - 1), 5.0, 6.0).astype(F32)
 
     def second(a, b, c):
@@ -247,9 +247,18 @@
     def second2(a, b, c, d, e):
         return a + e - 4.0 * (b + d) + centre_t2 * c
 
-    def operator(field, emit):
+    def flatten(field):
         for s, n in ext_chunks:
-            Y[pl.ds(s, n)] = B[pl.ds(s, n)] * (TV[pl.ds(s, n)] + flat(field, s, n))
+            Y[pl.ds(s, n)] = flat(field, s, n)
+
+    def once(emit=None):
+        for s, n in ext_chunks:
+            full = TV[pl.ds(s, n)] + Y[pl.ds(s, n)]
+            Y[pl.ds(s, n)] = B[pl.ds(s, n)] * full
+            if emit is not None and OFF <= s < OFF + N:
+                emit(s, n, full)
+
+    def twice(emit):
         for s, n in own_chunks:
             emit(s, n, B[pl.ds(s, n)] * (T2V[pl.ds(s, n)] + flat(TV, s, n)) + flat(Y, s, n))
 
@@ -276,7 +285,9 @@
         padded[l] = g
 
     with jax.named_scope("first operator"):
-        operator(E.at[2], emit_g)
+        flatten(E.at[2])
+        once()
+        twice(emit_g)
     for c in loads[5:7]:
         c.wait()
 
@@ -306,7 +317,7 @@
         return remote(some, some, ats.at[p, i], atr.at[p, i], tm, lon)
 
     def transform_start(p):
-        part = lax.dot(fwd[...], padded[...], precision=lax.Precision.HIGHEST, preferred_element_type=F32)
+        part = lax.dot(fwd[...], padded[...], precision=lax.Precision.HIGH, preferred_element_type=F32)
         amp[p] = jnp.where(half, pltpu.roll(part[:MW], MW, axis=1), part[MW:])
         for d in (2, 1, 3):
             rs_copy(p, d).start()
@@ -328,9 +339,10 @@
                 when_t(dt, lambda i=i, d=d: at_copy(p, i, d).start())
         AT[p, 2, pl.ds(16 * x, 16)] = total
 
-    def transform_finish(p):
+    def transform_finish(p, some):
         for i, dt in enumerate(days):
-            when_t(-dt, lambda i=i: at_all(p, i).wait_recv())
+            if dt in some:
+                when_t(-dt, lambda i=i: at_all(p, i).wait_recv())
 
     def transform_done(p):
         rs_all(p).wait_send()
@@ -339,26 +351,33 @@
             when_t(dt, lambda i=i: at_all(p, i).wait_send())
 
     def stack(a):
-        c = jnp.where(half, 0.0, pltpu.roll(a, MW, axis=1))
-        s = jnp.where(half, 0.0, a)
-        return jnp.concatenate([c, s], axis=0)
-
-    def filtered(p, X, field):
-        a = [AT[p, i] for i in range(5)]
-        three = jnp.concatenate(
-            [stack(a[2]), stack(second(a[1], a[3], a[2])), stack(second2(*a))], axis=1
+        return jnp.concatenate([pltpu.roll(a, MW, axis=1), a], axis=0) * shrink
+
+    def synthesis(s, n, amplitudes):
+        return lax.dot(
+            inv[pl.ds(s - EXT, n)], amplitudes, precision=lax.Precision.HIGH, preferred_element_type=F32
         )
+
+    def filter_local(X, field):
         for s, n in ext_chunks:
             r = pl.ds(s, n)
-            smooth = lax.dot(
-                inv[pl.ds(s - EXT, n)], three, precision=lax.Precision.HIGHEST, preferred_element_type=F32
-            )
-            field[r] = keep * X[2, r] + shrink * smooth[:, :rows]
-            TV[r] = keep * second(X[1, r], X[3, r], X[2, r]) + shrink * smooth[:, rows:2 * rows]
-            T2V[r] = (
-                keep * second2(X[0, r], X[1, r], X[2, r], X[3, r], X[4, r])
-                + shrink * smooth[:, 2 * rows:]
-            )
+            field[r] = keep * X[2, r]
+            TV[r] = keep * second(X[1, r], X[3, r], X[2, r])
+            T2V[r] = keep * second2(X[0, r], X[1, r], X[2, r], X[3, r], X[4, r])
+
+    def filter_own(p, field):
+        amplitudes = stack(AT[p, 2])
+        for s, n in ext_chunks:
+            field[pl.ds(s, n)] += synthesis(s, n, amplitudes)
+        flatten(field)
+
+    def filter_days(p):
+        a = [AT[p, i] for i in range(5)]
+        amplitudes = jnp.concatenate([stack(second(a[1], a[3], a[2])), stack(second2(*a))], axis=1)
+        for s, n in ext_chunks:
+            smooth = synthesis(s, n, amplitudes)
+            TV[pl.ds(s, n)] += smooth[:, :rows]
+            T2V[pl.ds(s, n)] += smooth[:, rows:]
 
     sizes = (32, 16)
 
@@ -435,11 +454,20 @@
         rim_take(1, G)
     with jax.named_scope("halo one wait"):
         halo_wait(1, G)
+    with jax.named_scope("filter zero local"):
+        filter_local(G, V0)
     with jax.named_scope("finish zero"):
-        transform_finish(0)
-    with jax.named_scope("filter zero"):
-        filtered(0, G, V0)
+        transform_finish(0, (0,))
+    with jax.named_scope("filter zero own"):
+        filter_own(0, V0)
+    with jax.named_scope("finish zero days"):
+        transform_finish(0, (1, -1, 2, -2))
+    with jax.named_scope("filter zero days"):
+        filter_days(0)
     acc = [jnp.zeros((1, rows), F32), jnp.zeros((1, rows), F32)]
+
+    def emit_first(s, n, full):
+        LV0[pl.ds(s - OFF, n)] = full
 
     def emit_u(s, n, u):
         l, r = pl.ds(s - OFF, n), pl.ds(s, n)
@@ -451,7 +479,8 @@
         acc[1] = acc[1] + jnp.sum(v * u, axis=0, keepdims=True)
 
     with jax.named_scope("operator one"):
-        operator(V0, emit_u)
+        once(emit_first)
+        twice(emit_u)
 
     with jax.named_scope("transform one"):
         transform_start(1)
@@ -472,34 +501,44 @@
         halo_hand(2, U)
     with jax.named_scope("rim two wait"):
         rim_take(2, U)
+    with jax.named_scope("halo two wait"):
+        halo_wait(2, U)
+    with jax.named_scope("filter one local"):
+        filter_local(U, V)
+    with jax.named_scope("finish one"):
+        transform_finish(1, (0,))
+    with jax.named_scope("filter one own"):
+        filter_own(1, V)
     with jax.named_scope("step zero"):
         step0 = ratio(dot_take(0, 1))
-    with jax.named_scope("halo two wait"):
-        halo_wait(2, U)
-    with jax.named_scope("finish one"):
-        transform_finish(1)
-    with jax.named_scope("filter one"):
-        filtered(1, U, V)
+    with jax.named_scope("finish one days"):
+        transform_finish(1, (1, -1, 2, -2))
+    with jax.named_scope("filter one days"):
+        filter_days(1)
     acc[0] = acc[1] = jnp.zeros((1, rows), F32)
+
+    def emit_sums(s, n, full):
+        l, r = pl.ds(s - OFF, n), pl.ds(s, n)
+        search = V0[r] - step0 * V[r]
+        gradient = G[2, r] - step0 * U[2, r]
+        bent = LV0[l] - step0 * full
+        acc[0] = acc[0] + jnp.sum(gradient * search, axis=0, keepdims=True)
+        acc[1] = acc[1] + jnp.sum(W[l] * (search * search) + B[r] * (bent * bent), axis=0, keepdims=True)
+        out_s[0, l] = search
+        out_g[0, l] = gradient
+
+    with jax.named_scope("operator two once"):
+        once(emit_sums)
+    with jax.named_scope("sums one a"):
+        dot_send(1, 0, pack(*acc))
 
     def emit_last(s, n, u1):
         l, r = pl.ds(s - OFF, n), pl.ds(s, n)
-        v1, v0, u0 = V[r], V0[r], U[2, r]
-        u1 = W[l] * v1 + u1
-        search = v0 - step0 * v1
-        curved = u0 - step0 * u1
-        out_c[0, l] = curved
-        out_s[0, l] = search
-        gradient = G[2, r] - step0 * u0
-        acc[0] = acc[0] + jnp.sum(gradient * search, axis=0, keepdims=True)
-        acc[1] = acc[1] + jnp.sum(search * curved, axis=0, keepdims=True)
-        out_g[0, l] = gradient
-        out_a[0, l] = E[2, r] - step0 * v0
-
-    with jax.named_scope("operator two"):
-        operator(V, emit_last)
-    with jax.named_scope("sums one a"):
-        dot_send(1, 0, pack(*acc))
+        out_c[0, l] = U[2, r] - step0 * (W[l] * V[r] + u1)
+        out_a[0, l] = E[2, r] - step0 * V0[r]
+
+    with jax.named_scope("operator two twice"):
+        twice(emit_last)
     with jax.named_scope("sums one b"):
         dot_send(1, 1, dot_take(1, 0))
     for p, X in enumerate((E, G, U)):
@@ -532,7 +571,7 @@
             pltpu.VMEM(row.shape, F32), planes, planes, planes,
             plane, flat, flat, whole, whole,
             pltpu.VMEM(forward.shape[1:], F32), pltpu.VMEM(inverse.shape[1:], F32),
-            plane, plane, plane, plane, plane,
+            plane, plane, plane, plane, plane, flat,
             pltpu.VMEM((forward.shape[2], rows), F32),
             pltpu.VMEM((2, MW, rows), F32),
             pltpu.VMEM((2, 4, 16, rows), F32),

time: 75.2 us -> 74.2 us (0.987)
  Pallas kernels: 73.6 us -> 72.6 us
    pallas_call x1, Pallas kernels: 73.6 us -> 72.6 us  [on_device(): pl.pallas_call(functools.partial(kernel, NT, N), out_shape=[pltpu.VMEM(fi...]
where the time goes in v4:
time: 74.2 us; the launch traced here: 74 us
  Pallas kernels  72.6 us (98%)
  other arithmetic  0.79 us (1%)
    pallas_call x1, Pallas kernels, on_device(): pl.pallas_call(functools.partial(kernel, NT, N), out_shape=[pltpu.VMEM(fi...  72.6 us

profile of v4, /device:TPU:1, one launch (start us, length us, event | category | flops | bytes accessed | tf_op | source)
XLA Modules:
  0.0 74.0 jit_solution(16857538593660331432)
XLA Ops:
  0.6 72.6 %shard_map.95 = (f32[1,360,128]{2,1,0:T(8,128)S(1)}, f32[1,360,128]{2,1,0:T(8,128)S(1)}, f32[1,360,128]{2,1,0:T(8,128)S(1)}, f32[1,360,128]{2,1,0:T(8,128)S(1)}, f32[1,128]{1,0:T(1,128)S(1)}) custom-call(f32[1,360,128]{2,1,0:T(8,128)} %first_ref.1, f32[1,360,128]{2,1,0:T(8,128)} %obs_ref.1, s32[1,360,128]{2,1,0:T(8,128)} %track_ref.1, s32[360,128]{1,0:T(8,128)} %land_ref.1, ...), custom_call_target="tpu_custom_call" | custom-call | tf_op jit(solution)/shard_map/pallas_call | solution.py:565
  73.2 0.8 %multiply_subtract_fusion = (f32[1,360,128]{2,1,0:T(8,128)}, f32[1,360,128]{2,1,0:T(8,128)}) fusion(f32[1,360,128]{2,1,0:T(8,128)S(1)} %get-tuple-element.10, f32[1,360,128]{2,1,0:T(8,128)S(1)} %get-tuple-element.11, f32[128]{0:T(128)S(1)} %bitcast.1, f32[1,360,128]{2,1,0:T(8,128)S(1)} %get-tuple-element.7, f32[1,360,128]{2,1,0:T(8,128)S(1)} %get-tuple-element.9), kind=kLoop, calls=%fused_computation | loop fusion | flops 184320 | bytes 1106432 | tf_op jit(solution)/shard_map/sub | solution.py:596

commit v5 on v4

--- a/solution.py
+++ b/solution.py
@@ -38,15 +38,22 @@
     row[1] = -2.0 * (bend + 1.0)
     row[2] = shrink
     row[3] = 1.0 - shrink
-    return forward, inverse, row
+    seams = np.zeros((4, 32, 128), np.float32)
+    for i, offset in enumerate((0, 1, -1, -2)):
+        place = (np.arange(segments) + 1) * length + offset
+        a = 2 * np.pi * (place[None, :] * harmonic[:, None] % circle) / circle
+        for q in range(4):
+            seams[q, :16, 8 * i:8 * i + 8] = np.cos(a[16 * q:16 * q + 16])
+            seams[q, 16:, 8 * i:8 * i + 8] = np.sin(a[16 * q:16 * q + 16])
+    return forward, inverse, row, seams
 
 
 def kernel(
-    NT, N, first_ref, obs_ref, track_ref, land_ref, bw_ref, fwd_ref, inv_ref, row_hbm,
+    NT, N, first_ref, obs_ref, track_ref, land_ref, bw_ref, fwd_ref, inv_ref, row_hbm, seams_hbm,
     out_a, out_s, out_g, out_c, out_step,
-    row_ref, E, G, U, B, W, obs, track, land, fwd, inv, V, TV, T2V, Y, V0, LV0, padded, amp, rs_buf, quarter,
+    row_ref, E, G, U, B, W, obs, track, land, fwd, inv, V, TV, T2V, Y, V0, LV0, padded, seams, seam_rows, seam_amp, ED, amp, rs_buf, quarter,
     z_buf, AT, dots_a, dots_b, ts, tr, ls, lr,
-    hello, lsem, hs, hr, es, er, rs_, rr, xs, xr, zs, zr, ats, atr, ds_, dr,
+    hello, hello2, sems, lsem, hs, hr, es, er, rs_, rr, xs, xr, zs, zr, ats, atr, ds_, dr,
 ):
     tm = lax.axis_index("tm")
     lon = lax.axis_index("lon")
@@ -76,6 +83,7 @@
         pltpu.make_async_copy(fwd_ref.at[lon], fwd, lsem.at[5]),
         pltpu.make_async_copy(inv_ref.at[lon], inv, lsem.at[6]),
         pltpu.make_async_copy(row_hbm, row_ref, lsem.at[7]),
+        pltpu.make_async_copy(seams_hbm.at[x], seams, lsem.at[8]),
     ]
     loads[0].start()
     loads[7].start()
@@ -104,7 +112,7 @@
     for dt in (-2, -1, 1, 2):
         when_t(dt, lambda dt=dt: greet(tm + dt, lon))
         count = count + jnp.where(inside(tm + dt), 1, 0)
-    for c in loads[1:7]:
+    for c in loads[1:7] + loads[8:]:
         c.start()
 
     for dt in (-2, -1, 1, 2):
@@ -116,9 +124,9 @@
             for p in range(2):
                 AT[p, 2 + dt] = jnp.zeros(AT.shape[2:], F32)
             if abs(dt) == 1:
-                for p in range(3):
-                    tr[p, (dt + 1) // 2] = jnp.zeros(tr.shape[2:], F32)
-
+                tr[(dt + 1) // 2] = jnp.zeros(tr.shape[1:], F32)
+
+    seam_rows[...] = jnp.zeros(seam_rows.shape, F32)
     padded[pl.ds(N, padded.shape[0] - N)] = jnp.zeros((padded.shape[0] - N, rows), F32)
 
     with jax.named_scope("entry barrier"):
@@ -167,58 +175,87 @@
 
     first_row, last_row = OFF, OFF + N - 1
 
-    def edge_copy(p, i):
-        return remote(ts.at[p], tr.at[p, i], es.at[p, i], er.at[p, i], tm + (1, -1)[i], lon)
-
-    def edge_send(p, X):
-        ts[p, 0:1] = X[2, first_row:first_row + 1]
-        ts[p, 1:2] = X[2, last_row:last_row + 1]
+    def edge_copy(i):
+        return remote(ts, tr.at[i], es.at[i], er.at[i], tm + (1, -1)[i], lon)
+
+    def edge_send():
+        ts[0:1] = E[2, first_row:first_row + 1]
+        ts[1:2] = E[2, last_row:last_row + 1]
         for i, dt in enumerate((1, -1)):
-            when_t(dt, lambda i=i: edge_copy(p, i).start())
-
-    def rim_copy(p, i):
-        return remote(ls.at[p, i], lr.at[p, i], rs_.at[p, i], rr.at[p, i], tm, lon_at((1, -1)[i]))
+            when_t(dt, lambda i=i: edge_copy(i).start())
+
+    def seam_copy(l):
+        return remote(ED.at[lon], ED.at[lon], sems.at[0], sems.at[1], tm, l)
+
+    def seam_all():
+        return remote(ED.at[pl.ds(0, 7)], ED.at[pl.ds(0, 7)], sems.at[0], sems.at[1], tm, lon)
+
+    def seam_fill():
+        for i, dt in enumerate((1, -1)):
+            when_t(-dt, lambda i=i: edge_copy(i).wait_recv())
+        bent = tr[0] + tr[1] - 2.0 * ts[...]
+        for at, row, inner, side_row in ((0, first_row, first_row + 1, 0), (4, last_row, last_row - 1, 1)):
+            ED[lon, at:at + 1] = E[2, row:row + 1]
+            ED[lon, at + 1:at + 2] = E[2, inner:inner + 1]
+            ED[lon, at + 2:at + 3] = bent[side_row:side_row + 1]
+            ED[lon, at + 3:at + 4] = B[row:row + 1]
+
+    def far_lon(d):
+        return lax.rem(x + d, 4) * 2 + 1 - zh
+
+    rim_days = (0, 1, -1)
+
+    def rim_copy(p, i, j):
+        dt = rim_days[i]
+        return remote(ls.at[p, j], lr.at[p, i, j], rs_.at[p, i], rr.at[p, i], tm + dt, lon_at((1, -1)[j]))
+
+    def rim_all(p, i):
+        return remote(lr.at[p, i], lr.at[p, i], rs_.at[p, i], rr.at[p, i], tm, lon)
 
     def rim_send(p, X):
-        for i, dt in enumerate((1, -1)):
-            when_t(-dt, lambda i=i: edge_copy(p, i).wait_recv())
-        bent = tr[p, 0] + tr[p, 1] - 2.0 * ts[p]
         ls[p, 0, 0:1] = X[2, last_row:last_row + 1]
         ls[p, 0, 1:2] = X[2, last_row - 1:last_row]
-        ls[p, 0, 2:3] = bent[1:2]
-        ls[p, 0, 3:4] = B[last_row:last_row + 1]
         ls[p, 1, 0:1] = X[2, first_row:first_row + 1]
         ls[p, 1, 1:2] = X[2, first_row + 1:first_row + 2]
-        ls[p, 1, 2:3] = bent[0:1]
-        ls[p, 1, 3:4] = B[first_row:first_row + 1]
-        for i in range(2):
-            rim_copy(p, i).start()
+        for i in (1, 2, 0):
+            for j in range(2):
+                when_t(rim_days[i], lambda i=i, j=j: rim_copy(p, i, j).start())
+
+    beside = ((first_row - 1, first_row - 2), (last_row + 1, last_row + 2))
 
     def rim_take(p, X):
-        for i in range(2):
-            rim_copy(p, i).wait_recv()
-        for i, (near, far) in enumerate(((first_row - 1, first_row - 2), (last_row + 1, last_row + 2))):
-            X[2, near:near + 1] = lr[p, i, 0:1]
-            X[2, far:far + 1] = lr[p, i, 1:2]
-            X[1, near:near + 1] = lr[p, i, 2:3] + 2.0 * lr[p, i, 0:1]
-            X[3, near:near + 1] = jnp.zeros((1, rows), F32)
-            if p == 0:
-                B[near:near + 1] = lr[p, i, 3:4]
-
-    def edge_done(p):
-        for i, dt in enumerate((1, -1)):
-            when_t(dt, lambda i=i: edge_copy(p, i).wait_send())
-            rim_copy(p, i).wait_send()
+        for i, dt in enumerate(rim_days):
+
+            def take(i=i, dt=dt):
+                rim_all(p, i).wait_recv()
+                for j, (near, far) in enumerate(beside):
+                    X[2 - dt, near:near + 1] = lr[p, i, j, 0:1]
+                    if dt == 0:
+                        X[2, far:far + 1] = lr[p, i, j, 1:2]
+
+            when_t(-dt, take)
+
+    def rim_done(p):
+        for i, dt in enumerate(rim_days):
+            when_t(dt, lambda i=i: rim_all(p, i).wait_send())
 
     with jax.named_scope("guess edges"):
         loads[0].wait()
-        edge_send(0, E)
+        edge_send()
         halo_send(0, E)
     loads[1].wait()
     with jax.named_scope("far hello"):
         pl.semaphore_wait(hello, len(fours))
-    with jax.named_scope("guess rim"):
-        rim_send(0, E)
+    with jax.named_scope("guess seams"):
+        for d in (1, 3):
+            greet(tm, lon_at(2 * d), sem=hello2)
+        seam_fill()
+        for d in (0, 1, 3):
+            seam_copy(far_lon(d)).start()
+        for d in (2, 1, 3):
+            seam_copy(lon_at(2 * d)).start()
+        pl.semaphore_wait(hello2, 2)
+        seam_copy(far_lon(2)).start()
     with jax.named_scope("guess hand on"):
         halo_hand(0, E)
 
@@ -269,11 +306,11 @@
 
     with jax.named_scope("guess halo wait"):
         halo_wait(0, E)
-    with jax.named_scope("guess rim wait"):
-        rim_take(0, E)
     for s, n in ext_chunks:
         r = pl.ds(s, n)
         TV[r] = second(E[1, r], E[3, r], E[2, r])
+    for near, _ in beside:
+        TV[near:near + 1] = jnp.zeros((1, rows), F32)
     for s, n in own_chunks:
         r = pl.ds(s, n)
         T2V[r] = second2(E[0, r], E[1, r], E[2, r], E[3, r], E[4, r])
@@ -285,10 +322,14 @@
         padded[l] = g
 
     with jax.named_scope("first operator"):
+        for near, _ in beside:
+            E[2, near:near + 1] = jnp.zeros((1, rows), F32)
         flatten(E.at[2])
         once()
+        for near, _ in beside:
+            Y[near:near + 1] = jnp.zeros((1, rows), F32)
         twice(emit_g)
-    for c in loads[5:7]:
+    for c in loads[5:7] + loads[8:]:
         c.wait()
 
     half = lax.broadcasted_iota(jnp.int32, (MW, rows), 1) < MW
@@ -315,6 +356,35 @@
     def at_all(p, i):
         some = AT.at[p, 2 - days[i], pl.ds(0, MW if days[i] else MW - 16)]
         return remote(some, some, ats.at[p, i], atr.at[p, i], tm, lon)
+
+    half16 = lax.broadcasted_iota(jnp.int32, (16, rows), 1) < MW
+
+    def seam_take():
+        seam_all().wait_recv()
+        er1, er2, ter, ber = (pltpu.roll(ED[:, i, :], 7, axis=0) for i in range(4))
+        el1, el2, tel, bel = (ED[:, i, :] for i in range(4, 8))
+
+        def across(v):
+            lo = jnp.where(first_lane, 0.0, pltpu.roll(v, 1, axis=1))
+            hi = jnp.where(last_lane, 0.0, pltpu.roll(v, rows - 1, axis=1))
+            return lo + hi - 2.0 * v
+
+        yl = bel * (tel + across(el1) + bend * (el2 + er1 - 2.0 * el1))
+        yr = ber * (ter + across(er1) + bend * (er2 + el1 - 2.0 * er1))
+        dr_, dl_ = ber * bend * el1, bel * bend * er1
+        seam_rows[0:8] = bend * (yl + ber * tel - 2.0 * dr_) + across(dr_)
+        seam_rows[8:16] = bend * dr_
+        seam_rows[16:24] = bend * (yr + bel * ter - 2.0 * dl_) + across(dl_)
+        seam_rows[24:32] = bend * dl_
+        before = lon_at(-1)
+        for row, place in (
+            (first_row, before), (first_row + 1, 8 + before), (last_row, 16 + lon), (last_row - 1, 24 + lon)
+        ):
+            G[2, row:row + 1] += seam_rows[pl.ds(place, 1)]
+        B[first_row - 1:first_row] = ED[before, 7:8]
+        B[last_row + 1:last_row + 2] = ED[lon_at(1), 3:4]
+        part = lax.dot(seams[...], seam_rows[...], precision=lax.Precision.HIGH, preferred_element_type=F32)
+        seam_amp[...] = jnp.where(half16, pltpu.roll(part[:16], MW, axis=1), part[16:])
 
     def transform_start(p):
         part = lax.dot(fwd[...], padded[...], precision=lax.Precision.HIGH, preferred_element_type=F32)
@@ -333,6 +403,8 @@
     def transform_spread(p):
         z_copy(p).wait_recv()
         total = quarter[p, 0] + z_buf[p]
+        if p == 0:
+            total = total + seam_amp[...]
         quarter[p, 1] = total
         for i, dt in enumerate(days):
             for d in (2, 1, 3, 0) if dt else (2, 1, 3):
@@ -438,12 +510,12 @@
 
     with jax.named_scope("transform zero"):
         transform_start(0)
-    with jax.named_scope("edges one send"):
-        edge_send(1, G)
     with jax.named_scope("cross zero"):
         transform_cross(0)
+    with jax.named_scope("seams"):
+        seam_take()
     with jax.named_scope("rim one send"):
-        rim_send(1, G)
+        rim_send(0, G)
     with jax.named_scope("halo one send"):
         halo_send(1, G)
     with jax.named_scope("spread zero"):
@@ -451,7 +523,7 @@
     with jax.named_scope("hand on one"):
         halo_hand(1, G)
     with jax.named_scope("rim one wait"):
-        rim_take(1, G)
+        rim_take(0, G)
     with jax.named_scope("halo one wait"):
         halo_wait(1, G)
     with jax.named_scope("filter zero local"):
@@ -486,11 +558,10 @@
         transform_start(1)
     with jax.named_scope("edges two send"):
         dot_send(0, 0, pack(*acc))
-        edge_send(2, U)
     with jax.named_scope("cross one"):
         transform_cross(1)
     with jax.named_scope("rim two send"):
-        rim_send(2, U)
+        rim_send(1, U)
     with jax.named_scope("halo two send"):
         halo_send(2, U)
     with jax.named_scope("sums zero"):
@@ -500,7 +571,7 @@
     with jax.named_scope("hand on two"):
         halo_hand(2, U)
     with jax.named_scope("rim two wait"):
-        rim_take(2, U)
+        rim_take(1, U)
     with jax.named_scope("halo two wait"):
         halo_wait(2, U)
     with jax.named_scope("filter one local"):
@@ -543,9 +614,12 @@
         dot_send(1, 1, dot_take(1, 0))
     for p, X in enumerate((E, G, U)):
         halo_done(p, X)
-        edge_done(p)
+    for i, dt in enumerate((1, -1)):
+        when_t(dt, lambda i=i: edge_copy(i).wait_send())
+    seam_all().wait_send()
     for p in range(2):
         transform_done(p)
+        rim_done(p)
     dot_done(0)
     with jax.named_scope("sums one c"):
         out_step[...] = jnp.broadcast_to(ratio(dot_take(1, 1)), out_step.shape)
@@ -555,7 +629,7 @@
 
 def on_device(NT, NL, first, obs, track, land, bw):
     _, N, rows = first.shape
-    forward, inverse, row = tables(NL, N, rows)
+    forward, inverse, row, seams = tables(NL, N, rows)
     plane = pltpu.VMEM((N + 32, rows), F32)
     planes = pltpu.VMEM((5, N + 32, rows), F32)
     flat = pltpu.VMEM((N, rows), F32)
@@ -565,7 +639,7 @@
     surface, search, gradient, curved, step = pl.pallas_call(
         functools.partial(kernel, NT, N),
         out_shape=[pltpu.VMEM(first.shape, F32)] * 4 + [pltpu.VMEM((1, rows), F32)],
-        in_specs=[hbm] * 8,
+        in_specs=[hbm] * 9,
         out_specs=[pl.BlockSpec(memory_space=pltpu.VMEM)] * 5,
         scratch_shapes=[
             pltpu.VMEM(row.shape, F32), planes, planes, planes,
@@ -573,6 +647,8 @@
             pltpu.VMEM(forward.shape[1:], F32), pltpu.VMEM(inverse.shape[1:], F32),
             plane, plane, plane, plane, plane, flat,
             pltpu.VMEM((forward.shape[2], rows), F32),
+            pltpu.VMEM(seams.shape[1:], F32), pltpu.VMEM((128, rows), F32),
+            pltpu.VMEM((16, rows), F32), pltpu.VMEM((8, 8, rows), F32),
             pltpu.VMEM((2, MW, rows), F32),
             pltpu.VMEM((2, 4, 16, rows), F32),
             pltpu.VMEM((2, 2, 16, rows), F32),
@@ -580,19 +656,19 @@
             pltpu.VMEM((2, 5, MW, rows), F32),
             pltpu.VMEM((2, 32, 1, rows), F32),
             pltpu.VMEM((2, 16, 1, rows), F32),
-            pltpu.VMEM((3, 2, rows), F32),
-            pltpu.VMEM((3, 2, 2, rows), F32),
-            pltpu.VMEM((3, 2, 4, rows), F32),
-            pltpu.VMEM((3, 2, 4, rows), F32),
-            pltpu.SemaphoreType.REGULAR, dma((8,)), dma((3, 4)), dma((3, 4)),
-            dma((3, 2)), dma((3, 2)), dma((3, 2)), dma((3, 2)),
+            pltpu.VMEM((2, rows), F32),
+            pltpu.VMEM((2, 2, rows), F32),
+            pltpu.VMEM((2, 2, 2, rows), F32),
+            pltpu.VMEM((2, 3, 2, 2, rows), F32),
+            pltpu.SemaphoreType.REGULAR, pltpu.SemaphoreType.REGULAR, dma((2,)), dma((9,)), dma((3, 4)), dma((3, 4)),
+            dma((2,)), dma((2,)), dma((2, 3)), dma((2, 3)),
             dma((2,)), dma((2,)), dma((2,)), dma((2,)), dma((2, 5)), dma((2, 5)),
             dma((2, 2)), dma((2, 2)),
         ],
         compiler_params=pltpu.CompilerParams(
             collective_id=0, has_side_effects=True, vmem_limit_bytes=56 * 1024 * 1024
         ),
-    )(first, obs, track, land, bw, forward, inverse, row)
+    )(first, obs, track, land, bw, forward, inverse, row, seams)
     return surface - step[None] * search, gradient - step[None] * curved
 
 

time: 74.2 us -> 69 us (0.930)
  Pallas kernels: 72.6 us -> 67.4 us
    pallas_call x1, Pallas kernels: 72.6 us -> 67.4 us  [on_device(): pl.pallas_call(functools.partial(kernel, NT, N), out_shape=[pltpu.VMEM(fi...]
where the time goes in v5:
time: 69 us; the launch traced here: 68.8 us
  Pallas kernels  67.4 us (98%)
  other arithmetic  0.79 us (1%)
    pallas_call x1, Pallas kernels, on_device(): pl.pallas_call(functools.partial(kernel, NT, N), out_shape=[pltpu.VMEM(fi...  67.4 us

profile of v5, /device:TPU:1, one launch (start us, length us, event | category | flops | bytes accessed | tf_op | source)
XLA Modules:
  0.0 68.8 jit_solution(10038271397761830107)
XLA Ops:
  0.6 67.4 %shard_map.104 = (f32[1,360,128]{2,1,0:T(8,128)S(1)}, f32[1,360,128]{2,1,0:T(8,128)S(1)}, f32[1,360,128]{2,1,0:T(8,128)S(1)}, f32[1,360,128]{2,1,0:T(8,128)S(1)}, f32[1,128]{1,0:T(1,128)S(1)}) custom-call(f32[1,360,128]{2,1,0:T(8,128)} %first_ref.1, f32[1,360,128]{2,1,0:T(8,128)} %obs_ref.1, s32[1,360,128]{2,1,0:T(8,128)} %track_ref.1, s32[360,128]{1,0:T(8,128)} %land_ref.1, ...), custom_call_target="tpu_custom_call" | custom-call | tf_op jit(solution)/shard_map/pallas_call | solution.py:639
  68.0 0.8 %multiply_subtract_fusion = (f32[1,360,128]{2,1,0:T(8,128)}, f32[1,360,128]{2,1,0:T(8,128)}) fusion(f32[1,360,128]{2,1,0:T(8,128)S(1)} %get-tuple-element.10, f32[1,360,128]{2,1,0:T(8,128)S(1)} %get-tuple-element.11, f32[128]{0:T(128)S(1)} %bitcast.1, f32[1,360,128]{2,1,0:T(8,128)S(1)} %get-tuple-element.7, f32[1,360,128]{2,1,0:T(8,128)S(1)} %get-tuple-element.9), kind=kLoop, calls=%fused_computation | loop fusion | flops 184320 | bytes 1106432 | tf_op jit(solution)/shard_map/sub | solution.py:672

commit v6 on v5

--- a/solution.py
+++ b/solution.py
@@ -52,8 +52,8 @@
     NT, N, first_ref, obs_ref, track_ref, land_ref, bw_ref, fwd_ref, inv_ref, row_hbm, seams_hbm,
     out_a, out_s, out_g, out_c, out_step,
     row_ref, E, G, U, B, W, obs, track, land, fwd, inv, V, TV, T2V, Y, V0, LV0, padded, seams, seam_rows, seam_amp, ED, amp, rs_buf, quarter,
-    z_buf, AT, dots_a, dots_b, ts, tr, ls, lr,
-    hello, hello2, sems, lsem, hs, hr, es, er, rs_, rr, xs, xr, zs, zr, ats, atr, ds_, dr,
+    z_buf, AT, dots_a, dots_b, ts, tr, ls, lr, bs, br,
+    hello, sems, bsem, brem, lsem, hs, hr, es, er, rs_, rr, xs, xr, zs, zr, ats, atr, ds_, dr,
 ):
     tm = lax.axis_index("tm")
     lon = lax.axis_index("lon")
@@ -97,18 +97,15 @@
 
     def on_z(place, xx):
         place = lax.rem(place + 16, 16)
-        return lax.rem(place, 8) * 8 + k, lax.rem(xx + 4, 4) * 2 + place // 8
-
-    fours = [(dz, dx) for dz in (4, -4) for dx in (0, 1, -1)]
-    for dz, dx in fours:
-        greet(*on_z(z + dz, x + dx))
-    for dz in (3, -3, 2, -2, 1, -1):
+        return lax.rem(place, 8) * 8 + k, xx * 2 + place // 8
+
+    for dz in (2, -2, 1, -1):
         greet(*on_z(z + dz, x))
     for d in range(1, 8):
         greet(zl * 8 + lax.rem(k + d, 8), lon)
     for d in range(1, 4):
         greet(tm, lon_at(2 * d))
-    count = jnp.int32(len(fours) + 6 + 7 + 3)
+    count = jnp.int32(4 + 7 + 3)
     for dt in (-2, -1, 1, 2):
         when_t(dt, lambda dt=dt: greet(tm + dt, lon))
         count = count + jnp.where(inside(tm + dt), 1, 0)
@@ -127,12 +124,13 @@
                 tr[(dt + 1) // 2] = jnp.zeros(tr.shape[1:], F32)
 
     seam_rows[...] = jnp.zeros(seam_rows.shape, F32)
+    bs[...] = jnp.zeros(bs.shape, F32)
     padded[pl.ds(N, padded.shape[0] - N)] = jnp.zeros((padded.shape[0] - N, rows), F32)
 
     with jax.named_scope("entry barrier"):
         pl.semaphore_wait(barrier, count)
-    for dz, dx in fours:
-        greet(*on_z(z + dz, x + dx), sem=hello)
+    for dz in (2, -2):
+        greet(*on_z(z + dz, x), sem=hello.at[0])
 
     def remote(src, dst, send, recv, t, l):
         return pltpu.make_async_remote_copy(
@@ -167,11 +165,11 @@
     def halo_wait(p, X):
         for i in (1, 2, 3):
             pl.when(inside(tm + recv_days[i]))(lambda i=i: plane_recv(p, X, i).wait_recv())
+        pl.when(inside(tm - side))(lambda: hand_copy(p, X).wait_send())
 
     def halo_done(p, X):
         for i in range(3):
             pl.when(inside(tm + send_days[i]))(lambda i=i: plane_copy(p, X, i).wait_send())
-        pl.when(inside(tm - side))(lambda: hand_copy(p, X).wait_send())
 
     first_row, last_row = OFF, OFF + N - 1
 
@@ -203,61 +201,81 @@
     def far_lon(d):
         return lax.rem(x + d, 4) * 2 + 1 - zh
 
-    rim_days = (0, 1, -1)
-
-    def rim_copy(p, i, j):
-        dt = rim_days[i]
-        return remote(ls.at[p, j], lr.at[p, i, j], rs_.at[p, i], rr.at[p, i], tm + dt, lon_at((1, -1)[j]))
-
-    def rim_all(p, i):
-        return remote(lr.at[p, i], lr.at[p, i], rs_.at[p, i], rr.at[p, i], tm, lon)
+    def rim_copy(p, j):
+        return remote(ls.at[p, j], lr.at[p, j], rs_.at[p], rr.at[p], tm, lon_at((1, -1)[j]))
+
+    def rim_all(p):
+        return remote(lr.at[p], lr.at[p], rs_.at[p], rr.at[p], tm, lon)
 
     def rim_send(p, X):
         ls[p, 0, 0:1] = X[2, last_row:last_row + 1]
         ls[p, 0, 1:2] = X[2, last_row - 1:last_row]
         ls[p, 1, 0:1] = X[2, first_row:first_row + 1]
         ls[p, 1, 1:2] = X[2, first_row + 1:first_row + 2]
-        for i in (1, 2, 0):
-            for j in range(2):
-                when_t(rim_days[i], lambda i=i, j=j: rim_copy(p, i, j).start())
+        for j in range(2):
+            rim_copy(p, j).start()
 
     beside = ((first_row - 1, first_row - 2), (last_row + 1, last_row + 2))
+    before = lon_at(-1)
 
     def rim_take(p, X):
-        for i, dt in enumerate(rim_days):
+        rim_all(p).wait_recv()
+        for j, (near, far) in enumerate(beside):
+            for i, row in enumerate((near, far)):
+                line = lr[p, j, i:i + 1]
+                if p == 0:
+                    line = line + seam_rows[pl.ds((16, 0)[j] + 8 * i + (before, lon)[j], 1)]
+                X[2, row:row + 1] = line
+
+    border_rows = (first_row, first_row + 1, last_row - 1, last_row, first_row - 1, last_row + 1)
+    border_days = (2, -2, 1, -1)
+
+    def border_copy(p, i):
+        return remote(bs.at[p], br.at[p, i], bsem.at[p, i], brem.at[p, i], tm + border_days[i], lon)
+
+    def border_send(p, X):
+        for i, row in enumerate(border_rows):
+            bs[p, i:i + 1] = X[2, row:row + 1]
+        for i, dt in enumerate(border_days):
+            when_t(dt, lambda i=i: border_copy(p, i).start())
+
+    def border_take(p, X):
+        for i, dt in enumerate(border_days):
 
             def take(i=i, dt=dt):
-                rim_all(p, i).wait_recv()
-                for j, (near, far) in enumerate(beside):
-                    X[2 - dt, near:near + 1] = lr[p, i, j, 0:1]
-                    if dt == 0:
-                        X[2, far:far + 1] = lr[p, i, j, 1:2]
+                border_copy(p, i).wait_recv()
+                for j, row in enumerate(border_rows[:6 if abs(dt) == 1 else 4]):
+                    X[2 - dt, row:row + 1] = br[p, i, j:j + 1]
 
             when_t(-dt, take)
 
-    def rim_done(p):
-        for i, dt in enumerate(rim_days):
-            when_t(dt, lambda i=i: rim_all(p, i).wait_send())
+    def border_done(p):
+        for i, dt in enumerate(border_days):
+            when_t(dt, lambda i=i: border_copy(p, i).wait_send())
 
     with jax.named_scope("guess edges"):
         loads[0].wait()
         edge_send()
         halo_send(0, E)
+    with jax.named_scope("far hello"):
+        pl.semaphore_wait(hello.at[0], 2)
+        for dz in (4, -4):
+            greet(*on_z(z + dz, x), sem=hello.at[1])
     loads[1].wait()
-    with jax.named_scope("far hello"):
-        pl.semaphore_wait(hello, len(fours))
     with jax.named_scope("guess seams"):
-        for d in (1, 3):
-            greet(tm, lon_at(2 * d), sem=hello2)
         seam_fill()
-        for d in (0, 1, 3):
-            seam_copy(far_lon(d)).start()
         for d in (2, 1, 3):
             seam_copy(lon_at(2 * d)).start()
-        pl.semaphore_wait(hello2, 2)
-        seam_copy(far_lon(2)).start()
+        pl.semaphore_wait(hello.at[1], 2)
+        for d in (2, 1, 3):
+            greet(tm, lon_at(2 * d), sem=hello.at[2])
+        seam_copy(far_lon(0)).start()
     with jax.named_scope("guess hand on"):
         halo_hand(0, E)
+    with jax.named_scope("guess far seams"):
+        pl.semaphore_wait(hello.at[2], 3)
+        for d in (2, 1, 3):
+            seam_copy(far_lon(d)).start()
 
     lane = lax.broadcasted_iota(jnp.int32, (8, rows), 1)
     first_lane, last_lane = lane[:1] == 0, lane[:1] == rows - 1
@@ -376,7 +394,6 @@
         seam_rows[8:16] = bend * dr_
         seam_rows[16:24] = bend * (yr + bel * ter - 2.0 * dl_) + across(dl_)
         seam_rows[24:32] = bend * dl_
-        before = lon_at(-1)
         for row, place in (
             (first_row, before), (first_row + 1, 8 + before), (last_row, 16 + lon), (last_row - 1, 24 + lon)
         ):
@@ -510,22 +527,26 @@
 
     with jax.named_scope("transform zero"):
         transform_start(0)
-    with jax.named_scope("cross zero"):
-        transform_cross(0)
-    with jax.named_scope("seams"):
-        seam_take()
     with jax.named_scope("rim one send"):
         rim_send(0, G)
     with jax.named_scope("halo one send"):
         halo_send(1, G)
+    with jax.named_scope("cross zero"):
+        transform_cross(0)
+    with jax.named_scope("seams"):
+        halo_done(1, G)
+        seam_take()
+    with jax.named_scope("rim one wait"):
+        rim_take(0, G)
+    with jax.named_scope("border one send"):
+        border_send(0, G)
+    with jax.named_scope("hand on one"):
+        halo_hand(1, G)
     with jax.named_scope("spread zero"):
         transform_spread(0)
-    with jax.named_scope("hand on one"):
-        halo_hand(1, G)
-    with jax.named_scope("rim one wait"):
-        rim_take(0, G)
     with jax.named_scope("halo one wait"):
         halo_wait(1, G)
+        border_take(0, G)
     with jax.named_scope("filter zero local"):
         filter_local(G, V0)
     with jax.named_scope("finish zero"):
@@ -558,22 +579,25 @@
         transform_start(1)
     with jax.named_scope("edges two send"):
         dot_send(0, 0, pack(*acc))
-    with jax.named_scope("cross one"):
-        transform_cross(1)
     with jax.named_scope("rim two send"):
         rim_send(1, U)
     with jax.named_scope("halo two send"):
         halo_send(2, U)
+    with jax.named_scope("cross one"):
+        transform_cross(1)
     with jax.named_scope("sums zero"):
         dot_send(0, 1, dot_take(0, 0))
+    with jax.named_scope("rim two wait"):
+        rim_take(1, U)
+    with jax.named_scope("border two send"):
+        border_send(1, U)
+    with jax.named_scope("hand on two"):
+        halo_hand(2, U)
     with jax.named_scope("spread one"):
         transform_spread(1)
-    with jax.named_scope("hand on two"):
-        halo_hand(2, U)
-    with jax.named_scope("rim two wait"):
-        rim_take(1, U)
     with jax.named_scope("halo two wait"):
         halo_wait(2, U)
+        border_take(1, U)
     with jax.named_scope("filter one local"):
         filter_local(U, V)
     with jax.named_scope("finish one"):
@@ -612,14 +636,15 @@
         twice(emit_last)
     with jax.named_scope("sums one b"):
         dot_send(1, 1, dot_take(1, 0))
-    for p, X in enumerate((E, G, U)):
-        halo_done(p, X)
+    halo_done(0, E)
+    halo_done(2, U)
     for i, dt in enumerate((1, -1)):
         when_t(dt, lambda i=i: edge_copy(i).wait_send())
     seam_all().wait_send()
     for p in range(2):
         transform_done(p)
-        rim_done(p)
+        rim_all(p).wait_send()
+        border_done(p)
     dot_done(0)
     with jax.named_scope("sums one c"):
         out_step[...] = jnp.broadcast_to(ratio(dot_take(1, 1)), out_step.shape)
@@ -659,9 +684,11 @@
             pltpu.VMEM((2, rows), F32),
             pltpu.VMEM((2, 2, rows), F32),
             pltpu.VMEM((2, 2, 2, rows), F32),
-            pltpu.VMEM((2, 3, 2, 2, rows), F32),
-            pltpu.SemaphoreType.REGULAR, pltpu.SemaphoreType.REGULAR, dma((2,)), dma((9,)), dma((3, 4)), dma((3, 4)),
-            dma((2,)), dma((2,)), dma((2, 3)), dma((2, 3)),
+            pltpu.VMEM((2, 2, 2, rows), F32),
+            pltpu.VMEM((2, 8, rows), F32),
+            pltpu.VMEM((2, 4, 8, rows), F32),
+            pltpu.SemaphoreType.REGULAR((3,)), dma((2,)), dma((2, 4)), dma((2, 4)), dma((9,)), dma((3, 4)), dma((3, 4)),
+            dma((2,)), dma((2,)), dma((2,)), dma((2,)),
             dma((2,)), dma((2,)), dma((2,)), dma((2,)), dma((2, 5)), dma((2, 5)),
             dma((2, 2)), dma((2, 2)),
         ],

time: 69 us -> 68.8 us (level)
  no operation moved by 1% of the time
where the time goes in v6:
time: 68.8 us; the launch traced here: 68.7 us
  Pallas kernels  67.3 us (98%)
  other arithmetic  0.79 us (1%)
    pallas_call x1, Pallas kernels, on_device(): pl.pallas_call(functools.partial(kernel, NT, N), out_shape=[pltpu.VMEM(fi...  67.3 us

profile of v6, /device:TPU:1, one launch (start us, length us, event | category | flops | bytes accessed | tf_op | source)
XLA Modules:
  0.0 68.7 jit_solution(908373881361662711)
XLA Ops:
  0.6 67.3 %shard_map.104 = (f32[1,360,128]{2,1,0:T(8,128)S(1)}, f32[1,360,128]{2,1,0:T(8,128)S(1)}, f32[1,360,128]{2,1,0:T(8,128)S(1)}, f32[1,360,128]{2,1,0:T(8,128)S(1)}, f32[1,128]{1,0:T(1,128)S(1)}) custom-call(f32[1,360,128]{2,1,0:T(8,128)} %first_ref.1, f32[1,360,128]{2,1,0:T(8,128)} %obs_ref.1, s32[1,360,128]{2,1,0:T(8,128)} %track_ref.1, s32[360,128]{1,0:T(8,128)} %land_ref.1, ...), custom_call_target="tpu_custom_call" | custom-call | tf_op jit(solution)/shard_map/pallas_call | solution.py:664
  67.9 0.8 %multiply_subtract_fusion = (f32[1,360,128]{2,1,0:T(8,128)}, f32[1,360,128]{2,1,0:T(8,128)}) fusion(f32[1,360,128]{2,1,0:T(8,128)S(1)} %get-tuple-element.10, f32[1,360,128]{2,1,0:T(8,128)S(1)} %get-tuple-element.11, f32[128]{0:T(128)S(1)} %bitcast.1, f32[1,360,128]{2,1,0:T(8,128)S(1)} %get-tuple-element.7, f32[1,360,128]{2,1,0:T(8,128)S(1)} %get-tuple-element.9), kind=kLoop, calls=%fused_computation | loop fusion | flops 184320 | bytes 1106432 | tf_op jit(solution)/shard_map/sub | solution.py:699

commit v7 on v6

--- a/solution.py
+++ b/solution.py
@@ -51,9 +51,9 @@
 def kernel(
     NT, N, first_ref, obs_ref, track_ref, land_ref, bw_ref, fwd_ref, inv_ref, row_hbm, seams_hbm,
     out_a, out_s, out_g, out_c, out_step,
-    row_ref, E, G, U, B, W, obs, track, land, fwd, inv, V, TV, T2V, Y, V0, LV0, padded, seams, seam_rows, seam_amp, ED, amp, rs_buf, quarter,
+    row_ref, E, G, U, B, W, obs, track, land, fwd, inv, V, TV, T2V, Y, V0, LV0, padded, seams, seam_rows, seam_amp, ED, three, amp3, rs3, sum3, day3, amp, rs_buf, quarter,
     z_buf, AT, dots_a, dots_b, ts, tr, ls, lr, bs, br,
-    hello, sems, bsem, brem, lsem, hs, hr, es, er, rs_, rr, xs, xr, zs, zr, ats, atr, ds_, dr,
+    hello, fs, fr, sems, bsem, brem, lsem, hs, hr, es, er, rs_, rr, xs, xr, zs, zr, ats, atr, ds_, dr,
 ):
     tm = lax.axis_index("tm")
     lon = lax.axis_index("lon")
@@ -122,10 +122,62 @@
                 AT[p, 2 + dt] = jnp.zeros(AT.shape[2:], F32)
             if abs(dt) == 1:
                 tr[(dt + 1) // 2] = jnp.zeros(tr.shape[1:], F32)
+            day3[2 + dt] = jnp.zeros(day3.shape[1:], F32)
 
     seam_rows[...] = jnp.zeros(seam_rows.shape, F32)
     bs[...] = jnp.zeros(bs.shape, F32)
+    three[pl.ds(N, three.shape[0] - N)] = jnp.zeros((three.shape[0] - N, 3 * rows), F32)
     padded[pl.ds(N, padded.shape[0] - N)] = jnp.zeros((padded.shape[0] - N, rows), F32)
+
+    lane = lax.broadcasted_iota(jnp.int32, (8, rows), 1)
+    first_lane, last_lane = lane[:1] == 0, lane[:1] == rows - 1
+    loads[7].wait()
+    bend = row_ref[0:1]
+    centre = row_ref[1:2]
+    shrink = row_ref[2:3]
+    keep = row_ref[3:4]
+
+    def flat(ref, start, n):
+        v = ref[pl.ds(start, n)]
+        up, down = ref[pl.ds(start + 1, n)], ref[pl.ds(start - 1, n)]
+        lo = jnp.where(first_lane, 0.0, pltpu.roll(v, 1, axis=1))
+        hi = jnp.where(last_lane, 0.0, pltpu.roll(v, rows - 1, axis=1))
+        return bend * (up + down) + (lo + hi) + centre * v
+
+    own_chunks = [(OFF + c, 72) for c in range(0, N, 72)]
+    ext_chunks = [(EXT, 8)] + own_chunks + [(OFF + N, 8)]
+    centre_t2 = jnp.where((tm == 0) | (tm == NT - 1), 5.0, 6.0).astype(F32)
+
+    def second(a, b, c):
+        return a + b - 2.0 * c
+
+    def second2(a, b, c, d, e):
+        return a + e - 4.0 * (b + d) + centre_t2 * c
+
+    half = lax.broadcasted_iota(jnp.int32, (MW, rows), 1) < MW
+
+    beside = ((OFF - 1, OFF - 2), (OFF + N, OFF + N + 1))
+    for c in loads[:6]:
+        c.wait()
+    W[...] = track[...].astype(F32) * (1.0 - land[...].astype(F32))
+    for near, _ in beside:
+        for ref in (E.at[2], TV, Y):
+            ref[near:near + 1] = jnp.zeros((1, rows), F32)
+    for s, n in own_chunks:
+        r = pl.ds(s, n)
+        TV[r] = B[r] * E[2, r]
+        Y[r] = B[r] * flat(E.at[2], s, n)
+    for s, n in own_chunks:
+        l, r = pl.ds(s - OFF, n), pl.ds(s, n)
+        three[l, 0:rows] = W[l] * (E[2, r] - obs[l]) + flat(Y, s, n)
+        three[l, rows:2 * rows] = Y[r] + flat(TV, s, n)
+        three[l, 2 * rows:3 * rows] = TV[r]
+    parts = lax.dot(fwd[...], three[...], precision=lax.Precision.HIGH, preferred_element_type=F32)
+    for f in range(3):
+        part = parts[:, f * rows:(f + 1) * rows]
+        part = jnp.where(half, pltpu.roll(part[:MW], MW, axis=1), part[MW:])
+        for q in range(4):
+            amp3[q, 16 * f:16 * f + 16] = part[16 * q:16 * q + 16]
 
     with jax.named_scope("entry barrier"):
         pl.semaphore_wait(barrier, count)
@@ -215,7 +267,6 @@
         for j in range(2):
             rim_copy(p, j).start()
 
-    beside = ((first_row - 1, first_row - 2), (last_row + 1, last_row + 2))
     before = lon_at(-1)
 
     def rim_take(p, X):
@@ -253,19 +304,63 @@
         for i, dt in enumerate(border_days):
             when_t(dt, lambda i=i: border_copy(p, i).wait_send())
 
+    def first_copy(d):
+        q = lax.rem(x + d, 4)
+        return remote(amp3.at[q], rs3.at[d], xs.at[0], xr.at[0], tm, q * 2 + zh)
+
+    def first_all():
+        return remote(rs3.at[pl.ds(1, 3)], rs3.at[pl.ds(1, 3)], xs.at[0], xr.at[0], tm, lon)
+
+    first_days = (2, -2, 1, -1)
+
+    def first_day_copy(i):
+        dt = first_days[i]
+        some = pl.ds(16, 32) if abs(dt) == 1 else pl.ds(32, 16)
+        return remote(sum3.at[some], day3.at[2 - dt, some], fs.at[i], fr.at[i], tm + dt, lon)
+
+    def first_sum():
+        first_all().wait_recv()
+        sum3[...] = amp3[x] + rs3[1] + rs3[2] + rs3[3]
+        for i, dt in enumerate(first_days):
+            when_t(dt, lambda i=i: first_day_copy(i).start())
+
+    def first_cross():
+        for i, dt in enumerate(first_days):
+            when_t(-dt, lambda i=i: first_day_copy(i).wait_recv())
+        one, two = pl.ds(16, 16), pl.ds(32, 16)
+        quarter[0, 0] = (
+            sum3[0:16]
+            + second(day3[1, one], day3[3, one], sum3[one])
+            + second2(day3[0, two], day3[1, two], sum3[two], day3[3, two], day3[4, two])
+        )
+        z_copy(0).start()
+
+    def first_done():
+        first_all().wait_send()
+        for i, dt in enumerate(first_days):
+            when_t(dt, lambda i=i: first_day_copy(i).wait_send())
+        z_copy(0).wait_send()
+
+    def z_copy(p):
+        return remote(quarter.at[p, 0], z_buf.at[p], zs.at[p], zr.at[p], tm, lon + 1 - 2 * zh)
+
+    with jax.named_scope("first amplitudes"):
+        for d in (2, 1, 3):
+            first_copy(d).start()
     with jax.named_scope("guess edges"):
-        loads[0].wait()
         edge_send()
         halo_send(0, E)
     with jax.named_scope("far hello"):
         pl.semaphore_wait(hello.at[0], 2)
         for dz in (4, -4):
             greet(*on_z(z + dz, x), sem=hello.at[1])
-    loads[1].wait()
     with jax.named_scope("guess seams"):
         seam_fill()
         for d in (2, 1, 3):
             seam_copy(lon_at(2 * d)).start()
+    with jax.named_scope("first sum"):
+        first_sum()
+    with jax.named_scope("guess far seam"):
         pl.semaphore_wait(hello.at[1], 2)
         for d in (2, 1, 3):
             greet(tm, lon_at(2 * d), sem=hello.at[2])
@@ -276,31 +371,8 @@
         pl.semaphore_wait(hello.at[2], 3)
         for d in (2, 1, 3):
             seam_copy(far_lon(d)).start()
-
-    lane = lax.broadcasted_iota(jnp.int32, (8, rows), 1)
-    first_lane, last_lane = lane[:1] == 0, lane[:1] == rows - 1
-    loads[7].wait()
-    bend = row_ref[0:1]
-    centre = row_ref[1:2]
-    shrink = row_ref[2:3]
-    keep = row_ref[3:4]
-
-    def flat(ref, start, n):
-        v = ref[pl.ds(start, n)]
-        up, down = ref[pl.ds(start + 1, n)], ref[pl.ds(start - 1, n)]
-        lo = jnp.where(first_lane, 0.0, pltpu.roll(v, 1, axis=1))
-        hi = jnp.where(last_lane, 0.0, pltpu.roll(v, rows - 1, axis=1))
-        return bend * (up + down) + (lo + hi) + centre * v
-
-    own_chunks = [(OFF + c, 72) for c in range(0, N, 72)]
-    ext_chunks = [(EXT, 8)] + own_chunks + [(OFF + N, 8)]
-    centre_t2 = jnp.where((tm == 0) | (tm == NT - 1), 5.0, 6.0).astype(F32)
-
-    def second(a, b, c):
-        return a + b - 2.0 * c
-
-    def second2(a, b, c, d, e):
-        return a + e - 4.0 * (b + d) + centre_t2 * c
+    with jax.named_scope("first cross"):
+        first_cross()
 
     def flatten(field):
         for s, n in ext_chunks:
@@ -316,11 +388,6 @@
     def twice(emit):
         for s, n in own_chunks:
             emit(s, n, B[pl.ds(s, n)] * (T2V[pl.ds(s, n)] + flat(TV, s, n)) + flat(Y, s, n))
-
-    with jax.named_scope("weights"):
-        for c in loads[2:5]:
-            c.wait()
-        W[...] = track[...].astype(F32) * (1.0 - land[...].astype(F32))
 
     with jax.named_scope("guess halo wait"):
         halo_wait(0, E)
@@ -337,7 +404,6 @@
         l = pl.ds(s - OFF, n)
         g = W[l] * (E[2, pl.ds(s, n)] - obs[l]) + u
         G[2, pl.ds(s, n)] = g
-        padded[l] = g
 
     with jax.named_scope("first operator"):
         for near, _ in beside:
@@ -347,10 +413,8 @@
         for near, _ in beside:
             Y[near:near + 1] = jnp.zeros((1, rows), F32)
         twice(emit_g)
-    for c in loads[5:7] + loads[8:]:
+    for c in loads[6:7] + loads[8:]:
         c.wait()
-
-    half = lax.broadcasted_iota(jnp.int32, (MW, rows), 1) < MW
 
     def rs_copy(p, d):
         q = lax.rem(x + d, 4)
@@ -358,9 +422,6 @@
 
     def rs_all(p):
         return remote(rs_buf.at[p, pl.ds(1, 3)], rs_buf.at[p, pl.ds(1, 3)], xs.at[p], xr.at[p], tm, lon)
-
-    def z_copy(p):
-        return remote(quarter.at[p, 0], z_buf.at[p], zs.at[p], zr.at[p], tm, lon + 1 - 2 * zh)
 
     days = (2, -2, 1, -1, 0)
 
@@ -434,8 +495,9 @@
                 when_t(-dt, lambda i=i: at_all(p, i).wait_recv())
 
     def transform_done(p):
-        rs_all(p).wait_send()
-        z_copy(p).wait_send()
+        if p == 1:
+            rs_all(p).wait_send()
+            z_copy(p).wait_send()
         for i, dt in enumerate(days):
             when_t(dt, lambda i=i: at_all(p, i).wait_send())
 
@@ -525,14 +587,10 @@
         slope = jnp.sum(jnp.where(low, line, 0.0), axis=1, keepdims=True)
         return slope / jnp.sum(jnp.where(low, 0.0, line), axis=1, keepdims=True)
 
-    with jax.named_scope("transform zero"):
-        transform_start(0)
     with jax.named_scope("rim one send"):
         rim_send(0, G)
     with jax.named_scope("halo one send"):
         halo_send(1, G)
-    with jax.named_scope("cross zero"):
-        transform_cross(0)
     with jax.named_scope("seams"):
         halo_done(1, G)
         seam_take()
@@ -641,6 +699,7 @@
     for i, dt in enumerate((1, -1)):
         when_t(dt, lambda i=i: edge_copy(i).wait_send())
     seam_all().wait_send()
+    first_done()
     for p in range(2):
         transform_done(p)
         rim_all(p).wait_send()
@@ -674,6 +733,9 @@
             pltpu.VMEM((forward.shape[2], rows), F32),
             pltpu.VMEM(seams.shape[1:], F32), pltpu.VMEM((128, rows), F32),
             pltpu.VMEM((16, rows), F32), pltpu.VMEM((8, 8, rows), F32),
+            pltpu.VMEM((forward.shape[2], 3 * rows), F32),
+            pltpu.VMEM((4, 48, rows), F32), pltpu.VMEM((4, 48, rows), F32),
+            pltpu.VMEM((48, rows), F32), pltpu.VMEM((5, 48, rows), F32),
             pltpu.VMEM((2, MW, rows), F32),
             pltpu.VMEM((2, 4, 16, rows), F32),
             pltpu.VMEM((2, 2, 16, rows), F32),
@@ -687,7 +749,7 @@
             pltpu.VMEM((2, 2, 2, rows), F32),
             pltpu.VMEM((2, 8, rows), F32),
             pltpu.VMEM((2, 4, 8, rows), F32),
-            pltpu.SemaphoreType.REGULAR((3,)), dma((2,)), dma((2, 4)), dma((2, 4)), dma((9,)), dma((3, 4)), dma((3, 4)),
+            pltpu.SemaphoreType.REGULAR((3,)), dma((4,)), dma((4,)), dma((2,)), dma((2, 4)), dma((2, 4)), dma((9,)), dma((3, 4)), dma((3, 4)),
             dma((2,)), dma((2,)), dma((2,)), dma((2,)),
             dma((2,)), dma((2,)), dma((2,)), dma((2,)), dma((2, 5)), dma((2, 5)),
             dma((2, 2)), dma((2, 2)),

time: 68.8 us -> 66.3 us (0.964)
  Pallas kernels: 67.3 us -> 64.8 us
    pallas_call x1, Pallas kernels: 67.3 us -> 64.8 us  [on_device(): pl.pallas_call(functools.partial(kernel, NT, N), out_shape=[pltpu.VMEM(fi...]
where the time goes in v7:
time: 66.3 us; the launch traced here: 66.2 us
  Pallas kernels  64.8 us (98%)
  other arithmetic  0.79 us (1%)
    pallas_call x1, Pallas kernels, on_device(): pl.pallas_call(functools.partial(kernel, NT, N), out_shape=[pltpu.VMEM(fi...  64.8 us

profile of v7, /device:TPU:1, one launch (start us, length us, event | category | flops | bytes accessed | tf_op | source)
XLA Modules:
  0.0 66.2 jit_solution(8880631619457535172)
XLA Ops:
  0.6 64.8 %shard_map.104 = (f32[1,360,128]{2,1,0:T(8,128)S(1)}, f32[1,360,128]{2,1,0:T(8,128)S(1)}, f32[1,360,128]{2,1,0:T(8,128)S(1)}, f32[1,360,128]{2,1,0:T(8,128)S(1)}, f32[1,128]{1,0:T(1,128)S(1)}) custom-call(f32[1,360,128]{2,1,0:T(8,128)} %first_ref.1, f32[1,360,128]{2,1,0:T(8,128)} %obs_ref.1, s32[1,360,128]{2,1,0:T(8,128)} %track_ref.1, s32[360,128]{1,0:T(8,128)} %land_ref.1, ...), custom_call_target="tpu_custom_call" | custom-call | tf_op jit(solution)/shard_map/pallas_call | solution.py:723
  65.4 0.8 %multiply_subtract_fusion = (f32[1,360,128]{2,1,0:T(8,128)}, f32[1,360,128]{2,1,0:T(8,128)}) fusion(f32[1,360,128]{2,1,0:T(8,128)S(1)} %get-tuple-element.10, f32[1,360,128]{2,1,0:T(8,128)S(1)} %get-tuple-element.11, f32[128]{0:T(128)S(1)} %bitcast.1, f32[1,360,128]{2,1,0:T(8,128)S(1)} %get-tuple-element.7, f32[1,360,128]{2,1,0:T(8,128)S(1)} %get-tuple-element.9), kind=kLoop, calls=%fused_computation | loop fusion | flops 184320 | bytes 1106432 | tf_op jit(solution)/shard_map/sub | solution.py:761

commit v8 on v7

--- a/solution.py
+++ b/solution.py
@@ -237,8 +237,15 @@
     def seam_copy(l):
         return remote(ED.at[lon], ED.at[lon], sems.at[0], sems.at[1], tm, l)
 
-    def seam_all():
-        return remote(ED.at[pl.ds(0, 7)], ED.at[pl.ds(0, 7)], sems.at[0], sems.at[1], tm, lon)
+    def seam_near():
+        return remote(ED.at[pl.ds(0, 3)], ED.at[pl.ds(0, 3)], sems.at[0], sems.at[1], tm, lon)
+
+    def seam_on(d):
+        slot = ED.at[lon_at(2 * d)]
+        return remote(slot, slot, sems.at[2], sems.at[3], tm, lon + 1 - 2 * zh)
+
+    def seam_far():
+        return remote(ED.at[pl.ds(0, 4)], ED.at[pl.ds(0, 4)], sems.at[2], sems.at[3], tm, lon)
 
     def seam_fill():
         for i, dt in enumerate((1, -1)):
@@ -249,9 +256,6 @@
             ED[lon, at + 1:at + 2] = E[2, inner:inner + 1]
             ED[lon, at + 2:at + 3] = bent[side_row:side_row + 1]
             ED[lon, at + 3:at + 4] = B[row:row + 1]
-
-    def far_lon(d):
-        return lax.rem(x + d, 4) * 2 + 1 - zh
 
     def rim_copy(p, j):
         return remote(ls.at[p, j], lr.at[p, j], rs_.at[p], rr.at[p], tm, lon_at((1, -1)[j]))
@@ -364,13 +368,13 @@
         pl.semaphore_wait(hello.at[1], 2)
         for d in (2, 1, 3):
             greet(tm, lon_at(2 * d), sem=hello.at[2])
-        seam_copy(far_lon(0)).start()
+        seam_on(0).start()
     with jax.named_scope("guess hand on"):
         halo_hand(0, E)
     with jax.named_scope("guess far seams"):
-        pl.semaphore_wait(hello.at[2], 3)
+        seam_near().wait_recv()
         for d in (2, 1, 3):
-            seam_copy(far_lon(d)).start()
+            seam_on(d).start()
     with jax.named_scope("first cross"):
         first_cross()
 
@@ -439,7 +443,7 @@
     half16 = lax.broadcasted_iota(jnp.int32, (16, rows), 1) < MW
 
     def seam_take():
-        seam_all().wait_recv()
+        seam_far().wait_recv()
         er1, er2, ter, ber = (pltpu.roll(ED[:, i, :], 7, axis=0) for i in range(4))
         el1, el2, tel, bel = (ED[:, i, :] for i in range(4, 8))
 
@@ -588,20 +592,21 @@
         return slope / jnp.sum(jnp.where(low, 0.0, line), axis=1, keepdims=True)
 
     with jax.named_scope("rim one send"):
+        pl.semaphore_wait(hello.at[2], 3)
         rim_send(0, G)
     with jax.named_scope("halo one send"):
         halo_send(1, G)
     with jax.named_scope("seams"):
         halo_done(1, G)
         seam_take()
+    with jax.named_scope("spread zero"):
+        transform_spread(0)
     with jax.named_scope("rim one wait"):
         rim_take(0, G)
     with jax.named_scope("border one send"):
         border_send(0, G)
     with jax.named_scope("hand on one"):
         halo_hand(1, G)
-    with jax.named_scope("spread zero"):
-        transform_spread(0)
     with jax.named_scope("halo one wait"):
         halo_wait(1, G)
         border_take(0, G)
@@ -698,7 +703,8 @@
     halo_done(2, U)
     for i, dt in enumerate((1, -1)):
         when_t(dt, lambda i=i: edge_copy(i).wait_send())
-    seam_all().wait_send()
+    seam_near().wait_send()
+    seam_far().wait_send()
     first_done()
     for p in range(2):
         transform_done(p)
@@ -749,7 +755,7 @@
             pltpu.VMEM((2, 2, 2, rows), F32),
             pltpu.VMEM((2, 8, rows), F32),
             pltpu.VMEM((2, 4, 8, rows), F32),
-            pltpu.SemaphoreType.REGULAR((3,)), dma((4,)), dma((4,)), dma((2,)), dma((2, 4)), dma((2, 4)), dma((9,)), dma((3, 4)), dma((3, 4)),
+            pltpu.SemaphoreType.REGULAR((3,)), dma((4,)), dma((4,)), dma((4,)), dma((2, 4)), dma((2, 4)), dma((9,)), dma((3, 4)), dma((3, 4)),
             dma((2,)), dma((2,)), dma((2,)), dma((2,)),
             dma((2,)), dma((2,)), dma((2,)), dma((2,)), dma((2, 5)), dma((2, 5)),
             dma((2, 2)), dma((2, 2)),

time: 66.3 us -> 65.2 us (0.983)
  Pallas kernels: 64.8 us -> 63.6 us
    pallas_call x1, Pallas kernels: 64.8 us -> 63.6 us  [on_device(): pl.pallas_call(functools.partial(kernel, NT, N), out_shape=[pltpu.VMEM(fi...]
where the time goes in v8:
time: 65.2 us; the launch traced here: 65 us
  Pallas kernels  63.6 us (98%)
  other arithmetic  0.79 us (1%)
    pallas_call x1, Pallas kernels, on_device(): pl.pallas_call(functools.partial(kernel, NT, N), out_shape=[pltpu.VMEM(fi...  63.6 us

profile of v8, /device:TPU:1, one launch (start us, length us, event | category | flops | bytes accessed | tf_op | source)
XLA Modules:
  0.0 65.0 jit_solution(5552397603329332180)
XLA Ops:
  0.6 63.6 %shard_map.104 = (f32[1,360,128]{2,1,0:T(8,128)S(1)}, f32[1,360,128]{2,1,0:T(8,128)S(1)}, f32[1,360,128]{2,1,0:T(8,128)S(1)}, f32[1,360,128]{2,1,0:T(8,128)S(1)}, f32[1,128]{1,0:T(1,128)S(1)}) custom-call(f32[1,360,128]{2,1,0:T(8,128)} %first_ref.1, f32[1,360,128]{2,1,0:T(8,128)} %obs_ref.1, s32[1,360,128]{2,1,0:T(8,128)} %track_ref.1, s32[360,128]{1,0:T(8,128)} %land_ref.1, ...), custom_call_target="tpu_custom_call" | custom-call | tf_op jit(solution)/shard_map/pallas_call | solution.py:729
  64.3 0.8 %multiply_subtract_fusion = (f32[1,360,128]{2,1,0:T(8,128)}, f32[1,360,128]{2,1,0:T(8,128)}) fusion(f32[1,360,128]{2,1,0:T(8,128)S(1)} %get-tuple-element.10, f32[1,360,128]{2,1,0:T(8,128)S(1)} %get-tuple-element.11, f32[128]{0:T(128)S(1)} %bitcast.1, f32[1,360,128]{2,1,0:T(8,128)S(1)} %get-tuple-element.7, f32[1,360,128]{2,1,0:T(8,128)S(1)} %get-tuple-element.9), kind=kLoop, calls=%fused_computation | loop fusion | flops 184320 | bytes 1106432 | tf_op jit(solution)/shard_map/sub | solution.py:767

commit v9 on v8

--- a/solution.py
+++ b/solution.py
@@ -51,9 +51,9 @@
 def kernel(
     NT, N, first_ref, obs_ref, track_ref, land_ref, bw_ref, fwd_ref, inv_ref, row_hbm, seams_hbm,
     out_a, out_s, out_g, out_c, out_step,
-    row_ref, E, G, U, B, W, obs, track, land, fwd, inv, V, TV, T2V, Y, V0, LV0, padded, seams, seam_rows, seam_amp, ED, three, amp3, rs3, sum3, day3, amp, rs_buf, quarter,
+    row_ref, E, G, U, B, W, obs, track, land, fwd, inv, V, TV, T2V, Y, V0, LV0, padded, seams, seam_rows, seam_amp, ED, three, amp3, rs3, sum3, day3, own_buf, own_sum, own_z_buf, amp, quarter,
     z_buf, AT, dots_a, dots_b, ts, tr, ls, lr, bs, br,
-    hello, fs, fr, sems, bsem, brem, lsem, hs, hr, es, er, rs_, rr, xs, xr, zs, zr, ats, atr, ds_, dr,
+    hello, ow, osend, fs, fr, sems, bsem, brem, lsem, hs, hr, es, er, rs_, rr, xs, xr, zs, zr, ats, atr, ds_, dr,
 ):
     tm = lax.axis_index("tm")
     lon = lax.axis_index("lon")
@@ -420,13 +420,6 @@
     for c in loads[6:7] + loads[8:]:
         c.wait()
 
-    def rs_copy(p, d):
-        q = lax.rem(x + d, 4)
-        return remote(amp.at[p, pl.ds(16 * q, 16)], rs_buf.at[p, d], xs.at[p], xr.at[p], tm, q * 2 + zh)
-
-    def rs_all(p):
-        return remote(rs_buf.at[p, pl.ds(1, 3)], rs_buf.at[p, pl.ds(1, 3)], xs.at[p], xr.at[p], tm, lon)
-
     days = (2, -2, 1, -1, 0)
 
     def at_copy(p, i, d):
@@ -471,16 +464,7 @@
     def transform_start(p):
         part = lax.dot(fwd[...], padded[...], precision=lax.Precision.HIGH, preferred_element_type=F32)
         amp[p] = jnp.where(half, pltpu.roll(part[:MW], MW, axis=1), part[MW:])
-        for d in (2, 1, 3):
-            rs_copy(p, d).start()
-
-    def transform_cross(p):
-        total = amp[p, pl.ds(16 * x, 16)]
-        rs_all(p).wait_recv()
-        for d in (1, 2, 3):
-            total = total + rs_buf[p, d]
-        quarter[p, 0] = total
-        z_copy(p).start()
+        own_start()
 
     def transform_spread(p):
         z_copy(p).wait_recv()
@@ -493,15 +477,102 @@
                 when_t(dt, lambda i=i, d=d: at_copy(p, i, d).start())
         AT[p, 2, pl.ds(16 * x, 16)] = total
 
+    core = lax.rem(tm, 2)
+    odd, even = core == 1, core == 0
+    top = tm + 1 - core
+
+    def own_send(d):
+        q = lax.rem(x + d, 4)
+        return remote(amp.at[1, pl.ds(16 * q, 16)], own_buf.at[core, d], xs.at[1], ow.at[core], top, q * 2 + zh)
+
+    def own_part(day, some):
+        return remote(own_buf.at[day, some], own_buf.at[day, some], xs.at[1], ow.at[day], tm, lon)
+
+    def own_z():
+        return remote(own_sum.at[0], own_z_buf, zs.at[1], zr.at[1], tm, lon + 1 - 2 * zh)
+
+    def own_start():
+        for d in (2, 1, 3):
+            own_send(d).start()
+        pl.when(even)(lambda: own_send(0).start())
+
+    def own_cross():
+        @pl.when(odd)
+        def _():
+            own_buf[1, 0] = amp[1, pl.ds(16 * x, 16)]
+            own_part(0, pl.ds(0, 4)).wait_recv()
+            own_part(1, pl.ds(1, 3)).wait_recv()
+            for day in range(2):
+                own_sum[0, day] = own_buf[day, 0] + own_buf[day, 1] + own_buf[day, 2] + own_buf[day, 3]
+            own_z().start()
+
+    def own_copy(day, i, d):
+        xx = lax.rem(x + d, 4)
+        return remote(
+            own_sum.at[1, day], AT.at[1, 2 - days[i], pl.ds(16 * x, 16)], osend.at[day, i], atr.at[1, i],
+            tm - 1 + day + days[i], xx * 2 + zh,
+        )
+
+    def mine(day, dt):
+        return day - 1 + dt == 0
+
+    def own_spread():
+        @pl.when(odd)
+        def _():
+            own_z().wait_recv()
+            own_sum[1] = own_sum[0] + own_z_buf[...]
+            for i, dt in enumerate(days):
+                for day in range(2):
+
+                    @pl.when(inside(tm - 1 + day + dt))
+                    def _(i=i, dt=dt, day=day):
+                        for d in (2, 1, 3) if mine(day, dt) else (2, 1, 3, 0):
+                            own_copy(day, i, d).start()
+
+            for day in range(2):
+                AT[1, 1 + day, pl.ds(16 * x, 16)] = own_sum[1, day]
+
+    def own_all(i, count, sem):
+        some = AT.at[1, 2 - days[i], pl.ds(0, 16 * count)]
+        return remote(some, some, sem, atr.at[1, i], tm, lon)
+
+    def own_finish(some):
+        for i, dt in enumerate(days):
+            if dt not in some:
+                continue
+            here = inside(tm - dt)
+            if dt in (0, 1):
+                pl.when(here & odd)(lambda i=i: own_all(i, 3, osend.at[0, 0]).wait_recv())
+                pl.when(here & even)(lambda i=i: own_all(i, 4, osend.at[0, 0]).wait_recv())
+            else:
+                pl.when(here)(lambda i=i: own_all(i, 4, osend.at[0, 0]).wait_recv())
+
+    def own_done():
+        pl.when(even)(lambda: own_part(0, pl.ds(0, 4)).wait_send())
+
+        @pl.when(odd)
+        def _():
+            own_part(0, pl.ds(0, 3)).wait_send()
+            own_z().wait_send()
+            for i, dt in enumerate(days):
+                for day in range(2):
+
+                    @pl.when(inside(tm - 1 + day + dt))
+                    def _(i=i, dt=dt, day=day):
+                        own_all(i, 3 if mine(day, dt) else 4, osend.at[day, i]).wait_send()
+
     def transform_finish(p, some):
+        if p == 1:
+            own_finish(some)
+            return
         for i, dt in enumerate(days):
             if dt in some:
                 when_t(-dt, lambda i=i: at_all(p, i).wait_recv())
 
     def transform_done(p):
         if p == 1:
-            rs_all(p).wait_send()
-            z_copy(p).wait_send()
+            own_done()
+            return
         for i, dt in enumerate(days):
             when_t(dt, lambda i=i: at_all(p, i).wait_send())
 
@@ -647,7 +718,7 @@
     with jax.named_scope("halo two send"):
         halo_send(2, U)
     with jax.named_scope("cross one"):
-        transform_cross(1)
+        own_cross()
     with jax.named_scope("sums zero"):
         dot_send(0, 1, dot_take(0, 0))
     with jax.named_scope("rim two wait"):
@@ -657,7 +728,7 @@
     with jax.named_scope("hand on two"):
         halo_hand(2, U)
     with jax.named_scope("spread one"):
-        transform_spread(1)
+        own_spread()
     with jax.named_scope("halo two wait"):
         halo_wait(2, U)
         border_take(1, U)
@@ -742,8 +813,9 @@
             pltpu.VMEM((forward.shape[2], 3 * rows), F32),
             pltpu.VMEM((4, 48, rows), F32), pltpu.VMEM((4, 48, rows), F32),
             pltpu.VMEM((48, rows), F32), pltpu.VMEM((5, 48, rows), F32),
+            pltpu.VMEM((2, 4, 16, rows), F32), pltpu.VMEM((2, 2, 16, rows), F32),
+            pltpu.VMEM((2, 16, rows), F32),
             pltpu.VMEM((2, MW, rows), F32),
-            pltpu.VMEM((2, 4, 16, rows), F32),
             pltpu.VMEM((2, 2, 16, rows), F32),
             pltpu.VMEM((2, 16, rows), F32),
             pltpu.VMEM((2, 5, MW, rows), F32),
@@ -755,7 +827,7 @@
             pltpu.VMEM((2, 2, 2, rows), F32),
             pltpu.VMEM((2, 8, rows), F32),
             pltpu.VMEM((2, 4, 8, rows), F32),
-            pltpu.SemaphoreType.REGULAR((3,)), dma((4,)), dma((4,)), dma((4,)), dma((2, 4)), dma((2, 4)), dma((9,)), dma((3, 4)), dma((3, 4)),
+            pltpu.SemaphoreType.REGULAR((3,)), dma((2,)), dma((2, 5)), dma((4,)), dma((4,)), dma((4,)), dma((2, 4)), dma((2, 4)), dma((9,)), dma((3, 4)), dma((3, 4)),
             dma((2,)), dma((2,)), dma((2,)), dma((2,)),
             dma((2,)), dma((2,)), dma((2,)), dma((2,)), dma((2, 5)), dma((2, 5)),
             dma((2, 2)), dma((2, 2)),

time: 65.2 us -> 64 us (0.982)
  Pallas kernels: 63.6 us -> 62.4 us
    pallas_call x1, Pallas kernels: 63.6 us -> 62.4 us  [on_device(): pl.pallas_call(functools.partial(kernel, NT, N), out_shape=[pltpu.VMEM(fi...]
where the time goes in v9:
time: 64 us; the launch traced here: 63.8 us
  Pallas kernels  62.4 us (98%)
  other arithmetic  0.79 us (1%)
  between operations  0.64 us (1%)
    pallas_call x1, Pallas kernels, on_device(): pl.pallas_call(functools.partial(kernel, NT, N), out_shape=[pltpu.VMEM(fi...  62.4 us

profile of v9, /device:TPU:1, one launch (start us, length us, event | category | flops | bytes accessed | tf_op | source)
XLA Modules:
  0.0 63.8 jit_solution(17289033728829621793)
XLA Ops:
  0.6 62.4 %shard_map.104 = (f32[1,360,128]{2,1,0:T(8,128)S(1)}, f32[1,360,128]{2,1,0:T(8,128)S(1)}, f32[1,360,128]{2,1,0:T(8,128)S(1)}, f32[1,360,128]{2,1,0:T(8,128)S(1)}, f32[1,128]{1,0:T(1,128)S(1)}) custom-call(f32[1,360,128]{2,1,0:T(8,128)} %first_ref.1, f32[1,360,128]{2,1,0:T(8,128)} %obs_ref.1, s32[1,360,128]{2,1,0:T(8,128)} %track_ref.1, s32[360,128]{1,0:T(8,128)} %land_ref.1, ...), custom_call_target="tpu_custom_call" | custom-call | tf_op jit(solution)/shard_map/pallas_call | solution.py:800
  63.0 0.8 %multiply_subtract_fusion = (f32[1,360,128]{2,1,0:T(8,128)}, f32[1,360,128]{2,1,0:T(8,128)}) fusion(f32[1,360,128]{2,1,0:T(8,128)S(1)} %get-tuple-element.10, f32[1,360,128]{2,1,0:T(8,128)S(1)} %get-tuple-element.11, f32[128]{0:T(128)S(1)} %bitcast.1, f32[1,360,128]{2,1,0:T(8,128)S(1)} %get-tuple-element.7, f32[1,360,128]{2,1,0:T(8,128)S(1)} %get-tuple-element.9), kind=kLoop, calls=%fused_computation | loop fusion | flops 184320 | bytes 1106432 | tf_op jit(solution)/shard_map/sub | solution.py:839

commit v10 on v9

--- a/solution.py
+++ b/solution.py
@@ -196,13 +196,13 @@
 
     def plane_copy(p, X, i):
         dt = send_days[i]
-        return remote(X.at[2, own], X.at[2 - dt, own], hs.at[p, i], hr.at[p, i], tm + dt, lon)
+        return remote(X.at[2, own], X.at[2 - dt, own], hs.at[i], hr.at[p, i], tm + dt, lon)
 
     def hand_copy(p, X):
-        return remote(X.at[2 - side, own], X.at[2 - 2 * side, own], hs.at[p, 3], hr.at[p, 3], tm + side, lon)
+        return remote(X.at[2 - side, own], X.at[2 - 2 * side, own], hs.at[3], hr.at[p, 3], tm + side, lon)
 
     def plane_recv(p, X, i):
-        return remote(X.at[2, own], X.at[2 + recv_days[i], own], hs.at[p, i], hr.at[p, i], tm, lon)
+        return remote(X.at[2, own], X.at[2 + recv_days[i], own], hs.at[i], hr.at[p, i], tm, lon)
 
     def halo_send(p, X):
         for i in range(3):
@@ -286,7 +286,7 @@
     border_days = (2, -2, 1, -1)
 
     def border_copy(p, i):
-        return remote(bs.at[p], br.at[p, i], bsem.at[p, i], brem.at[p, i], tm + border_days[i], lon)
+        return remote(bs.at[p], br.at[p, i], bsem.at[i], brem.at[p, i], tm + border_days[i], lon)
 
     def border_send(p, X):
         for i, row in enumerate(border_rows):
@@ -426,12 +426,12 @@
         dt = days[i]
         xx = lax.rem(x + d, 4)
         return remote(
-            quarter.at[p, 1], AT.at[p, 2 - dt, pl.ds(16 * x, 16)], ats.at[p, i], atr.at[p, i], tm + dt, xx * 2 + zh
+            quarter.at[p, 1], AT.at[p, 2 - dt, pl.ds(16 * x, 16)], ats.at[i], atr.at[p, i], tm + dt, xx * 2 + zh
         )
 
     def at_all(p, i):
         some = AT.at[p, 2 - days[i], pl.ds(0, MW if days[i] else MW - 16)]
-        return remote(some, some, ats.at[p, i], atr.at[p, i], tm, lon)
+        return remote(some, some, ats.at[i], atr.at[p, i], tm, lon)
 
     half16 = lax.broadcasted_iota(jnp.int32, (16, rows), 1) < MW
 
@@ -473,8 +473,12 @@
             total = total + seam_amp[...]
         quarter[p, 1] = total
         for i, dt in enumerate(days):
-            for d in (2, 1, 3, 0) if dt else (2, 1, 3):
-                when_t(dt, lambda i=i, d=d: at_copy(p, i, d).start())
+
+            def shift(i=i, dt=dt):
+                for d in (2, 1, 3, 0) if dt else (2, 1, 3):
+                    at_copy(p, i, d).start()
+
+            when_t(dt, shift)
         AT[p, 2, pl.ds(16 * x, 16)] = total
 
     core = lax.rem(tm, 2)
@@ -666,6 +670,7 @@
         pl.semaphore_wait(hello.at[2], 3)
         rim_send(0, G)
     with jax.named_scope("halo one send"):
+        halo_done(0, E)
         halo_send(1, G)
     with jax.named_scope("seams"):
         halo_done(1, G)
@@ -724,6 +729,7 @@
     with jax.named_scope("rim two wait"):
         rim_take(1, U)
     with jax.named_scope("border two send"):
+        border_done(0)
         border_send(1, U)
     with jax.named_scope("hand on two"):
         halo_hand(2, U)
@@ -770,7 +776,6 @@
         twice(emit_last)
     with jax.named_scope("sums one b"):
         dot_send(1, 1, dot_take(1, 0))
-    halo_done(0, E)
     halo_done(2, U)
     for i, dt in enumerate((1, -1)):
         when_t(dt, lambda i=i: edge_copy(i).wait_send())
@@ -780,7 +785,7 @@
     for p in range(2):
         transform_done(p)
         rim_all(p).wait_send()
-        border_done(p)
+    border_done(1)
     dot_done(0)
     with jax.named_scope("sums one c"):
         out_step[...] = jnp.broadcast_to(ratio(dot_take(1, 1)), out_step.shape)
@@ -827,9 +832,9 @@
             pltpu.VMEM((2, 2, 2, rows), F32),
             pltpu.VMEM((2, 8, rows), F32),
             pltpu.VMEM((2, 4, 8, rows), F32),
-            pltpu.SemaphoreType.REGULAR((3,)), dma((2,)), dma((2, 5)), dma((4,)), dma((4,)), dma((4,)), dma((2, 4)), dma((2, 4)), dma((9,)), dma((3, 4)), dma((3, 4)),
+            pltpu.SemaphoreType.REGULAR((3,)), dma((2,)), dma((2, 5)), dma((4,)), dma((4,)), dma((4,)), dma((4,)), dma((2, 4)), dma((9,)), dma((4,)), dma((3, 4)),
             dma((2,)), dma((2,)), dma((2,)), dma((2,)),
-            dma((2,)), dma((2,)), dma((2,)), dma((2,)), dma((2, 5)), dma((2, 5)),
+            dma((2,)), dma((2,)), dma((2,)), dma((2,)), dma((5,)), dma((2, 5)),
             dma((2, 2)), dma((2, 2)),
         ],
         compiler_params=pltpu.CompilerParams(

time: 64 us -> 63.8 us (level)
  no operation moved by 1% of the time
where the time goes in v10:
time: 63.8 us; the launch traced here: 63.7 us
  Pallas kernels  62.2 us (97%)
  other arithmetic  0.79 us (1%)
  between operations  0.64 us (1%)
    pallas_call x1, Pallas kernels, on_device(): pl.pallas_call(functools.partial(kernel, NT, N), out_shape=[pltpu.VMEM(fi...  62.2 us

profile of v10, /device:TPU:1, one launch (start us, length us, event | category | flops | bytes accessed | tf_op | source)
XLA Modules:
  0.0 63.7 jit_solution(1824473259728690580)
XLA Ops:
  0.6 62.2 %shard_map.104 = (f32[1,360,128]{2,1,0:T(8,128)S(1)}, f32[1,360,128]{2,1,0:T(8,128)S(1)}, f32[1,360,128]{2,1,0:T(8,128)S(1)}, f32[1,360,128]{2,1,0:T(8,128)S(1)}, f32[1,128]{1,0:T(1,128)S(1)}) custom-call(f32[1,360,128]{2,1,0:T(8,128)} %first_ref.1, f32[1,360,128]{2,1,0:T(8,128)} %obs_ref.1, s32[1,360,128]{2,1,0:T(8,128)} %track_ref.1, s32[360,128]{1,0:T(8,128)} %land_ref.1, ...), custom_call_target="tpu_custom_call" | custom-call | tf_op jit(solution)/shard_map/pallas_call | solution.py:805
  62.9 0.8 %multiply_subtract_fusion = (f32[1,360,128]{2,1,0:T(8,128)}, f32[1,360,128]{2,1,0:T(8,128)}) fusion(f32[1,360,128]{2,1,0:T(8,128)S(1)} %get-tuple-element.10, f32[1,360,128]{2,1,0:T(8,128)S(1)} %get-tuple-element.11, f32[128]{0:T(128)S(1)} %bitcast.1, f32[1,360,128]{2,1,0:T(8,128)S(1)} %get-tuple-element.7, f32[1,360,128]{2,1,0:T(8,128)S(1)} %get-tuple-element.9), kind=kLoop, calls=%fused_computation | loop fusion | flops 184320 | bytes 1106432 | tf_op jit(solution)/shard_map/sub | solution.py:844
